TPU v7x, 256 devices: a whole 4x4x8 slice. The times are simulated.
256 devices in a mesh: dp: 4 (over z_hi), ctx: 8 (over y, core), head: 8 (over z_lo, x).
Axes of the slice: x: 4, y: 4, z: 8 (z_hi: 4, z_lo: 2; z = z_hi * 2 + z_lo), core: 2. Of those that a mesh axis runs over, the one named last changes fastest.
Arguments:
- q_nope: bfloat16 [4, 1024, 8192], P('dp', 'ctx', 'head'), may hold values from -6 to 6
- q_rope: bfloat16 [4, 1024, 4096], P('dp', 'ctx', 'head'), may hold values from -7.5 to 7.5
- kv_latent: bfloat16 [4, 1024, 576], P('dp', 'ctx'), may hold values from -7.5 to 7.5
- d_out: bfloat16 [4, 1024, 8192], P('dp', 'ctx', 'head'), may hold values from -6 to 6
- w_uk: bfloat16 [512, 8192], P(None, 'head'), may hold values from -0.25 to 0.25
- w_uv: bfloat16 [512, 8192], P(None, 'head'), may hold values from -0.25 to 0.25
- segment_ids: int32 [4, 1024], P('dp'), may hold values from 0 to 3, never falling along the last dimension, each value on 1 to 512 neighbouring positions
- span_order: int32 [16], replicated, may hold values from 0 to 15, as said below
Outputs:
- dq_nope: bfloat16 [4, 1024, 8192], P('dp', 'ctx', 'head')
- dq_rope: bfloat16 [4, 1024, 4096], P('dp', 'ctx', 'head')
- d_kv: bfloat16 [4, 1024, 576], P('dp', ('ctx', 'head'))
- dw_uk: float32 [512, 8192], P(None, 'head')
- dw_uv: float32 [512, 8192], P(None, 'head')
Inputs may be any that keep to these rules, and one draw needn't show every extreme that they name: `span_order`: a permutation of the 16 span numbers in which storage slots 2 c and 2 c + 1 hold two spans whose numbers add up to 15.
All inputs are finite; a program needn't handle non-finite values.
Results may differ from a plain program's by a relative error of at most 0.03.
Values may be sent and summed in bfloat16 or wider, within the bound.
No kernel may reach another device: no remote copies, remote signals or barrier semaphores. Data moves between devices by JAX's collectives and lax.ppermute only.
A program may use at most 64 MiB of HBM per device.

v0:
```python
import jax
import jax.numpy as jnp
from jax import lax
from jax.sharding import PartitionSpec as P

LAT = 512
ROPE = 64
NOPE = 128
VDIM = 128


def storage_positions(span_order, seq_rows):
    span_rows = seq_rows // span_order.shape[0]
    slot_ids = jnp.arange(seq_rows, dtype=jnp.int32)
    numbers = jnp.arange(span_order.shape[0], dtype=jnp.int32)
    owners = jnp.sum(
        jnp.where((slot_ids // span_rows)[:, None] == numbers[None, :], span_order[None, :], 0),
        axis=1,
    )
    return owners * span_rows + slot_ids % span_rows


def local(q_nope, q_rope, kv_latent, d_out, w_uk, w_uv, segment_ids, span_order):
    tok_rows = q_nope.shape[1]
    head_count = q_nope.shape[2] // NOPE
    latent_width = kv_latent.shape[2]
    softmax_scale = (NOPE + ROPE) ** (-0.5)
    keys_all = lax.all_gather(kv_latent[0], "ctx", axis=0, tiled=True)
    seq_rows = keys_all.shape[0]
    blocks = seq_rows // tok_rows
    places = storage_positions(span_order, seq_rows)
    labels = jnp.take(segment_ids[0], places)
    own_start = lax.axis_index("ctx") * tok_rows
    q_places = lax.dynamic_slice_in_dim(places, own_start, tok_rows)
    q_labels = lax.dynamic_slice_in_dim(labels, own_start, tok_rows)
    nope_heads = q_nope[0].reshape(tok_rows, head_count, NOPE)
    uk_heads = w_uk.reshape(LAT, head_count, NOPE)
    q_latent = jnp.einsum(
        "thn,chn->htc", nope_heads, uk_heads, preferred_element_type=jnp.float32
    ).astype(jnp.bfloat16)
    rope_heads = q_rope[0].reshape(tok_rows, head_count, ROPE).transpose(1, 0, 2)
    q_full = jnp.concatenate([q_latent, rope_heads], axis=2)
    grad_heads = d_out[0].reshape(tok_rows, head_count, VDIM)
    uv_heads = w_uv.reshape(LAT, head_count, VDIM)
    do_latent = jnp.einsum("thv,chv->htc", grad_heads, uv_heads, preferred_element_type=jnp.float32)
    do_bf = do_latent.astype(jnp.bfloat16)

    def key_block(block_idx):
        block_start = block_idx * tok_rows
        block_keys = lax.dynamic_slice_in_dim(keys_all, block_start, tok_rows, 0)
        key_places = lax.dynamic_slice_in_dim(places, block_start, tok_rows)
        key_labels = lax.dynamic_slice_in_dim(labels, block_start, tok_rows)
        visible = (key_labels[None, :] == q_labels[:, None]) & (
            key_places[None, :] <= q_places[:, None]
        )
        return (block_keys, visible)

    def block_scores(block_keys):
        return (
            jnp.einsum("hqd,kd->hqk", q_full, block_keys, preferred_element_type=jnp.float32)
            * softmax_scale
        )

    def stats_step(running, block_keys, visible):
        run_max, run_sum = running
        scores = block_scores(block_keys)
        masked = jnp.where(visible[None], scores, -1e30)
        new_max = jnp.maximum(run_max, jnp.max(masked, axis=2))
        weights = jnp.where(visible[None], jnp.exp(scores - new_max[:, :, None]), 0.0)
        run_sum = run_sum * jnp.exp(run_max - new_max) + jnp.sum(weights, axis=2)
        return (new_max, run_sum)

    def stats_visit(running, block_idx):
        block_keys, visible = key_block(block_idx)
        running = stats_step(running, block_keys, visible)
        return (running, None)

    start_state = (
        jnp.full((head_count, tok_rows), -1e30, jnp.float32),
        jnp.zeros((head_count, tok_rows), jnp.float32),
    )
    final_state, unused = lax.scan(stats_visit, start_state, jnp.arange(blocks))
    run_max, run_sum = final_state
    lse = run_max + jnp.log(run_sum)

    def block_probs(block_keys, visible):
        scores = block_scores(block_keys)
        return jnp.where(visible[None], jnp.exp(scores - lse[:, :, None]), 0.0)

    def value_step(acc, block_keys, visible):
        probs_bf = block_probs(block_keys, visible).astype(jnp.bfloat16)
        return acc + jnp.einsum(
            "hqk,kc->hqc", probs_bf, block_keys[:, :LAT], preferred_element_type=jnp.float32
        )

    def value_visit(acc, block_idx):
        block_keys, visible = key_block(block_idx)
        acc = value_step(acc, block_keys, visible)
        return (acc, None)

    o_latent, unused = lax.scan(
        value_visit, jnp.zeros((head_count, tok_rows, LAT), jnp.float32), jnp.arange(blocks)
    )
    row_dot = jnp.sum(do_latent * o_latent, axis=2)
    uv_grad = jnp.einsum(
        "htc,thv->chv",
        o_latent.astype(jnp.bfloat16),
        grad_heads,
        preferred_element_type=jnp.float32,
    ).reshape(LAT, head_count * VDIM)
    uv_total = uv_grad

    def backward_step(dq_acc, block_keys, visible):
        probs_f = block_probs(block_keys, visible)
        probs_bf = probs_f.astype(jnp.bfloat16)
        dprobs = jnp.einsum(
            "hqc,kc->hqk", do_bf, block_keys[:, :LAT], preferred_element_type=jnp.float32
        )
        dscores = (probs_f * (dprobs - row_dot[:, :, None]) * softmax_scale).astype(jnp.bfloat16)
        dq_acc = dq_acc + jnp.einsum(
            "hqk,kd->hqd", dscores, block_keys, preferred_element_type=jnp.float32
        )
        value_part = jnp.einsum("hqk,hqc->kc", probs_bf, do_bf, preferred_element_type=jnp.float32)
        key_grad = jnp.einsum("hqk,hqd->kd", dscores, q_full, preferred_element_type=jnp.float32)
        key_grad = key_grad + jnp.concatenate(
            [value_part, jnp.zeros((tok_rows, ROPE), jnp.float32)], axis=1
        )
        return (dq_acc, key_grad)

    def backward_visit(dq_acc, block_idx):
        block_keys, visible = key_block(block_idx)
        return backward_step(dq_acc, block_keys, visible)

    dq_start = jnp.zeros((head_count, tok_rows, latent_width), jnp.float32)
    dq_full, stacked = lax.scan(backward_visit, dq_start, jnp.arange(blocks))
    dq_latent = dq_full[:, :, :LAT].astype(jnp.bfloat16)
    dq_nope = jnp.einsum(
        "htc,chn->thn", dq_latent, uk_heads, preferred_element_type=jnp.float32
    ).astype(jnp.bfloat16)
    dq_nope = dq_nope.reshape(1, tok_rows, head_count * NOPE)
    dq_rope = (
        dq_full[:, :, LAT:]
        .astype(jnp.bfloat16)
        .transpose(1, 0, 2)
        .reshape(1, tok_rows, head_count * ROPE)
    )
    uk_grad = jnp.einsum(
        "htc,thn->chn", dq_latent, nope_heads, preferred_element_type=jnp.float32
    ).reshape(LAT, head_count * NOPE)
    key_grads = stacked.reshape(seq_rows, latent_width)
    summed = lax.psum_scatter(key_grads, ("ctx", "head"), scatter_dimension=0, tiled=True)
    d_kv = summed.astype(jnp.bfloat16)[None]
    uk_total, uv_total = (
        lax.psum(uk_grad.astype(jnp.bfloat16), ("dp", "ctx")).astype(jnp.float32),
        lax.psum(uv_total.astype(jnp.bfloat16), ("dp", "ctx")).astype(jnp.float32),
    )
    return (dq_nope, dq_rope, d_kv, uk_total, uv_total)


def solution(mesh):
    return jax.shard_map(
        local,
        mesh=mesh,
        in_specs=(
            P("dp", "ctx", "head"),
            P("dp", "ctx", "head"),
            P("dp", "ctx", None),
            P("dp", "ctx", "head"),
            P(None, "head"),
            P(None, "head"),
            P("dp", None),
            P(),
        ),
        out_specs=(
            P("dp", "ctx", "head"),
            P("dp", "ctx", "head"),
            P("dp", ("ctx", "head"), None),
            P(None, "head"),
            P(None, "head"),
        ),
        check_vma=False,
    )
```

profile of v0, /device:TPU:2, one launch (start us, length us, event | category | flops | bytes accessed | tf_op | source)
XLA Modules:
  0.0 817.1 jit_solution(13355813575318189926)
XLA Ops:
  8.9 4.5 gather_fusion
  18.8 20.4 %all-gather.3.cloned.1.call-done = bf16[1,1024,576]{1,2,0:T(8,128)(2,1)} async-done(((bf16[1,128,576]{1,2,0:T(8,128)(2,1)}), bf16[1,1024,576]{1,2,0:T(8,128)(2,1)}) %all-gather.3.cloned.1.call-update) | async-done | bytes 1179664 | tf_op jit(solution)/shard_map/all_gather | solution.py:28
  39.2 35.0 %while.37 = (s32[]{:T(128)}, f32[8,128]{1,0:T(8,128)S(1)}, f32[8,128]{1,0:T(8,128)S(1)}, s32[8]{0:T(128)S(1)}, s32[1024]{0:T(1024)}, /*index=5*/s32[128]{0:T(128...) while((s32[]{:T(128)}, f32[8,128]{1,0:T(8,128)S(1)}, ...), condition=%wide.region_4.5_spmd.clone, body=%wide.region_1.4_spmd.clone.sunk | while | flops 151835648 | bytes 2482398 | solution.py:82
  74.8 58.3 %while.38 = (s32[]{:T(128)}, f32[8,128,512]{2,1,0:T(8,128)}, s32[8]{0:T(128)S(1)}, s32[1024]{0:T(1024)}, s32[128]{0:T(128)}, /*index=5*/s32[1024]{0:T(1024)}, s3...) while((s32[]{:T(128)}, f32[8,128,512]{2,1,0:T(8,128)}, ...), condition=%wide.region_6.7_spmd.clone, body=%wide.region_5.6_spmd.clone.sunk | while | flops 286834688 | bytes 5695192 | solution.py:101
  78.2 3.1 select_add_fusion.4
  84.8 3.9 select_add_fusion.4
  92.2 3.9 select_add_fusion.4
  99.6 3.9 select_add_fusion.4
  107.0 3.9 select_add_fusion.4
  114.4 3.9 select_add_fusion.4
  121.8 3.9 select_add_fusion.4
  129.2 3.9 select_add_fusion.4
  133.1 3.2 convolution_convert_fusion
  136.9 2.3 copy.77
  139.2 84.4 %while.39 = (s32[]{:T(128)}, f32[8,128,576]{1,2,0:T(8,128)}, f32[8,128,576]{1,2,0:T(8,128)}, s32[8]{0:T(128)S(1)}, s32[1024]{0:T(1024)}, /*index=5*/s32[128]{0:T...) while((s32[]{:T(128)}, f32[8,128,576]{1,2,0:T(8,128)}, ...), condition=%wide.region_9.10_spmd.clone, body=%wide.region_8.9_spmd.clone.sunk | while | flops 723771392 | bytes 31699256 | solution.py:135
  146.6 1.7 select_add_fusion.5
  148.3 1.4 copy-done.4
  157.1 1.7 select_add_fusion.5
  158.9 1.4 copy-done.4
  167.6 1.7 select_add_fusion.5
  178.2 1.7 select_add_fusion.5
  188.7 1.7 select_add_fusion.5
  199.3 1.7 select_add_fusion.5
  209.8 1.7 select_add_fusion.5
  220.4 1.7 select_add_fusion.5
  223.5 1.9 copy.70
  228.2 3.2 copy.73
  233.8 1.8 copy.78
  236.5 285.0 %all-reduce.4.cloned.1.call-done = (bf16[512,1024]{1,0:T(8,128)(2,1)}, bf16[512,1024]{1,0:T(8,128)(2,1)}) async-done(((bf16[512,1024]{1,0:T(8,128)(2,1)}, bf16[512,1024]{1,0:T(8,128)(2,1)}), (bf16[512,1024]{1,0:T(8,128)(2,1)}, bf16[512,1024]{1,0:T(8,128)(2,1)})) %all-reduce.4.cloned.1.call-update) | async-done | bytes 2097168 | tf_op jit(solution)/shard_map/psum | solution.py:154
  521.5 2.9 convert_element_type.61
  524.4 1.6 convert_element_type.66
  526.0 283.2 %reduce-scatter.2.cloned.1.call-done = f32[16,576]{1,0:T(8,128)} async-done(((f32[1024,576]{1,0:T(8,128)}), f32[16,576]{1,0:T(8,128)}) %reduce-scatter.2.cloned.1.call-update) | async-done | bytes 36880 | tf_op jit(solution)/shard_map/reduce_scatter | solution.py:151
  (271 shorter events, 129.6 us)
Async XLA Ops:
  7.2 129.1 %copy-start = (bf16[512,1024]{1,0:T(8,128)(2,1)S(1)}, bf16[512,1024]{1,0:T(8,128)(2,1)}, u32[]{:S(2)}) copy-start(bf16[512,1024]{1,0:T(8,128)(2,1)} %param.19) | copy-start | bytes 3145732
  7.2 1.6 copy-start.1
  7.2 32.0 %all-gather.3.cloned.1.call-start = ((), (), s32[]{:S(2)}) async-start(), calls=%async_computation.2 | async-start | bytes 1327104 | tf_op jit(solution)/shard_map/all_gather | solution.py:28
  7.9 513.6 %all-reduce.4.cloned.1.call-start = ((), (), s32[]{:S(2)}) async-start(), calls=%async_computation.3 | async-start | bytes 4194304 | tf_op jit(solution)/shard_map/psum | solution.py:154
  8.8 5.3 copy-start.14
  8.8 6.3 copy-start.12
  8.9 6.4 copy-start.13
  8.9 7.3 copy-start.11
  15.3 1.9 copy-start.7
  16.7 1.1 copy-start.10
  74.8 58.3 %copy-start.8 = (bf16[1,128,1024]{1,2,0:T(8,128)(2,1)S(1)}, bf16[1,128,1024]{1,2,0:T(8,128)(2,1)}, u32[]{:S(2)}) copy-start(bf16[1,128,1024]{1,2,0:T(8,128)(2,1)} %copy.91) | copy-start | bytes 786436
  133.1 3.2 copy-start.2
  136.9 2.3 copy-start.16
  144.8 1.8 copy-start.3
  148.3 1.4 copy-start.4
  155.4 1.7 copy-start.3
  158.9 1.4 copy-start.4
  165.9 1.7 copy-start.3
  169.4 1.4 copy-start.4
  176.5 1.7 copy-start.3
  179.9 1.4 copy-start.4
  187.0 1.7 copy-start.3
  190.5 1.4 copy-start.4
  197.5 1.7 copy-start.3
  201.0 1.4 copy-start.4
  208.1 1.7 copy-start.3
  211.6 1.4 copy-start.4
  218.6 1.7 copy-start.3
  222.1 1.4 copy-start.4
  228.2 581.0 %reduce-scatter.2.cloned.1.call-start = ((), (), s32[]{:S(2)}) async-start(), calls=%async_computation.1 | async-start | bytes 2662400 | tf_op jit(solution)/shard_map/reduce_scatter | solution.py:151
  231.4 1.2 copy-start.6
  521.5 2.9 copy-start.9
  (4 other events, 2.7 us)
Sparse Core Ops, SparseCore 0:
  9.8 29.2 all-gather.2
  228.3 293.1 all-reduce.3
  524.2 284.9 reduce-scatter.1
where the time goes:
time: 824 us; the launch traced here: 817 us
  waiting for transfers between devices  589 us (71%)
  matrix products  97.6 us (12%)
  local copies, waits for them, and re-layouts  84.4 us (10%)
  loops' own time  16.2 us (2%)
  other arithmetic  15.4 us (2%)
  between operations  14.1 us (2%)
    psum x1, waiting for transfers between devices, local(): lax.psum(uk_grad.astype(jnp.bfloat16), ('dp', 'ctx')).astype(jnp.float32)  285 us
    reduce_scatter x1, waiting for transfers between devices, local(): lax.psum_scatter(key_grads, ('ctx', 'head'), scatter_dimension=0, tiled=T...  283 us
    dot_general x8, matrix products, value_step(): jnp.einsum('hqk,kc->hqc', probs_bf, block_keys[:, :LAT], preferred_elemen...  30.6 us
    dot_general x16, matrix products, block_scores(): jnp.einsum('hqd,kd->hqk', q_full, block_keys, preferred_element_type=jnp....  21.4 us
    all_gather x1, waiting for transfers between devices, local(): keys_all = lax.all_gather(kv_latent[0], 'ctx', axis=0, tiled=True)  20.4 us
    dynamic_slice x24, local copies, waits for them, and re-layouts, key_block(): key_places = lax.dynamic_slice_in_dim(places, block_start, tok_rows)  18.3 us
    dynamic_slice x24, local copies, waits for them, and re-layouts, key_block(): key_labels = lax.dynamic_slice_in_dim(labels, block_start, tok_rows)  18.2 us
  transfers between devices with their start and end apart: 3, of which 3 were waited for; matrix products, arithmetic and copies ran while one was open for 3% of the time, Pallas kernels for 0%

commit v1 on v0

v1 whole, which is shorter than its diff:
```python
import jax
import jax.numpy as jnp
from jax import lax
from jax.experimental import pallas as pl
from jax.experimental.pallas import tpu as pltpu
from jax.sharding import Mesh, PartitionSpec as P

LAT = 512
ROPE = 64
NOPE = 128
VDIM = 128
SEQ = 1024
SPAN = 64
SCALE = (NOPE + ROPE) ** -0.5
F32 = jnp.float32
BF16 = jnp.bfloat16
MIB = 1 << 20


def dot(a, b, dims):
    return lax.dot_general(a, b, (dims, ((), ())), preferred_element_type=F32)


NN = ((1,), (0,))
NT = ((1,), (1,))
TN = ((0,), (0,))


def pack_kernel(qn_ref, qr_ref, do_ref, kv_ref, x_ref, k_ref):
    for h in range(8):
        x_ref[h, 0:128, :] = qn_ref[0, :, h * 128:(h + 1) * 128]
        x_ref[h, 128:256, :] = do_ref[0, :, h * 128:(h + 1) * 128]
        x_ref[h, 256:320, 0:64] = qr_ref[0, 0:64, h * 64:(h + 1) * 64]
        x_ref[h, 256:320, 64:128] = qr_ref[0, 64:128, h * 64:(h + 1) * 64]
    for j in range(4):
        k_ref[j * 128:(j + 1) * 128, :] = kv_ref[0, :, j * 128:(j + 1) * 128]
    k_ref[512:576, 0:64] = kv_ref[0, 0:64, 512:576]
    k_ref[512:576, 64:128] = kv_ref[0, 64:128, 512:576]


def pack(q_nope, q_rope, d_out, kv):
    return pl.pallas_call(
        pack_kernel,
        out_shape=(
            jax.ShapeDtypeStruct((8, 320, 128), BF16),
            jax.ShapeDtypeStruct((576, 128), BF16),
        ),
        compiler_params=pltpu.CompilerParams(vmem_limit_bytes=16 * MIB),
        name="pack",
    )(q_nope, q_rope, d_out, kv)


def main_kernel(order_ref, ids_ref, x_ref, *refs):
    kv_refs = refs[:8]
    uk_ref, uv_ref, segc_ref, segr_ref = refs[8:12]
    dq_ref, keep_ref, send_ref, dw_ref = refs[12:16]
    keys, qfull, qn, g, dob, dkv, dqs, dwk, dwv = refs[16:]
    y = ids_ref[0]
    core = ids_ref[1]

    for slot in range(16):
        c, e = slot // 2, slot % 2
        row = pl.ds(pl.multiple_of(order_ref[slot] * SPAN, SPAN), SPAN)
        qn[row, :] = x_ref[c, e * 64:(e + 1) * 64, :]
        g[row, :] = x_ref[c, 128 + e * 64:128 + (e + 1) * 64, :]
        qfull[row, LAT:LAT + ROPE] = x_ref[c, 256:320, e * 64:(e + 1) * 64]
    for d in range(4):
        for cr in range(2):
            ref = kv_refs[d * 2 + cr]
            ctx = (y ^ d) * 2 + (core ^ cr)
            for e in range(2):
                row = pl.ds(pl.multiple_of(order_ref[ctx * 2 + e] * SPAN, SPAN), SPAN)
                for j in range(4):
                    keys[row, j * 128:(j + 1) * 128] = ref[j * 128 + e * 64:j * 128 + (e + 1) * 64, :]
                keys[row, LAT:LAT + ROPE] = ref[512:576, e * 64:(e + 1) * 64]
    uk = uk_ref[...]
    uv = uv_ref[...]
    qfull[:, 0:LAT] = dot(qn[...], uk, NT).astype(BF16)
    dob[...] = dot(g[...], uv, NT).astype(BF16)
    dkv[...] = jnp.zeros_like(dkv)
    dwk[...] = jnp.zeros_like(dwk)
    dwv[...] = jnp.zeros_like(dwv)

    for b in range(4):
        q0 = b * 256
        w0 = max(0, q0 - 512)
        w1 = q0 + 256
        width = w1 - w0
        kw = keys[w0:w1, :]
        qb = qfull[q0:w1, :]
        do_b = dob[q0:w1, :]
        scores = dot(qb, kw, NT) * SCALE
        rows = lax.broadcasted_iota(jnp.int32, (256, width), 0) + q0
        cols = lax.broadcasted_iota(jnp.int32, (256, width), 1) + w0
        visible = (segc_ref[q0:w1, :] == segr_ref[:, w0:w1]) & (cols <= rows)
        scores = jnp.where(visible, scores, -1e30)
        top = jnp.max(scores, axis=1, keepdims=True)
        ex = jnp.exp(scores - top)
        probs = ex * (1.0 / jnp.sum(ex, axis=1, keepdims=True))
        pb = probs.astype(BF16)
        o_lat = dot(pb, kw[:, 0:LAT], NN)
        dprobs = dot(do_b, kw[:, 0:LAT], NT)
        row_dot = jnp.sum(probs * dprobs, axis=1, keepdims=True)
        ds = (probs * (dprobs - row_dot) * SCALE).astype(BF16)
        dq = dot(ds, kw, NN)
        dkv[w0:w1, :] += dot(ds, qb, TN)
        dkv[w0:w1, 0:LAT] += dot(pb, do_b, TN)
        dql = dq[:, 0:LAT].astype(BF16)
        dqs[q0:w1, 0:128] = dot(dql, uk, NN).astype(BF16)
        dqs[q0:w1, 128:192] = dq[:, LAT:].astype(BF16)
        dwk[...] += dot(dql, qn[q0:w1, :], TN)
        dwv[...] += dot(o_lat.astype(BF16), g[q0:w1, :], TN)

    dw_ref[0:512, :] = dwk[...].astype(BF16)
    dw_ref[512:1024, :] = dwv[...].astype(BF16)
    for slot in range(16):
        c, e = slot // 2, slot % 2
        row = pl.ds(pl.multiple_of(order_ref[slot] * SPAN, SPAN), SPAN)
        dq_ref[c, e * 64:(e + 1) * 64, :] = dqs[row, 0:128]
        dq_ref[c, 128:192, e * 64:(e + 1) * 64] = dqs[row, 128:192]
        part = dkv[row, :].astype(BF16)
        out_row = pl.ds((c // 2) * 128 + e * 64, 64)

        @pl.when(core == c % 2)
        def _():
            keep_ref[out_row, :] = part

        @pl.when(core != c % 2)
        def _():
            send_ref[out_row, :] = part


def attend(order, ids, x, kvs, w_uk, w_uv, segc, segr):
    def full(shape):
        return pl.BlockSpec(shape, lambda i, order, ids: (0,) * len(shape))

    head = pl.BlockSpec((LAT, 128), lambda i, order, ids: (0, ids[0] * 2 + ids[1]))
    return pl.pallas_call(
        main_kernel,
        grid_spec=pltpu.PrefetchScalarGridSpec(
            num_scalar_prefetch=2,
            grid=(1,),
            in_specs=[full((8, 320, 128))] + [full((576, 128))] * 8
            + [head, head, full((SEQ, 1)), full((1, SEQ))],
            out_specs=[full((8, 192, 128)), full((512, 576)), full((512, 576)), full((1024, 128))],
            scratch_shapes=[
                pltpu.VMEM((SEQ, 576), BF16),
                pltpu.VMEM((SEQ, 576), BF16),
                pltpu.VMEM((SEQ, 128), BF16),
                pltpu.VMEM((SEQ, 128), BF16),
                pltpu.VMEM((SEQ, LAT), BF16),
                pltpu.VMEM((SEQ, 576), F32),
                pltpu.VMEM((SEQ, 192), BF16),
                pltpu.VMEM((LAT, 128), F32),
                pltpu.VMEM((LAT, 128), F32),
            ],
        ),
        out_shape=(
            jax.ShapeDtypeStruct((8, 192, 128), BF16),
            jax.ShapeDtypeStruct((512, 576), BF16),
            jax.ShapeDtypeStruct((512, 576), BF16),
            jax.ShapeDtypeStruct((1024, 128), BF16),
        ),
        compiler_params=pltpu.CompilerParams(vmem_limit_bytes=48 * MIB),
        name="attend",
    )(order, ids, x, *kvs, w_uk, w_uv, segc, segr)


def unpack_kernel(x_ref, qn_ref, qr_ref):
    for h in range(8):
        qn_ref[0, :, h * 128:(h + 1) * 128] = x_ref[h, 0:128, :]
        qr_ref[0, 0:64, h * 64:(h + 1) * 64] = x_ref[h, 128:192, 0:64]
        qr_ref[0, 64:128, h * 64:(h + 1) * 64] = x_ref[h, 128:192, 64:128]


def unpack(x):
    return pl.pallas_call(
        unpack_kernel,
        out_shape=(
            jax.ShapeDtypeStruct((1, 128, 1024), BF16),
            jax.ShapeDtypeStruct((1, 128, 512), BF16),
        ),
        compiler_params=pltpu.CompilerParams(vmem_limit_bytes=16 * MIB),
        name="unpack",
    )(x)


def widen_kernel(ids_ref, mine_ref, sib_ref, uk_ref, uv_ref):
    core = ids_ref[1]
    at = pl.ds(pl.multiple_of(core * 128, 128), 128)
    other = pl.ds(pl.multiple_of((1 - core) * 128, 128), 128)
    uk_ref[:, at] = mine_ref[0, 0:512, :].astype(F32)
    uk_ref[:, other] = sib_ref[0, 0:512, :].astype(F32)
    uv_ref[:, at] = mine_ref[0, 512:1024, :].astype(F32)
    uv_ref[:, other] = sib_ref[0, 512:1024, :].astype(F32)


def widen(ids, mine, sib):
    piece = pl.BlockSpec((1, 1024, 128), lambda i, ids: (i, 0, 0))
    out = pl.BlockSpec((512, 256), lambda i, ids: (0, i))
    return pl.pallas_call(
        widen_kernel,
        grid_spec=pltpu.PrefetchScalarGridSpec(
            num_scalar_prefetch=1, grid=(4,), in_specs=[piece, piece], out_specs=[out, out]
        ),
        out_shape=(jax.ShapeDtypeStruct((512, 1024), F32),) * 2,
        compiler_params=pltpu.CompilerParams(vmem_limit_bytes=16 * MIB),
        name="widen",
    )(ids, mine, sib)


def across(x, axis, step):
    size = 2 if axis == "core" else 4
    return lax.ppermute(x, axis, [(i, i ^ step) for i in range(size)])


def local(q_nope, q_rope, kv_latent, d_out, w_uk, w_uv, segment_ids, span_order):
    y = lax.axis_index("y")
    core = lax.axis_index("core")
    ids = jnp.stack([y, core]).astype(jnp.int32)
    send, kvp = pack(q_nope, q_rope, d_out, kv_latent)
    col = [kvp] + [across(kvp, "y", d) for d in (1, 2, 3)]
    x = lax.all_to_all(send, ("y", "core"), 0, 0, tiled=True)
    kvs = []
    for piece in col:
        kvs += [piece, across(piece, "core", 1)]
    dq, keep, away, dw = attend(
        span_order, ids, x, kvs, w_uk, w_uv, segment_ids.reshape(SEQ, 1), segment_ids
    )
    came = across(away, "core", 1)
    half = (keep.astype(F32) + came.astype(F32)).astype(BF16).reshape(32, 16, 576)
    parts = lax.all_to_all(half, ("y", "zl", "x"), 0, 0, tiled=True)
    d_kv = jnp.sum(parts.astype(F32), axis=0).astype(BF16)[None]
    pieces = lax.all_to_all(dw.reshape(4, 256, 128), "dp", 0, 0, tiled=True)
    total = jnp.sum(pieces.astype(F32), axis=0).astype(BF16)
    whole = lax.all_to_all(jnp.broadcast_to(total[None], (4, 256, 128)), "dp", 0, 0, tiled=True)
    whole = whole.reshape(1, 1024, 128)
    mine = lax.all_to_all(jnp.broadcast_to(whole, (4, 1024, 128)), "y", 0, 0, tiled=True)
    sib = across(mine, "core", 1)
    dw_uk, dw_uv = widen(ids, mine, sib)
    back = lax.all_to_all(dq, ("y", "core"), 0, 0, tiled=True)
    dq_nope, dq_rope = unpack(back)
    return dq_nope, dq_rope, d_kv, dw_uk, dw_uv


def solution(mesh):
    split = Mesh(mesh.devices.reshape(4, 4, 2, 2, 4), ("dp", "y", "core", "zl", "x"))
    ctx = ("y", "core")
    head = ("zl", "x")
    return jax.shard_map(
        local,
        mesh=split,
        in_specs=(
            P("dp", ctx, head),
            P("dp", ctx, head),
            P("dp", ctx, None),
            P("dp", ctx, head),
            P(None, head),
            P(None, head),
            P("dp", None),
            P(),
        ),
        out_specs=(
            P("dp", ctx, head),
            P("dp", ctx, head),
            P("dp", ctx + head, None),
            P(None, head),
            P(None, head),
        ),
        check_vma=False,
    )
```

time: 824 us -> 136 us (0.17)
  waiting for transfers between devices: 589 us -> 51.6 us
  matrix products: 97.6 us -> 0 us
  local copies, waits for them, and re-layouts: 84.4 us -> 18.3 us
  starting transfers between devices: 0.12 us -> 26.3 us
  blocking collectives: 0 us -> 19.7 us
  Pallas kernels: 0 us -> 16.2 us
  loops' own time: 16.2 us -> 0 us
  other arithmetic: 15.4 us -> 1.84 us
  between operations: 14.1 us -> 0.81 us
    psum x1 -> x0, waiting for transfers between devices: 285 us -> none  [local(): lax.psum(uk_grad.astype(jnp.bfloat16), ('dp', 'ctx')).astype(jnp.float32)]
    reduce_scatter x1 -> x0, waiting for transfers between devices: 283 us -> none  [local(): lax.psum_scatter(key_grads, ('ctx', 'head'), scatter_dimension=0, tiled=T...]
    dot_general x61 -> x0, matrix products: 97.6 us -> none  [the longest x8 30.6 us: value_step(): jnp.einsum('hqk,kc->hqc', probs_bf, block_keys[:, :LAT], preferred_elemen...]
    dynamic_slice x74 -> x0, local copies, waits for them, and re-layouts: 50.8 us -> none  [the longest x24 18.3 us: key_block(): key_places = lax.dynamic_slice_in_dim(places, block_start, tok_rows)]
    all_to_all x0 -> x5, waiting for transfers between devices: none -> 38 us  [the longest x1 10.4 us: local(): lax.all_to_all(jnp.broadcast_to(whole, (4, 1024, 128)), 'y', 0, 0, tiled=...]
    all_to_all x0 -> x5, starting transfers between devices: none -> 21.2 us  [the longest x1 6.39 us: local(): parts = lax.all_to_all(half, ('y', 'zl', 'x'), 0, 0, tiled=True)]
    all_gather x1 -> x0, waiting for transfers between devices: 20.4 us -> none  [local(): keys_all = lax.all_gather(kv_latent[0], 'ctx', axis=0, tiled=True)]
    all_to_all x0 -> x1, blocking collectives: none -> 19.7 us  [local(): pieces = lax.all_to_all(dw.reshape(4, 256, 128), 'dp', 0, 0, tiled=True)]
  transfers between devices with their start and end apart: 3 -> 14, of which waited for: 3 -> 5; matrix products, arithmetic and copies ran while one was open for 3% -> 4% of each run, Pallas kernels for 0% -> 1%
where the time goes in v1:
time: 136 us; the launch traced here: 135 us
  waiting for transfers between devices  51.6 us (38%)
  starting transfers between devices  26.3 us (19%)
  blocking collectives  19.7 us (14%)
  local copies, waits for them, and re-layouts  18.3 us (13%)
  Pallas kernels  16.2 us (12%)
  other arithmetic  1.84 us (1%)
    all_to_all x1, blocking collectives, local(): pieces = lax.all_to_all(dw.reshape(4, 256, 128), 'dp', 0, 0, tiled=True)  19.7 us
    unnamed x47, local copies, waits for them, and re-layouts  13.8 us
    ppermute x9, waiting for transfers between devices, across(): return lax.ppermute(x, axis, [(i, i ^ step) for i in range(size)])  13.7 us
    pallas_call x1, Pallas kernels, attend(): pl.pallas_call(main_kernel, grid_spec=pltpu.PrefetchScalarGridSpec(num_sc...  11.4 us
    all_to_all x1, waiting for transfers between devices, local(): lax.all_to_all(jnp.broadcast_to(whole, (4, 1024, 128)), 'y', 0, 0, tiled=...  10.4 us
    all_to_all x1, waiting for transfers between devices, local(): lax.all_to_all(jnp.broadcast_to(total[None], (4, 256, 128)), 'dp', 0, 0,...  9.7 us
    all_to_all x1, waiting for transfers between devices, local(): parts = lax.all_to_all(half, ('y', 'zl', 'x'), 0, 0, tiled=True)  9.13 us
    all_to_all x1, waiting for transfers between devices, local(): back = lax.all_to_all(dq, ('y', 'core'), 0, 0, tiled=True)  8.81 us
  transfers between devices with their start and end apart: 14, of which 5 were waited for; matrix products, arithmetic and copies ran while one was open for 4% of the time, Pallas kernels for 1%

profile of v1, /device:TPU:2, one launch (start us, length us, event | category | flops | bytes accessed | tf_op | source)
XLA Modules:
  0.0 134.8 jit_solution(6010959226448162945)
XLA Ops:
  0.6 1.1 copy.16.kv_ref
  1.7 0.9 copy-done.2
  2.7 0.9 copy-done.3
  3.6 0.9 copy-done.20
  4.5 1.0 pack.1
  5.5 4.5 %all-to-all-start = ((bf16[8,320,128]{2,1,0:T(8,128)(2,1)}), bf16[8,320,128]{2,1,0:T(8,128)(2,1)S(1)}, u32[]{:S(2)}, u32[]{:S(2)}) async-start(bf16[8,320,128]{2,1,0:T(8,128)(2,1)} %get-tuple-element.15), calls=%async_computation | async-start | bytes 1310720 | tf_op jit(solution)/shard_map/all_to_all | solution.py:223
  10.0 3.2 %collective-permute-start.5 = (bf16[576,128]{1,0:T(8,128)(2,1)S(1)}, bf16[576,128]{1,0:T(8,128)(2,1)S(1)}, u32[]{:S(2)}, u32[]{:S(2)}) collective-permute-start(bf16[576,128]{1,0:T(8,128)(2,1)S(1)} %get-tuple-element.16.refs_0_), channel_id=1, source_target_pairs={{0,48},{16,32},{32,16},{48,0},{1,49},{17,33},{33,17},{49,1},{2,50}... | collective-permute-start | bytes 442376 | tf_op jit(solution)/shard_map/ppermute | solution.py:214
  13.2 0.9 collective-permute-start.3
  14.2 13.6 %collective-permute-done.5.refs_6_ = bf16[576,128]{1,0:T(8,128)(2,1)S(1)} collective-permute-done((bf16[576,128]{1,0:T(8,128)(2,1)S(1)}, bf16[576,128]{1,0:T(8,128)(2,1)S(1)}, u32[]{:S(2)}, u32[]{:S(2)}) %collective-permute-start.5) | collective-permute-done | bytes 147488 | tf_op jit(solution)/shard_map/ppermute | solution.py:214
  31.6 0.9 copy-done.5
  32.5 0.9 copy-done.7
  33.4 0.9 copy-done.9
  34.3 0.9 copy-done.11
  35.3 0.9 copy-done.13
  36.2 0.9 copy-done.15
  37.1 0.9 copy-done.17
  38.0 0.9 copy-done.19
  38.9 11.4 %attend.1 = (bf16[8,192,128]{2,1,0:T(8,128)(2,1)S(1)}, bf16[512,576]{1,0:T(8,128)(2,1)S(1)}, bf16[512,576]{1,0:T(8,128)(2,1)S(1)}, bf16[1024,128]{1,0:T(8,128)(2,1)S(1)}) custom-call(s32[16]{0:T(128)S(1)} %copy-done.22, s32[2]{0:T(128)S(1)} %pad_add_fusion.ids_ref, bf16[8,320,128]{2,1,0:T(8,128)(2,1)S(1)} %all-to-all-done.x_ref, ...), custom_call_target="tpu_custom_call" | custom-call | tf_op jit(solution)/shard_map/attend/pallas_call | solution.py:138
  50.3 19.7 %all_to_all.30 = bf16[4,256,128]{2,1,0:T(8,128)(2,1)S(1)} all-to-all(bf16[4,256,128]{2,1,0:T(8,128)(2,1)S(1)} %bitcast.7), channel_id=1, replica_groups=mesh['dp'=4,'y'=4,'core'=2,'zl'=2,'x'=4] {'dp'}, dimensions={0} | all-to-all | bytes 524288 | tf_op jit(solution)/shard_map/all_to_all | solution.py:234
  70.0 3.5 %all-to-all-start.1 = ((bf16[8,192,128]{2,1,0:T(8,128)(2,1)}), bf16[8,192,128]{2,1,0:T(8,128)(2,1)S(1)}, u32[]{:S(2)}, u32[]{:S(2)}) async-start(bf16[8,192,128]{2,1,0:T(8,128)(2,1)} %copy-done.1), calls=%async_computation.1 | async-start | bytes 786432 | tf_op jit(solution)/shard_map/all_to_all | solution.py:241
  73.6 8.8 %all-to-all-done.1.x_ref = bf16[8,192,128]{2,1,0:T(8,128)(2,1)S(1)} async-done(((bf16[8,192,128]{2,1,0:T(8,128)(2,1)}), bf16[8,192,128]{2,1,0:T(8,128)(2,1)S(1)}, u32[]{:S(2)}, u32[]{:S(2)}) %all-to-all-start.1) | async-done | bytes 393248 | tf_op jit(solution)/shard_map/all_to_all | solution.py:241
  83.1 3.4 %all-to-all-start.4 = ((bf16[4,256,128]{2,1,0:T(8,128)(2,1)}), bf16[4,256,128]{2,1,0:T(8,128)(2,1)S(1)}, u32[]{:S(2)}, u32[]{:S(2)}) async-start(bf16[4,256,128]{2,1,0:T(8,128)(2,1)} %broadcast_in_dim.17), calls=%async_computation.4 | async-start | bytes 524288 | tf_op jit(solution)/shard_map/all_to_all | solution.py:236
  86.5 1.1 copy.18
  87.6 9.7 %all-to-all-done.4 = bf16[4,256,128]{2,1,0:T(8,128)(2,1)S(1)} async-done(((bf16[4,256,128]{2,1,0:T(8,128)(2,1)}), bf16[4,256,128]{2,1,0:T(8,128)(2,1)S(1)}, u32[]{:S(2)}, u32[]{:S(2)}) %all-to-all-start.4) | async-done | bytes 262176 | tf_op jit(solution)/shard_map/all_to_all | solution.py:236
  97.3 1.1 broadcast_in_dim.19
  98.4 3.5 %all-to-all-start.5 = ((bf16[4,1024,128]{2,1,0:T(8,128)(2,1)}), bf16[4,1024,128]{2,1,0:T(8,128)(2,1)S(1)}, u32[]{:S(2)}, u32[]{:S(2)}) async-start(bf16[4,1024,128]{2,1,0:T(8,128)(2,1)} %broadcast_in_dim.19), calls=%async_computation.5 | async-start | bytes 2097152 | tf_op jit(solution)/shard_map/all_to_all | solution.py:238
  101.9 1.4 %copy.19 = bf16[512,576]{1,0:T(8,128)(2,1)S(1)} copy(bf16[512,576]{0,1:T(8,128)(2,1)} %collective-permute-done.7) | data formatting | bytes 1179648 | tf_op jit(solution)/shard_map/ppermute | solution.py:214
  103.3 1.0 add_convert_fusion
  104.3 10.4 %all-to-all-done.5.mine_ref = bf16[4,1024,128]{2,1,0:T(8,128)(2,1)S(1)} async-done(((bf16[4,1024,128]{2,1,0:T(8,128)(2,1)}), bf16[4,1024,128]{2,1,0:T(8,128)(2,1)S(1)}, u32[]{:S(2)}, u32[]{:S(2)}) %all-to-all-start.5) | async-done | bytes 1048608 | tf_op jit(solution)/shard_map/all_to_all | solution.py:238
  114.6 6.4 %all-to-all-start.2 = ((bf16[32,16,576]{2,1,0:T(8,128)(2,1)}), bf16[32,16,576]{2,1,0:T(8,128)(2,1)S(1)}, u32[]{:S(2)}, u32[]{:S(2)}) async-start(bf16[32,16,576]{2,1,0:T(8,128)(2,1)} %bitcast.9), calls=%async_computation.2 | async-start | bytes 1310720 | tf_op jit(solution)/shard_map/all_to_all | solution.py:232
  122.0 9.1 %all-to-all-done.2 = bf16[32,16,576]{2,1,0:T(8,128)(2,1)S(1)} async-done(((bf16[32,16,576]{2,1,0:T(8,128)(2,1)}), bf16[32,16,576]{2,1,0:T(8,128)(2,1)S(1)}, u32[]{:S(2)}, u32[]{:S(2)}) %all-to-all-start.2) | async-done | bytes 589856 | tf_op jit(solution)/shard_map/all_to_all | solution.py:232
  131.8 3.0 %widen.1 = (f32[512,1024]{1,0:T(8,128)}, f32[512,1024]{1,0:T(8,128)}) custom-call(s32[2]{0:T(128)S(1)} %pad_add_fusion.ids_ref, bf16[4,1024,128]{2,1,0:T(8,128)(2,1)S(1)} %all-to-all-done.5.mine_ref, bf16[4,1024,128]{2,1,0:T(8,128)(2,1)S(1)} %collective-permute-done.8.sib_ref), custom_call_target="tpu_custom_call" | custom-call | tf_op jit(solution)/shard_map/widen/pallas_call | solution.py:201
  (57 shorter events, 6.3 us)
Async XLA Ops:
  0.6 28.0 %copy-start.21 = (s32[1,1024]{1,0:T(1,128)S(1)}, s32[1,1024]{1,0:T(1,128)}, u32[]{:S(2)}) copy-start(s32[1,1024]{1,0:T(1,128)} %refs_11_.1) | copy-start | bytes 12292
  1.7 1.0 copy-start.2
  2.7 0.9 copy-start.3
  4.5 27.1 %copy-start = (bf16[512,1024]{1,0:T(8,128)(2,1)S(1)}, bf16[512,1024]{1,0:T(8,128)(2,1)}, u32[]{:S(2)}) copy-start(bf16[512,1024]{1,0:T(8,128)(2,1)} %refs_8_.1) | copy-start | bytes 3145732
  4.5 27.1 %copy-start.22 = (s32[16]{0:T(128)S(1)}, s32[16]{0:T(128)}, u32[]{:S(2)}) copy-start(s32[16]{0:T(128)} %order_ref.1) | copy-start | bytes 196
  5.5 25.4 %copy-start.4 = (bf16[576,128]{1,0:T(8,128)(2,1)}, bf16[576,128]{1,0:T(8,128)(2,1)S(1)}, u32[]{:S(2)}) copy-start(bf16[576,128]{1,0:T(8,128)(2,1)S(1)} %get-tuple-element.16.refs_0_) | copy-start | bytes 442372
  5.5 26.1 %all-to-all-start = ((bf16[8,320,128]{2,1,0:T(8,128)(2,1)}), bf16[8,320,128]{2,1,0:T(8,128)(2,1)S(1)}, u32[]{:S(2)}, u32[]{:S(2)}) async-start(bf16[8,320,128]{2,1,0:T(8,128)(2,1)} %get-tuple-element.15), calls=%async_computation | async-start | bytes 1310720 | tf_op jit(solution)/shard_map/all_to_all | solution.py:223
  10.0 17.8 %collective-permute-start.5 = (bf16[576,128]{1,0:T(8,128)(2,1)S(1)}, bf16[576,128]{1,0:T(8,128)(2,1)S(1)}, u32[]{:S(2)}, u32[]{:S(2)}) collective-permute-start(bf16[576,128]{1,0:T(8,128)(2,1)S(1)} %get-tuple-element.16.refs_0_), channel_id=1, source_target_pairs={{0,48},{16,32},{32,16},{48,0},{1,49},{17,33},{33,17},{49,1},{2,50}... | collective-permute-start | bytes 442376 | tf_op jit(solution)/shard_map/ppermute | solution.py:214
  13.2 14.6 %collective-permute-start.3 = (bf16[576,128]{1,0:T(8,128)(2,1)S(1)}, bf16[576,128]{1,0:T(8,128)(2,1)S(1)}, u32[]{:S(2)}, u32[]{:S(2)}) collective-permute-start(bf16[576,128]{1,0:T(8,128)(2,1)S(1)} %get-tuple-element.16.refs_0_), channel_id=1, source_target_pairs={{0,32},{16,48},{32,0},{48,16},{1,33},{17,49},{33,1},{49,17},{2,34}... | collective-permute-start | bytes 442376 | tf_op jit(solution)/shard_map/ppermute | solution.py:214
  14.1 14.2 %collective-permute-start.1 = (bf16[576,128]{1,0:T(8,128)(2,1)S(1)}, bf16[576,128]{1,0:T(8,128)(2,1)S(1)}, u32[]{:S(2)}, u32[]{:S(2)}) collective-permute-start(bf16[576,128]{1,0:T(8,128)(2,1)S(1)} %get-tuple-element.16.refs_0_), channel_id=1, source_target_pairs={{0,16},{16,0},{32,48},{48,32},{1,17},{17,1},{33,49},{49,33},{2,18}... | collective-permute-start | bytes 442376 | tf_op jit(solution)/shard_map/ppermute | solution.py:214
  14.2 14.8 %collective-permute-start = (bf16[576,128]{1,0:T(8,128)(2,1)S(1)}, bf16[576,128]{1,0:T(8,128)(2,1)S(1)}, u32[]{:S(2)}, u32[]{:S(2)}) collective-permute-start(bf16[576,128]{1,0:T(8,128)(2,1)S(1)} %get-tuple-element.16.refs_0_), channel_id=1, source_target_pairs={{0,8},{8,0},{1,9},{9,1},{2,10},{10,2},{3,11},{11,3},{4,12},{12,4},... | collective-permute-start | bytes 442376 | tf_op jit(solution)/shard_map/ppermute | solution.py:214
  27.8 3.1 %copy-start.6 = (bf16[576,128]{1,0:T(8,128)(2,1)}, bf16[576,128]{1,0:T(8,128)(2,1)S(1)}, u32[]{:S(2)}) copy-start(bf16[576,128]{1,0:T(8,128)(2,1)S(1)} %collective-permute-done.5.refs_6_) | copy-start | bytes 442372
  27.8 1.8 %collective-permute-start.6 = (bf16[576,128]{1,0:T(8,128)(2,1)S(1)}, bf16[576,128]{1,0:T(8,128)(2,1)S(1)}, u32[]{:S(2)}, u32[]{:S(2)}) collective-permute-start(bf16[576,128]{1,0:T(8,128)(2,1)S(1)} %collective-permute-done.5.refs_6_), channel_id=1, source_target_pairs={{0,8},{8,0},{1,9},{9,1},{2,10},{10,2},{3,11},{11,3},{4,12},{12,4},... | collective-permute-start | bytes 442376 | tf_op jit(solution)/shard_map/ppermute | solution.py:214
  27.8 3.1 %copy-start.8 = (bf16[576,128]{1,0:T(8,128)(2,1)}, bf16[576,128]{1,0:T(8,128)(2,1)S(1)}, u32[]{:S(2)}) copy-start(bf16[576,128]{1,0:T(8,128)(2,1)S(1)} %collective-permute-done.3.refs_4_) | copy-start | bytes 442372
  27.8 2.4 %collective-permute-start.4 = (bf16[576,128]{1,0:T(8,128)(2,1)S(1)}, bf16[576,128]{1,0:T(8,128)(2,1)S(1)}, u32[]{:S(2)}, u32[]{:S(2)}) collective-permute-start(bf16[576,128]{1,0:T(8,128)(2,1)S(1)} %collective-permute-done.3.refs_4_), channel_id=1, source_target_pairs={{0,8},{8,0},{1,9},{9,1},{2,10},{10,2},{3,11},{11,3},{4,12},{12,4},... | collective-permute-start | bytes 442376 | tf_op jit(solution)/shard_map/ppermute | solution.py:214
  28.3 2.6 %copy-start.10 = (bf16[576,128]{1,0:T(8,128)(2,1)}, bf16[576,128]{1,0:T(8,128)(2,1)S(1)}, u32[]{:S(2)}) copy-start(bf16[576,128]{1,0:T(8,128)(2,1)S(1)} %collective-permute-done.1.refs_2_) | copy-start | bytes 442372
  28.3 2.6 %collective-permute-start.2 = (bf16[576,128]{1,0:T(8,128)(2,1)S(1)}, bf16[576,128]{1,0:T(8,128)(2,1)S(1)}, u32[]{:S(2)}, u32[]{:S(2)}) collective-permute-start(bf16[576,128]{1,0:T(8,128)(2,1)S(1)} %collective-permute-done.1.refs_2_), channel_id=1, source_target_pairs={{0,8},{8,0},{1,9},{9,1},{2,10},{10,2},{3,11},{11,3},{4,12},{12,4},... | collective-permute-start | bytes 442376 | tf_op jit(solution)/shard_map/ppermute | solution.py:214
  31.6 0.9 copy-start.5
  32.5 0.9 copy-start.7
  33.4 0.9 copy-start.9
  34.3 0.9 copy-start.11
  35.3 0.9 copy-start.13
  36.2 0.9 copy-start.15
  37.1 0.9 copy-start.17
  38.0 0.9 copy-start.19
  50.3 19.8 %copy-start.1 = (bf16[8,192,128]{2,1,0:T(8,128)(2,1)}, bf16[8,192,128]{2,1,0:T(8,128)(2,1)S(1)}, u32[]{:S(2)}) copy-start(bf16[8,192,128]{2,1,0:T(8,128)(2,1)S(1)} %get-tuple-element.17) | copy-start | bytes 1179652
  70.0 12.3 %all-to-all-start.1 = ((bf16[8,192,128]{2,1,0:T(8,128)(2,1)}), bf16[8,192,128]{2,1,0:T(8,128)(2,1)S(1)}, u32[]{:S(2)}, u32[]{:S(2)}) async-start(bf16[8,192,128]{2,1,0:T(8,128)(2,1)} %copy-done.1), calls=%async_computation.1 | async-start | bytes 786432 | tf_op jit(solution)/shard_map/all_to_all | solution.py:241
  83.1 14.2 %all-to-all-start.4 = ((bf16[4,256,128]{2,1,0:T(8,128)(2,1)}), bf16[4,256,128]{2,1,0:T(8,128)(2,1)S(1)}, u32[]{:S(2)}, u32[]{:S(2)}) async-start(bf16[4,256,128]{2,1,0:T(8,128)(2,1)} %broadcast_in_dim.17), calls=%async_computation.4 | async-start | bytes 524288 | tf_op jit(solution)/shard_map/all_to_all | solution.py:236
  87.6 14.3 %collective-permute-start.7 = (bf16[512,576]{0,1:T(8,128)(2,1)}, bf16[512,576]{0,1:T(8,128)(2,1)}, u32[]{:S(2)}, u32[]{:S(2)}) collective-permute-start(bf16[512,576]{0,1:T(8,128)(2,1)} %copy.18), channel_id=1, source_target_pairs={{0,8},{8,0},{1,9},{9,1},{2,10},{10,2},{3,11},{11,3},{4,12},{12,4},... | collective-permute-start | bytes 1769480 | tf_op jit(solution)/shard_map/ppermute | solution.py:214
  98.4 16.2 %all-to-all-start.5 = ((bf16[4,1024,128]{2,1,0:T(8,128)(2,1)}), bf16[4,1024,128]{2,1,0:T(8,128)(2,1)S(1)}, u32[]{:S(2)}, u32[]{:S(2)}) async-start(bf16[4,1024,128]{2,1,0:T(8,128)(2,1)} %broadcast_in_dim.19), calls=%async_computation.5 | async-start | bytes 2097152 | tf_op jit(solution)/shard_map/all_to_all | solution.py:238
  114.6 16.5 %all-to-all-start.2 = ((bf16[32,16,576]{2,1,0:T(8,128)(2,1)}), bf16[32,16,576]{2,1,0:T(8,128)(2,1)S(1)}, u32[]{:S(2)}, u32[]{:S(2)}) async-start(bf16[32,16,576]{2,1,0:T(8,128)(2,1)} %bitcast.9), calls=%async_computation.2 | async-start | bytes 1310720 | tf_op jit(solution)/shard_map/all_to_all | solution.py:232
  121.0 10.8 %collective-permute-start.8 = (bf16[4,1024,128]{2,1,0:T(8,128)(2,1)S(1)}, bf16[4,1024,128]{2,1,0:T(8,128)(2,1)S(1)}, u32[]{:S(2)}, u32[]{:S(2)}) collective-permute-start(bf16[4,1024,128]{2,1,0:T(8,128)(2,1)S(1)} %all-to-all-done.5.mine_ref), channel_id=1, source_target_pairs={{0,8},{8,0},{1,9},{9,1},{2,10},{10,2},{3,11},{11,3},{4,12},{12,4},... | collective-permute-start | bytes 3145736 | tf_op jit(solution)/shard_map/ppermute | solution.py:214
  (5 other events, 3.5 us)

commit v2 on v1

v2 whole, which is shorter than its diff:
```python
import jax
import jax.numpy as jnp
from jax import lax
from jax.experimental import pallas as pl
from jax.experimental.pallas import tpu as pltpu
from jax.sharding import Mesh, PartitionSpec as P

LAT = 512
ROPE = 64
NOPE = 128
VDIM = 128
SEQ = 1024
SPAN = 64
SCALE = (NOPE + ROPE) ** -0.5
F32 = jnp.float32
BF16 = jnp.bfloat16
MIB = 1 << 20
LOG2E = 1.4426950408889634


def dot(a, b, dims):
    return lax.dot_general(a, b, (dims, ((), ())), preferred_element_type=F32)


NN = ((1,), (0,))
NT = ((1,), (1,))
TN = ((0,), (0,))


def pack_kernel(qn_ref, qr_ref, do_ref, after_ref, x_ref):
    for h in range(8):
        x_ref[h, 0:128, :] = qn_ref[0, :, h * 128:(h + 1) * 128]
        x_ref[h, 128:256, :] = do_ref[0, :, h * 128:(h + 1) * 128]
        x_ref[h, 256:320, 0:64] = qr_ref[0, 0:64, h * 64:(h + 1) * 64]
        x_ref[h, 256:320, 64:128] = qr_ref[0, 64:128, h * 64:(h + 1) * 64]


def pack(q_nope, q_rope, d_out, after):
    whole = pl.BlockSpec(memory_space=pltpu.VMEM)
    return pl.pallas_call(
        pack_kernel,
        in_specs=[whole] * 3 + [pl.BlockSpec(memory_space=pl.ANY)],
        out_specs=whole,
        out_shape=jax.ShapeDtypeStruct((8, 320, 128), BF16),
        compiler_params=pltpu.CompilerParams(vmem_limit_bytes=60 * MIB),
        cost_estimate=pl.CostEstimate(flops=0, bytes_accessed=5 * MIB, transcendentals=0),
        name="pack",
    )(q_nope, q_rope, d_out, after)


def attend_kernel(order_ref, x_hbm, *refs):
    kv_hbm = refs[:8]
    uk_hbm, uv_hbm, seg_ref = refs[8:11]
    back_ref = refs[11]
    dw_refs = refs[12:16]
    x_in, kv_in, uk_in, uv_in, keys, keyt, qfull, qn, g, dob, pt, dst, ot, dqt, dqr, dqs, dkv, dw, sems = refs[16:]
    y = lax.axis_index("y")
    core = lax.axis_index("core")
    me = y * 2 + core
    block = y ^ lax.axis_index("x")
    cols = pl.ds(pl.multiple_of(me * 128, 128), 128)

    load_x = pltpu.make_async_copy(x_hbm, x_in, sems.at[8])
    load_uk = pltpu.make_async_copy(uk_hbm.at[:, cols], uk_in, sems.at[9])
    load_uv = pltpu.make_async_copy(uv_hbm.at[:, cols], uv_in, sems.at[10])
    loads = [pltpu.make_async_copy(kv_hbm[i], kv_in.at[i], sems.at[i]) for i in range(8)]
    for load in [load_x, load_uk, load_uv] + loads:
        load.start()

    load_x.wait()
    for slot in range(16):
        c, e = slot // 2, slot % 2
        row = pl.ds(pl.multiple_of(order_ref[slot] * SPAN, SPAN), SPAN)
        qn[row, :] = x_in[c, e * 64:(e + 1) * 64, :]
        g[row, :] = x_in[c, 128 + e * 64:128 + (e + 1) * 64, :]
        qfull[row, LAT:LAT + ROPE] = x_in[c, 256:320, e * 64:(e + 1) * 64]
    load_uk.wait()
    load_uv.wait()
    uk = uk_in[...]
    qfull[:, 0:LAT] = dot(qn[...], uk, NT).astype(BF16)
    dob[...] = dot(g[...], uv_in[...], NT).astype(BF16)
    for d in range(4):
        for cr in range(2):
            i = d * 2 + cr
            ctx = (block ^ d) * 2 + (core ^ cr)
            loads[i].wait()
            piece = jnp.transpose(kv_in[i], (1, 0))
            for e in range(2):
                row = pl.ds(pl.multiple_of(order_ref[ctx * 2 + e] * SPAN, SPAN), SPAN)
                keys[row, :] = piece[e * 64:(e + 1) * 64, :]
    for b in range(4):
        keyt[:, b * 256:(b + 1) * 256] = jnp.transpose(keys[b * 256:(b + 1) * 256, :], (1, 0))
    seg = seg_ref[...]
    begin = jnp.zeros_like(seg)
    for v in range(1, 4):
        below = jnp.sum((seg < v).astype(jnp.int32), axis=1, keepdims=True)
        begin = jnp.where(seg >= v, below, begin)

    def window(b):
        return max(0, b * 256 - 512), b * 256, b * 256 + 256

    def products(b):
        w0, q0, w1 = window(b)
        kw = keys[w0:w1, :]
        return dot(kw, qfull[q0:w1, :], NT), dot(kw[:, 0:LAT], dob[q0:w1, :], NT)

    def softmax(b, scores, dprobs):
        w0, q0, w1 = window(b)
        width = w1 - w0
        k_at = lax.broadcasted_iota(jnp.int32, (width, 256), 0) + w0
        q_at = lax.broadcasted_iota(jnp.int32, (1, 256), 1) + q0
        visible = (k_at >= begin[:, q0:w1]) & (k_at <= q_at)
        scores = jnp.where(visible, scores, -1e30)
        top = jnp.max(scores, axis=0, keepdims=True)
        ex = jnp.exp2((scores - top) * (SCALE * LOG2E))
        probs = ex * (1.0 / jnp.sum(ex, axis=0, keepdims=True))
        row_dot = jnp.sum(probs * dprobs, axis=0, keepdims=True)
        pb = probs.astype(BF16)
        ds = ((probs * SCALE) * (dprobs - row_dot)).astype(BF16)
        pt[b, 0:width, :] = pb
        dst[b, 0:width, :] = ds

    def outputs(b):
        w0, q0, w1 = window(b)
        width = w1 - w0
        ot[:, q0:w1] = dot(keyt[0:LAT, w0:w1], pt[b, 0:width, :], NN).astype(BF16)
        dq = dot(keyt[:, w0:w1], dst[b, 0:width, :], NN)
        dqt[:, q0:w1] = dq[0:LAT, :].astype(BF16)
        dqr[:, q0:w1] = dq[LAT:, :].astype(BF16)

    flight = products(0)
    for b in range(4):
        following = products(b + 1) if b < 3 else None
        softmax(b, *flight)
        outputs(b)
        flight = following
    dw[0:512, :] = dot(dqt[...], qn[...], NN).astype(BF16)
    dw[512:1024, :] = dot(ot[...], g[...], NN).astype(BF16)
    dp = lax.axis_index("dp")
    for d in range(4):
        dw_refs[d][...] = dw[pl.ds(pl.multiple_of((dp ^ d) * 256, 256), 256), :]
    dqs[:, 0:128] = dot(dqt[...], uk, TN).astype(BF16)
    dqs[:, 128:192] = jnp.transpose(dqr[...], (1, 0))
    for slot in range(16):
        c, e = slot // 2, slot % 2
        row = pl.ds(pl.multiple_of(order_ref[slot] * SPAN, SPAN), SPAN)
        back_ref[c, 576 + e * 64:576 + (e + 1) * 64, :] = dqs[row, 0:128]
        back_ref[c, 704:768, e * 64:(e + 1) * 64] = dqs[row, 128:192]

    for kb in range(4):
        last = min(kb + 3, 4)
        ds = []
        pb = []
        for b in range(kb, last):
            at = kb * 256 - max(0, b * 256 - 512)
            ds.append(dst[b, at:at + 256, :])
            pb.append(pt[b, at:at + 256, :])
        ds = jnp.concatenate(ds, axis=1)
        pb = jnp.concatenate(pb, axis=1)
        lo, hi = kb * 256, last * 256
        dkv[lo:lo + 256, 0:LAT] = (dot(ds, qfull[lo:hi, 0:LAT], NN) + dot(pb, dob[lo:hi, :], NN)).astype(BF16)
        dkv[lo:lo + 256, LAT:] = dot(ds, qfull[lo:hi, LAT:], NN).astype(BF16)
    for slot in range(16):
        c, e = slot // 2, slot % 2
        row = pl.ds(pl.multiple_of(order_ref[slot] * SPAN, SPAN), SPAN)
        for j in range(4):
            back_ref[c, j * 128 + e * 64:j * 128 + (e + 1) * 64, :] = dkv[row, j * 128:(j + 1) * 128]
        back_ref[c, 512:576, e * 64:(e + 1) * 64] = dkv[row, LAT:LAT + ROPE]


def attend(order, x, kvs, w_uk, w_uv, seg):
    hbm = pl.BlockSpec(memory_space=pl.ANY)
    vmem = pl.BlockSpec(memory_space=pltpu.VMEM)
    outs = [(8, 768, 128)] + [(256, 128)] * 4
    return pl.pallas_call(
        attend_kernel,
        in_specs=[pl.BlockSpec(memory_space=pltpu.SMEM)] + [hbm] * 11 + [vmem],
        out_specs=[vmem] * 5,
        scratch_shapes=[
            pltpu.VMEM((8, 320, 128), BF16),
            pltpu.VMEM((8, 576, 128), BF16),
            pltpu.VMEM((LAT, 128), BF16),
            pltpu.VMEM((LAT, 128), BF16),
            pltpu.VMEM((SEQ, 576), BF16),
            pltpu.VMEM((576, SEQ), BF16),
            pltpu.VMEM((SEQ, 576), BF16),
            pltpu.VMEM((SEQ, 128), BF16),
            pltpu.VMEM((SEQ, 128), BF16),
            pltpu.VMEM((SEQ, LAT), BF16),
            pltpu.VMEM((4, 768, 256), BF16),
            pltpu.VMEM((4, 768, 256), BF16),
            pltpu.VMEM((LAT, SEQ), BF16),
            pltpu.VMEM((LAT, SEQ), BF16),
            pltpu.VMEM((64, SEQ), BF16),
            pltpu.VMEM((SEQ, 192), BF16),
            pltpu.VMEM((SEQ, 576), BF16),
            pltpu.VMEM((1024, 128), BF16),
            pltpu.SemaphoreType.DMA((11,)),
        ],
        out_shape=[jax.ShapeDtypeStruct(shape, BF16) for shape in outs],
        compiler_params=pltpu.CompilerParams(vmem_limit_bytes=60 * MIB),
        cost_estimate=pl.CostEstimate(flops=9_000_000_000, bytes_accessed=12 * MIB, transcendentals=600_000),
        name="attend",
    )(order, x, *kvs, w_uk, w_uv, seg)


def call(kernel, name, out, *args):
    return pl.pallas_call(
        kernel,
        out_shape=out,
        compiler_params=pltpu.CompilerParams(vmem_limit_bytes=16 * MIB),
        cost_estimate=pl.CostEstimate(flops=0, bytes_accessed=3 * MIB, transcendentals=0),
        name=name,
    )(*args)


def sum4_kernel(a_ref, b_ref, c_ref, d_ref, out_ref):
    total = (a_ref[...].astype(F32) + b_ref[...].astype(F32)) + (c_ref[...].astype(F32) + d_ref[...].astype(F32))
    out_ref[...] = total.astype(BF16)


def sum_ctx_kernel(x_ref, out_ref):
    total = x_ref[0].astype(F32)
    for i in range(1, 8):
        total = total + x_ref[i].astype(F32)
    total = total.astype(BF16)
    for i in range(8):
        for j in range(4):
            out_ref[i, :, j * 128:(j + 1) * 128] = total[j * 128 + i * 16:j * 128 + (i + 1) * 16, :]
        lane = (i // 4) * 64
        low = 512 + (i % 4) * 16
        out_ref[i, :, 512:576] = total[low:low + 16, lane:lane + 64]
        out_ref[i, :, 576:640] = jnp.zeros((16, 64), BF16)


def sum_ctx(x):
    return pl.pallas_call(
        sum_ctx_kernel,
        grid=(1,),
        in_specs=[pl.BlockSpec((8, 576, 128), lambda i: (0, 0, 0))],
        out_specs=pl.BlockSpec((8, 16, 640), lambda i: (0, 0, 0)),
        out_shape=jax.ShapeDtypeStruct((8, 16, 640), BF16),
        compiler_params=pltpu.CompilerParams(vmem_limit_bytes=16 * MIB),
        name="sum_ctx",
    )(x)


def sum_head_kernel(x_ref, out_ref):
    total = x_ref[0].astype(F32)
    for i in range(1, 8):
        total = total + x_ref[i].astype(F32)
    out_ref[0] = total[:, 0:576].astype(BF16)


def join_kernel(a_ref, b_ref, c_ref, d_ref, out_ref):
    dp = lax.axis_index("dp")
    for d, ref in enumerate((a_ref, b_ref, c_ref, d_ref)):
        out_ref[pl.ds(pl.multiple_of((dp ^ d) * 256, 256), 256), :] = ref[...]


def unpack_kernel(x_ref, qn_ref, qr_ref):
    for h in range(8):
        qn_ref[0, :, h * 128:(h + 1) * 128] = x_ref[h, 0:128, :]
        qr_ref[0, 0:64, h * 64:(h + 1) * 64] = x_ref[h, 128:192, 0:64]
        qr_ref[0, 64:128, h * 64:(h + 1) * 64] = x_ref[h, 128:192, 64:128]


def unpack(x):
    return pl.pallas_call(
        unpack_kernel,
        grid=(1,),
        in_specs=[pl.BlockSpec((8, 192, 128), lambda i: (0, 3, 0))],
        out_specs=[
            pl.BlockSpec((1, 128, 1024), lambda i: (0, 0, 0)),
            pl.BlockSpec((1, 128, 512), lambda i: (0, 0, 0)),
        ],
        out_shape=(
            jax.ShapeDtypeStruct((1, 128, 1024), BF16),
            jax.ShapeDtypeStruct((1, 128, 512), BF16),
        ),
        compiler_params=pltpu.CompilerParams(vmem_limit_bytes=16 * MIB),
        name="unpack",
    )(x)


def widen_kernel(*refs):
    uk_ref, uv_ref = refs[8:]
    y = lax.axis_index("y")
    core = lax.axis_index("core")
    for d in range(4):

        @pl.when(pl.program_id(0) == (y ^ d))
        def _():
            for cr in range(2):
                ref = refs[d * 2 + cr]
                at = pl.ds(pl.multiple_of((core ^ cr) * 128, 128), 128)
                uk_ref[:, at] = ref[0:512, :].astype(F32)
                uv_ref[:, at] = ref[512:1024, :].astype(F32)


def widen(pieces):
    piece = pl.BlockSpec((1024, 128), lambda i: (0, 0))
    out = pl.BlockSpec((512, 256), lambda i: (0, i))
    return pl.pallas_call(
        widen_kernel,
        grid=(4,),
        in_specs=[piece] * 8,
        out_specs=[out, out],
        out_shape=(jax.ShapeDtypeStruct((512, 1024), F32),) * 2,
        compiler_params=pltpu.CompilerParams(vmem_limit_bytes=16 * MIB),
        name="widen",
    )(*pieces)


SIZES = {"core": 2, "x": 4, "y": 4, "dp": 4}


def across(x, axis, step):
    return lax.ppermute(x, axis, [(i, i ^ step) for i in range(SIZES[axis])])


def local(q_nope, q_rope, kv_latent, d_out, w_uk, w_uv, segment_ids, span_order):
    kvt = kv_latent[0].T
    skew = [(i * 4 + j, (i ^ j) * 4 + j) for i in range(4) for j in range(4)]
    first = lax.ppermute(kvt, ("y", "x"), skew)
    kvs = []
    for piece in [first] + [across(first, "x", d) for d in (1, 2, 3)]:
        kvs += [piece, across(piece, "core", 1)]
    send = pack(q_nope, q_rope, d_out, kvt)
    send, first = lax.optimization_barrier((send, first))
    x = lax.all_to_all(send, ("y", "core"), 0, 0, tiled=True)
    back, dw0, dw1, dw2, dw3 = attend(span_order, x, kvs, w_uk, w_uv, segment_ids)
    back = lax.all_to_all(back, ("y", "core"), 0, 0, tiled=True)
    dq_nope, dq_rope = unpack(back)
    parts = lax.all_to_all(sum_ctx(back), ("zl", "x"), 0, 0, tiled=True)
    d_kv = call(sum_head_kernel, "sum_head", jax.ShapeDtypeStruct((1, 16, 576), BF16), parts)
    chunk = jax.ShapeDtypeStruct((256, 128), BF16)
    total = call(sum4_kernel, "sum4", chunk, dw0, across(dw1, "dp", 1), across(dw2, "dp", 2), across(dw3, "dp", 3))
    gathered = [across(total, "dp", d) for d in (1, 2, 3)]
    whole = call(join_kernel, "join", jax.ShapeDtypeStruct((1024, 128), BF16), total, *gathered)
    pieces = []
    for piece in [whole] + [across(whole, "y", d) for d in (1, 2, 3)]:
        pieces += [piece, across(piece, "core", 1)]
    dw_uk, dw_uv = widen(pieces)
    return dq_nope, dq_rope, d_kv, dw_uk, dw_uv


def solution(mesh):
    split = Mesh(mesh.devices.reshape(4, 4, 2, 2, 4), ("dp", "y", "core", "zl", "x"))
    ctx = ("y", "core")
    head = ("zl", "x")
    return jax.shard_map(
        local,
        mesh=split,
        in_specs=(
            P("dp", ctx, head),
            P("dp", ctx, head),
            P("dp", ctx, None),
            P("dp", ctx, head),
            P(None, head),
            P(None, head),
            P("dp", None),
            P(),
        ),
        out_specs=(
            P("dp", ctx, head),
            P("dp", ctx, head),
            P("dp", ctx + head, None),
            P(None, head),
            P(None, head),
        ),
        check_vma=False,
    )
```

time: 136 us -> 95.6 us (0.70)
  waiting for transfers between devices: 51.6 us -> 30.7 us
  blocking collectives: 19.7 us -> 0 us
  local copies, waits for them, and re-layouts: 18.3 us -> 1.47 us
  starting transfers between devices: 26.3 us -> 43 us
  other arithmetic: 1.84 us -> 0 us
  Pallas kernels: 16.2 us -> 18 us
    all_to_all x4 -> x2, waiting for transfers between devices: 38 us -> 0.01 us  [the longest x1 0.01 us: local(): parts = lax.all_to_all(sum_ctx(back), ('zl', 'x'), 0, 0, tiled=True)]
    ppermute x9 -> x21, starting transfers between devices: 5.03 us -> 28.9 us  [the longest x20 25.4 us: across(): return lax.ppermute(x, axis, [(i, i ^ step) for i in range(SIZES[axis])])]
    all_to_all x1 -> x0, blocking collectives: 19.7 us -> none  [local(): pieces = lax.all_to_all(dw.reshape(4, 256, 128), 'dp', 0, 0, tiled=True)]
    ppermute x9 -> x21, waiting for transfers between devices: 13.7 us -> 30.7 us  [the longest x20 28.5 us: across(): return lax.ppermute(x, axis, [(i, i ^ step) for i in range(SIZES[axis])])]
    unnamed x47 -> x26, local copies, waits for them, and re-layouts: 13.8 us -> 1.47 us
    all_to_all x4 -> x2, starting transfers between devices: 16.8 us -> 9.65 us  [the longest x1 5.08 us: local(): parts = lax.all_to_all(sum_ctx(back), ('zl', 'x'), 0, 0, tiled=True)]
    broadcast_in_dim x2 -> x0, local copies, waits for them, and re-layouts: 1.84 us -> none  [the longest x1 1.11 us: local(): jnp.broadcast_to(whole, (4, 1024, 128))]
    pallas_call x4 -> x8, Pallas kernels: 16.2 us -> 18 us  [the longest x1 11 us: attend(): pl.pallas_call(attend_kernel, in_specs=[pl.BlockSpec(memory_space=pltpu.S...]
  transfers between devices with their start and end apart: 14 -> 24, of which waited for: 5 -> 13; matrix products, arithmetic and copies ran while one was open for 4% -> 0% of each run, Pallas kernels for 1% -> 7%
where the time goes in v2:
time: 95.6 us; the launch traced here: 93.9 us
  starting transfers between devices  43 us (45%)
  waiting for transfers between devices  30.7 us (32%)
  Pallas kernels  18 us (19%)
  local copies, waits for them, and re-layouts  1.47 us (2%)
    ppermute x20, waiting for transfers between devices, across(): return lax.ppermute(x, axis, [(i, i ^ step) for i in range(SIZES[axis])])  28.5 us
    ppermute x20, starting transfers between devices, across(): return lax.ppermute(x, axis, [(i, i ^ step) for i in range(SIZES[axis])])  25.4 us
    pallas_call x1, Pallas kernels, attend(): pl.pallas_call(attend_kernel, in_specs=[pl.BlockSpec(memory_space=pltpu.S...  11 us
    all_to_all x1, starting transfers between devices, local(): parts = lax.all_to_all(sum_ctx(back), ('zl', 'x'), 0, 0, tiled=True)  5.08 us
    all_to_all x1, starting transfers between devices, local(): back = lax.all_to_all(back, ('y', 'core'), 0, 0, tiled=True)  4.57 us
    all_to_all x1, starting transfers between devices, local(): x = lax.all_to_all(send, ('y', 'core'), 0, 0, tiled=True)  4.47 us
    ppermute x1, starting transfers between devices, local(): first = lax.ppermute(kvt, ('y', 'x'), skew)  3.48 us
    pallas_call x1, Pallas kernels, widen(): pl.pallas_call(widen_kernel, grid=(4,), in_specs=[piece] * 8, out_specs=[...  2.46 us
  transfers between devices with their start and end apart: 24, of which 13 were waited for; matrix products, arithmetic and copies ran while one was open for 0% of the time, Pallas kernels for 7%

profile of v2, /device:TPU:2, one launch (start us, length us, event | category | flops | bytes accessed | tf_op | source)
XLA Modules:
  0.0 93.9 jit_solution(10489636387821677569)
XLA Ops:
  0.6 3.5 %collective-permute-start = (bf16[576,128]{1,0:T(8,128)(2,1)}, bf16[576,128]{1,0:T(8,128)(2,1)S(1)}, u32[]{:S(2)}, u32[]{:S(2)}) collective-permute-start(bf16[576,128]{1,0:T(8,128)(2,1)} %bitcast.3), channel_id=1, source_target_pairs={{0,0},{1,17},{2,34},{3,51},{16,16},{17,1},{18,50},{19,35},{32,32},... | collective-permute-start | bytes 442376 | tf_op jit(solution)/shard_map/ppermute | solution.py:325
  4.1 2.1 %pack.1 = bf16[8,320,128]{2,1,0:T(8,128)(2,1)} custom-call(bf16[1,128,1024]{2,1,0:T(8,128)(2,1)} %qn_ref.1, bf16[1,128,512]{2,1,0:T(8,128)(2,1)} %qr_ref.1, bf16[1,128,1024]{2,1,0:T(8,128)(2,1)} %do_ref.1, bf16[576,128]{1,0:T(8,128)(2,1)} %bitcast.4), custom_call_target="tpu_custom_call" | custom-call | bytes 5242880 | tf_op jit(solution)/shard_map/pack/pallas_call | solution.py:40
  6.2 2.1 %collective-permute-done.refs_0_ = bf16[576,128]{1,0:T(8,128)(2,1)S(1)} collective-permute-done((bf16[576,128]{1,0:T(8,128)(2,1)}, bf16[576,128]{1,0:T(8,128)(2,1)S(1)}, u32[]{:S(2)}, u32[]{:S(2)}) %collective-permute-start) | collective-permute-done | bytes 147488 | tf_op jit(solution)/shard_map/ppermute | solution.py:325
  8.3 4.5 %all-to-all-start = ((bf16[8,320,128]{2,1,0:T(8,128)(2,1)}), bf16[8,320,128]{2,1,0:T(8,128)(2,1)S(1)}, u32[]{:S(2)}, u32[]{:S(2)}) async-start(bf16[8,320,128]{2,1,0:T(8,128)(2,1)} %pack.1), calls=%async_computation | async-start | bytes 1310720 | tf_op jit(solution)/shard_map/all_to_all | solution.py:331
  12.8 3.0 %collective-permute-start.6 = (bf16[576,128]{1,0:T(8,128)(2,1)S(1)}, bf16[576,128]{1,0:T(8,128)(2,1)S(1)}, u32[]{:S(2)}, u32[]{:S(2)}) collective-permute-start(bf16[576,128]{1,0:T(8,128)(2,1)S(1)} %collective-permute-done.refs_0_), channel_id=1, source_target_pairs={{0,3},{1,2},{2,1},{3,0},{4,7},{5,6},{6,5},{7,4},{8,11},{9,10},{10,... | collective-permute-start | bytes 442376 | tf_op jit(solution)/shard_map/ppermute | solution.py:319
  16.0 1.9 %collective-permute-start.2 = (bf16[576,128]{1,0:T(8,128)(2,1)S(1)}, bf16[576,128]{1,0:T(8,128)(2,1)S(1)}, u32[]{:S(2)}, u32[]{:S(2)}) collective-permute-start(bf16[576,128]{1,0:T(8,128)(2,1)S(1)} %collective-permute-done.refs_0_), channel_id=1, source_target_pairs={{0,1},{1,0},{2,3},{3,2},{4,5},{5,4},{6,7},{7,6},{8,9},{9,8},{10,11... | collective-permute-start | bytes 442376 | tf_op jit(solution)/shard_map/ppermute | solution.py:319
  18.0 4.9 %collective-permute-done.6.refs_6_ = bf16[576,128]{1,0:T(8,128)(2,1)S(1)} collective-permute-done((bf16[576,128]{1,0:T(8,128)(2,1)S(1)}, bf16[576,128]{1,0:T(8,128)(2,1)S(1)}, u32[]{:S(2)}, u32[]{:S(2)}) %collective-permute-start.6) | collective-permute-done | bytes 147488 | tf_op jit(solution)/shard_map/ppermute | solution.py:319
  22.9 1.1 %collective-permute-done.4.refs_4_ = bf16[576,128]{1,0:T(8,128)(2,1)S(1)} collective-permute-done((bf16[576,128]{1,0:T(8,128)(2,1)S(1)}, bf16[576,128]{1,0:T(8,128)(2,1)S(1)}, u32[]{:S(2)}, u32[]{:S(2)}) %collective-permute-start.4) | collective-permute-done | bytes 147488 | tf_op jit(solution)/shard_map/ppermute | solution.py:319
  24.0 1.3 %collective-permute-done.2.refs_2_ = bf16[576,128]{1,0:T(8,128)(2,1)S(1)} collective-permute-done((bf16[576,128]{1,0:T(8,128)(2,1)S(1)}, bf16[576,128]{1,0:T(8,128)(2,1)S(1)}, u32[]{:S(2)}, u32[]{:S(2)}) %collective-permute-start.2) | collective-permute-done | bytes 147488 | tf_op jit(solution)/shard_map/ppermute | solution.py:319
  25.4 1.3 %collective-permute-done.3.refs_3_ = bf16[576,128]{1,0:T(8,128)(2,1)S(1)} collective-permute-done((bf16[576,128]{1,0:T(8,128)(2,1)S(1)}, bf16[576,128]{1,0:T(8,128)(2,1)S(1)}, u32[]{:S(2)}, u32[]{:S(2)}) %collective-permute-start.3) | collective-permute-done | bytes 147488 | tf_op jit(solution)/shard_map/ppermute | solution.py:319
  26.8 0.6 copy-done.9
  27.4 0.8 copy-done.1
  28.2 11.0 %attend.1 = (bf16[8,768,128]{2,1,0:T(8,128)(2,1)}, bf16[256,128]{1,0:T(8,128)(2,1)}, bf16[256,128]{1,0:T(8,128)(2,1)}, bf16[256,128]{1,0:T(8,128)(2,1)}, bf16[256,128]{1,0:T(8,128)(2,1)}) custom-call(s32[16]{0:T(128)} %order_ref.1, bf16[8,320,128]{2,1,0:T(8,128)(2,1)} %copy-done.1, bf16[576,128]{1,0:T(8,128)(2,1)} %copy-done.2, bf16[576,128]{1,0:T(8,128)(2,1)} %copy-done.6, ...), custom_call_target="tpu_custom_call" | custom-call | flops 8999999488 | bytes 12582912 | tf_op jit(solution)/shard_map/attend/pallas_call | solution.py:175
  39.2 4.6 %all-to-all-start.1 = ((bf16[8,768,128]{2,1,0:T(8,128)(2,1)}), bf16[8,768,128]{2,1,0:T(8,128)(2,1)S(1)}, u32[]{:S(2)}, u32[]{:S(2)}) async-start(bf16[8,768,128]{2,1,0:T(8,128)(2,1)} %get-tuple-element.16), calls=%async_computation.1 | async-start | bytes 3145728 | tf_op jit(solution)/shard_map/all_to_all | solution.py:333
  43.8 3.5 %collective-permute-start.8 = (bf16[256,128]{1,0:T(8,128)(2,1)S(1)}, bf16[256,128]{1,0:T(8,128)(2,1)S(1)}, u32[]{:S(2)}, u32[]{:S(2)}) collective-permute-start(bf16[256,128]{1,0:T(8,128)(2,1)S(1)} %copy-done.12), channel_id=1, source_target_pairs={{0,64},{64,0},{128,192},{192,128},{1,65},{65,1},{129,193},{193,129... | collective-permute-start | bytes 196616 | tf_op jit(solution)/shard_map/ppermute | solution.py:319
  47.3 5.4 %collective-permute-start.9 = (bf16[256,128]{1,0:T(8,128)(2,1)S(1)}, bf16[256,128]{1,0:T(8,128)(2,1)S(1)}, u32[]{:S(2)}, u32[]{:S(2)}) collective-permute-start(bf16[256,128]{1,0:T(8,128)(2,1)S(1)} %copy-done.11), channel_id=1, source_target_pairs={{0,128},{64,192},{128,0},{192,64},{1,129},{65,193},{129,1},{193,65... | collective-permute-start | bytes 196616 | tf_op jit(solution)/shard_map/ppermute | solution.py:319
  52.7 3.7 %collective-permute-done.9.c_ref = bf16[256,128]{1,0:T(8,128)(2,1)S(1)} collective-permute-done((bf16[256,128]{1,0:T(8,128)(2,1)S(1)}, bf16[256,128]{1,0:T(8,128)(2,1)S(1)}, u32[]{:S(2)}, u32[]{:S(2)}) %collective-permute-start.9) | collective-permute-done | bytes 65568 | tf_op jit(solution)/shard_map/ppermute | solution.py:319
  56.4 2.7 %collective-permute-done.10.d_ref = bf16[256,128]{1,0:T(8,128)(2,1)S(1)} collective-permute-done((bf16[256,128]{1,0:T(8,128)(2,1)S(1)}, bf16[256,128]{1,0:T(8,128)(2,1)S(1)}, u32[]{:S(2)}, u32[]{:S(2)}) %collective-permute-start.10) | collective-permute-done | bytes 65568 | tf_op jit(solution)/shard_map/ppermute | solution.py:319
  59.1 4.0 %collective-permute-start.13 = (bf16[256,128]{1,0:T(8,128)(2,1)S(1)}, bf16[256,128]{1,0:T(8,128)(2,1)S(1)}, u32[]{:S(2)}, u32[]{:S(2)}) collective-permute-start(bf16[256,128]{1,0:T(8,128)(2,1)S(1)} %sum4.1.a_ref), channel_id=1, source_target_pairs={{0,192},{64,128},{128,64},{192,0},{1,193},{65,129},{129,65},{193,1... | collective-permute-start | bytes 196616 | tf_op jit(solution)/shard_map/ppermute | solution.py:319
  63.1 2.2 %collective-permute-start.12 = (bf16[256,128]{1,0:T(8,128)(2,1)S(1)}, bf16[256,128]{1,0:T(8,128)(2,1)S(1)}, u32[]{:S(2)}, u32[]{:S(2)}) collective-permute-start(bf16[256,128]{1,0:T(8,128)(2,1)S(1)} %sum4.1.a_ref), channel_id=1, source_target_pairs={{0,128},{64,192},{128,0},{192,64},{1,129},{65,193},{129,1},{193,65... | collective-permute-start | bytes 196616 | tf_op jit(solution)/shard_map/ppermute | solution.py:319
  65.3 0.4 collective-permute-start.11
  65.7 8.0 %collective-permute-done.12.c_ref = bf16[256,128]{1,0:T(8,128)(2,1)S(1)} collective-permute-done((bf16[256,128]{1,0:T(8,128)(2,1)S(1)}, bf16[256,128]{1,0:T(8,128)(2,1)S(1)}, u32[]{:S(2)}, u32[]{:S(2)}) %collective-permute-start.12) | collective-permute-done | bytes 65568 | tf_op jit(solution)/shard_map/ppermute | solution.py:319
  73.7 3.0 %collective-permute-start.19 = (bf16[1024,128]{1,0:T(8,128)(2,1)S(1)}, bf16[1024,128]{1,0:T(8,128)(2,1)S(1)}, u32[]{:S(2)}, u32[]{:S(2)}) collective-permute-start(bf16[1024,128]{1,0:T(8,128)(2,1)S(1)} %join.1.refs_0_), channel_id=1, source_target_pairs={{0,48},{16,32},{32,16},{48,0},{1,49},{17,33},{33,17},{49,1},{2,50}... | collective-permute-start | bytes 786440 | tf_op jit(solution)/shard_map/ppermute | solution.py:319
  76.7 0.9 collective-permute-start.17
  77.9 0.9 sum_ctx.1
  78.8 5.1 %all-to-all-start.2 = ((bf16[8,16,640]{2,1,0:T(8,128)(2,1)}), bf16[8,16,640]{2,1,0:T(8,128)(2,1)S(1)}, u32[]{:S(2)}, u32[]{:S(2)}) async-start(bf16[8,16,640]{2,1,0:T(8,128)(2,1)} %sum_ctx.1), calls=%async_computation.2 | async-start | bytes 327680 | tf_op jit(solution)/shard_map/all_to_all | solution.py:335
  83.9 3.7 %collective-permute-done.19.refs_6_ = bf16[1024,128]{1,0:T(8,128)(2,1)S(1)} collective-permute-done((bf16[1024,128]{1,0:T(8,128)(2,1)S(1)}, bf16[1024,128]{1,0:T(8,128)(2,1)S(1)}, u32[]{:S(2)}, u32[]{:S(2)}) %collective-permute-start.19) | collective-permute-done | bytes 262176 | tf_op jit(solution)/shard_map/ppermute | solution.py:319
  87.7 0.5 collective-permute-start.18
  88.3 0.9 collective-permute-done.20.refs_7_
  89.9 2.5 %widen.1 = (f32[512,1024]{1,0:T(8,128)}, f32[512,1024]{1,0:T(8,128)}) custom-call(bf16[1024,128]{1,0:T(8,128)(2,1)S(1)} %join.1.refs_0_, bf16[1024,128]{1,0:T(8,128)(2,1)S(1)} %collective-permute-done.14.refs_1_, bf16[1024,128]{1,0:T(8,128)(2,1)S(1)} %collective-permute-done.15.refs_2_, bf16[1024,128]{1,0:T(8,128)(2,1)S(1)} %collective-permute-done.16.refs_3_, ...), custom_call_target="tpu_custom_call" | custom-call | tf_op jit(solution)/shard_map/widen/pallas_call | solution.py:304
  92.4 0.9 unpack.1
  93.3 0.6 sum_head.1
  (50 shorter events, 1.7 us)
Async XLA Ops:
  0.6 7.7 %collective-permute-start = (bf16[576,128]{1,0:T(8,128)(2,1)}, bf16[576,128]{1,0:T(8,128)(2,1)S(1)}, u32[]{:S(2)}, u32[]{:S(2)}) collective-permute-start(bf16[576,128]{1,0:T(8,128)(2,1)} %bitcast.3), channel_id=1, source_target_pairs={{0,0},{1,17},{2,34},{3,51},{16,16},{17,1},{18,50},{19,35},{32,32},... | collective-permute-start | bytes 442376 | tf_op jit(solution)/shard_map/ppermute | solution.py:325
  8.3 18.4 %copy-start.2 = (bf16[576,128]{1,0:T(8,128)(2,1)}, bf16[576,128]{1,0:T(8,128)(2,1)S(1)}, u32[]{:S(2)}) copy-start(bf16[576,128]{1,0:T(8,128)(2,1)S(1)} %collective-permute-done.refs_0_) | copy-start | bytes 442372
  8.3 18.4 %all-to-all-start = ((bf16[8,320,128]{2,1,0:T(8,128)(2,1)}), bf16[8,320,128]{2,1,0:T(8,128)(2,1)S(1)}, u32[]{:S(2)}, u32[]{:S(2)}) async-start(bf16[8,320,128]{2,1,0:T(8,128)(2,1)} %pack.1), calls=%async_computation | async-start | bytes 1310720 | tf_op jit(solution)/shard_map/all_to_all | solution.py:331
  12.8 10.1 %collective-permute-start.6 = (bf16[576,128]{1,0:T(8,128)(2,1)S(1)}, bf16[576,128]{1,0:T(8,128)(2,1)S(1)}, u32[]{:S(2)}, u32[]{:S(2)}) collective-permute-start(bf16[576,128]{1,0:T(8,128)(2,1)S(1)} %collective-permute-done.refs_0_), channel_id=1, source_target_pairs={{0,3},{1,2},{2,1},{3,0},{4,7},{5,6},{6,5},{7,4},{8,11},{9,10},{10,... | collective-permute-start | bytes 442376 | tf_op jit(solution)/shard_map/ppermute | solution.py:319
  15.8 8.2 %collective-permute-start.4 = (bf16[576,128]{1,0:T(8,128)(2,1)S(1)}, bf16[576,128]{1,0:T(8,128)(2,1)S(1)}, u32[]{:S(2)}, u32[]{:S(2)}) collective-permute-start(bf16[576,128]{1,0:T(8,128)(2,1)S(1)} %collective-permute-done.refs_0_), channel_id=1, source_target_pairs={{0,2},{1,3},{2,0},{3,1},{4,6},{5,7},{6,4},{7,5},{8,10},{9,11},{10,... | collective-permute-start | bytes 442376 | tf_op jit(solution)/shard_map/ppermute | solution.py:319
  16.0 9.3 %collective-permute-start.2 = (bf16[576,128]{1,0:T(8,128)(2,1)S(1)}, bf16[576,128]{1,0:T(8,128)(2,1)S(1)}, u32[]{:S(2)}, u32[]{:S(2)}) collective-permute-start(bf16[576,128]{1,0:T(8,128)(2,1)S(1)} %collective-permute-done.refs_0_), channel_id=1, source_target_pairs={{0,1},{1,0},{2,3},{3,2},{4,5},{5,4},{6,7},{7,6},{8,9},{9,8},{10,11... | collective-permute-start | bytes 442376 | tf_op jit(solution)/shard_map/ppermute | solution.py:319
  18.0 7.4 %collective-permute-start.1 = (bf16[576,128]{1,0:T(8,128)(2,1)S(1)}, bf16[576,128]{1,0:T(8,128)(2,1)S(1)}, u32[]{:S(2)}, u32[]{:S(2)}) collective-permute-start(bf16[576,128]{1,0:T(8,128)(2,1)S(1)} %collective-permute-done.refs_0_), channel_id=1, source_target_pairs={{0,8},{8,0},{1,9},{9,1},{2,10},{10,2},{3,11},{11,3},{4,12},{12,4},... | collective-permute-start | bytes 442376 | tf_op jit(solution)/shard_map/ppermute | solution.py:319
  22.9 3.8 %copy-start.3 = (bf16[576,128]{1,0:T(8,128)(2,1)}, bf16[576,128]{1,0:T(8,128)(2,1)S(1)}, u32[]{:S(2)}) copy-start(bf16[576,128]{1,0:T(8,128)(2,1)S(1)} %collective-permute-done.6.refs_6_) | copy-start | bytes 442372
  22.9 2.4 %collective-permute-start.7 = (bf16[576,128]{1,0:T(8,128)(2,1)S(1)}, bf16[576,128]{1,0:T(8,128)(2,1)S(1)}, u32[]{:S(2)}, u32[]{:S(2)}) collective-permute-start(bf16[576,128]{1,0:T(8,128)(2,1)S(1)} %collective-permute-done.6.refs_6_), channel_id=1, source_target_pairs={{0,8},{8,0},{1,9},{9,1},{2,10},{10,2},{3,11},{11,3},{4,12},{12,4},... | collective-permute-start | bytes 442376 | tf_op jit(solution)/shard_map/ppermute | solution.py:319
  24.0 2.7 %copy-start.4 = (bf16[576,128]{1,0:T(8,128)(2,1)}, bf16[576,128]{1,0:T(8,128)(2,1)S(1)}, u32[]{:S(2)}) copy-start(bf16[576,128]{1,0:T(8,128)(2,1)S(1)} %collective-permute-done.4.refs_4_) | copy-start | bytes 442372
  24.0 1.4 %collective-permute-start.5 = (bf16[576,128]{1,0:T(8,128)(2,1)S(1)}, bf16[576,128]{1,0:T(8,128)(2,1)S(1)}, u32[]{:S(2)}, u32[]{:S(2)}) collective-permute-start(bf16[576,128]{1,0:T(8,128)(2,1)S(1)} %collective-permute-done.4.refs_4_), channel_id=1, source_target_pairs={{0,8},{8,0},{1,9},{9,1},{2,10},{10,2},{3,11},{11,3},{4,12},{12,4},... | collective-permute-start | bytes 442376 | tf_op jit(solution)/shard_map/ppermute | solution.py:319
  25.3 1.4 %copy-start.5 = (bf16[576,128]{1,0:T(8,128)(2,1)}, bf16[576,128]{1,0:T(8,128)(2,1)S(1)}, u32[]{:S(2)}) copy-start(bf16[576,128]{1,0:T(8,128)(2,1)S(1)} %collective-permute-done.2.refs_2_) | copy-start | bytes 442372
  25.3 1.4 %collective-permute-start.3 = (bf16[576,128]{1,0:T(8,128)(2,1)S(1)}, bf16[576,128]{1,0:T(8,128)(2,1)S(1)}, u32[]{:S(2)}, u32[]{:S(2)}) collective-permute-start(bf16[576,128]{1,0:T(8,128)(2,1)S(1)} %collective-permute-done.2.refs_2_), channel_id=1, source_target_pairs={{0,8},{8,0},{1,9},{9,1},{2,10},{10,2},{3,11},{11,3},{4,12},{12,4},... | collective-permute-start | bytes 442376 | tf_op jit(solution)/shard_map/ppermute | solution.py:319
  39.2 4.6 %copy-start.12 = (bf16[256,128]{1,0:T(8,128)(2,1)S(1)}, bf16[256,128]{1,0:T(8,128)(2,1)}, u32[]{:S(2)}) copy-start(bf16[256,128]{1,0:T(8,128)(2,1)} %get-tuple-element.20) | copy-start | bytes 196612
  39.2 8.2 %copy-start.11 = (bf16[256,128]{1,0:T(8,128)(2,1)S(1)}, bf16[256,128]{1,0:T(8,128)(2,1)}, u32[]{:S(2)}) copy-start(bf16[256,128]{1,0:T(8,128)(2,1)} %get-tuple-element.21) | copy-start | bytes 196612
  39.2 13.5 %copy-start.10 = (bf16[256,128]{1,0:T(8,128)(2,1)S(1)}, bf16[256,128]{1,0:T(8,128)(2,1)}, u32[]{:S(2)}) copy-start(bf16[256,128]{1,0:T(8,128)(2,1)} %get-tuple-element.22) | copy-start | bytes 196612
  39.2 19.9 %copy-start = (bf16[256,128]{1,0:T(8,128)(2,1)S(1)}, bf16[256,128]{1,0:T(8,128)(2,1)}, u32[]{:S(2)}) copy-start(bf16[256,128]{1,0:T(8,128)(2,1)} %get-tuple-element.19.a_ref) | copy-start | bytes 196612
  39.2 38.7 %all-to-all-start.1 = ((bf16[8,768,128]{2,1,0:T(8,128)(2,1)}), bf16[8,768,128]{2,1,0:T(8,128)(2,1)S(1)}, u32[]{:S(2)}, u32[]{:S(2)}) async-start(bf16[8,768,128]{2,1,0:T(8,128)(2,1)} %get-tuple-element.16), calls=%async_computation.1 | async-start | bytes 3145728 | tf_op jit(solution)/shard_map/all_to_all | solution.py:333
  43.8 8.9 %collective-permute-start.8 = (bf16[256,128]{1,0:T(8,128)(2,1)S(1)}, bf16[256,128]{1,0:T(8,128)(2,1)S(1)}, u32[]{:S(2)}, u32[]{:S(2)}) collective-permute-start(bf16[256,128]{1,0:T(8,128)(2,1)S(1)} %copy-done.12), channel_id=1, source_target_pairs={{0,64},{64,0},{128,192},{192,128},{1,65},{65,1},{129,193},{193,129... | collective-permute-start | bytes 196616 | tf_op jit(solution)/shard_map/ppermute | solution.py:319
  47.3 9.1 %collective-permute-start.9 = (bf16[256,128]{1,0:T(8,128)(2,1)S(1)}, bf16[256,128]{1,0:T(8,128)(2,1)S(1)}, u32[]{:S(2)}, u32[]{:S(2)}) collective-permute-start(bf16[256,128]{1,0:T(8,128)(2,1)S(1)} %copy-done.11), channel_id=1, source_target_pairs={{0,128},{64,192},{128,0},{192,64},{1,129},{65,193},{129,1},{193,65... | collective-permute-start | bytes 196616 | tf_op jit(solution)/shard_map/ppermute | solution.py:319
  52.7 6.4 %collective-permute-start.10 = (bf16[256,128]{1,0:T(8,128)(2,1)S(1)}, bf16[256,128]{1,0:T(8,128)(2,1)S(1)}, u32[]{:S(2)}, u32[]{:S(2)}) collective-permute-start(bf16[256,128]{1,0:T(8,128)(2,1)S(1)} %copy-done.10), channel_id=1, source_target_pairs={{0,192},{64,128},{128,64},{192,0},{1,193},{65,129},{129,65},{193,1... | collective-permute-start | bytes 196616 | tf_op jit(solution)/shard_map/ppermute | solution.py:319
  59.1 6.6 %collective-permute-start.13 = (bf16[256,128]{1,0:T(8,128)(2,1)S(1)}, bf16[256,128]{1,0:T(8,128)(2,1)S(1)}, u32[]{:S(2)}, u32[]{:S(2)}) collective-permute-start(bf16[256,128]{1,0:T(8,128)(2,1)S(1)} %sum4.1.a_ref), channel_id=1, source_target_pairs={{0,192},{64,128},{128,64},{192,0},{1,193},{65,129},{129,65},{193,1... | collective-permute-start | bytes 196616 | tf_op jit(solution)/shard_map/ppermute | solution.py:319
  63.1 10.6 %collective-permute-start.12 = (bf16[256,128]{1,0:T(8,128)(2,1)S(1)}, bf16[256,128]{1,0:T(8,128)(2,1)S(1)}, u32[]{:S(2)}, u32[]{:S(2)}) collective-permute-start(bf16[256,128]{1,0:T(8,128)(2,1)S(1)} %sum4.1.a_ref), channel_id=1, source_target_pairs={{0,128},{64,192},{128,0},{192,64},{1,129},{65,193},{129,1},{193,65... | collective-permute-start | bytes 196616 | tf_op jit(solution)/shard_map/ppermute | solution.py:319
  65.3 8.4 %collective-permute-start.11 = (bf16[256,128]{1,0:T(8,128)(2,1)S(1)}, bf16[256,128]{1,0:T(8,128)(2,1)S(1)}, u32[]{:S(2)}, u32[]{:S(2)}) collective-permute-start(bf16[256,128]{1,0:T(8,128)(2,1)S(1)} %sum4.1.a_ref), channel_id=1, source_target_pairs={{0,64},{64,0},{128,192},{192,128},{1,65},{65,1},{129,193},{193,129... | collective-permute-start | bytes 196616 | tf_op jit(solution)/shard_map/ppermute | solution.py:319
  73.7 13.9 %collective-permute-start.19 = (bf16[1024,128]{1,0:T(8,128)(2,1)S(1)}, bf16[1024,128]{1,0:T(8,128)(2,1)S(1)}, u32[]{:S(2)}, u32[]{:S(2)}) collective-permute-start(bf16[1024,128]{1,0:T(8,128)(2,1)S(1)} %join.1.refs_0_), channel_id=1, source_target_pairs={{0,48},{16,32},{32,16},{48,0},{1,49},{17,33},{33,17},{49,1},{2,50}... | collective-permute-start | bytes 786440 | tf_op jit(solution)/shard_map/ppermute | solution.py:319
  76.7 11.0 %collective-permute-start.17 = (bf16[1024,128]{1,0:T(8,128)(2,1)S(1)}, bf16[1024,128]{1,0:T(8,128)(2,1)S(1)}, u32[]{:S(2)}, u32[]{:S(2)}) collective-permute-start(bf16[1024,128]{1,0:T(8,128)(2,1)S(1)} %join.1.refs_0_), channel_id=1, source_target_pairs={{0,32},{16,48},{32,0},{48,16},{1,33},{17,49},{33,1},{49,17},{2,34}... | collective-permute-start | bytes 786440 | tf_op jit(solution)/shard_map/ppermute | solution.py:319
  77.5 10.7 %collective-permute-start.15 = (bf16[1024,128]{1,0:T(8,128)(2,1)S(1)}, bf16[1024,128]{1,0:T(8,128)(2,1)S(1)}, u32[]{:S(2)}, u32[]{:S(2)}) collective-permute-start(bf16[1024,128]{1,0:T(8,128)(2,1)S(1)} %join.1.refs_0_), channel_id=1, source_target_pairs={{0,16},{16,0},{32,48},{48,32},{1,17},{17,1},{33,49},{49,33},{2,18}... | collective-permute-start | bytes 786440 | tf_op jit(solution)/shard_map/ppermute | solution.py:319
  78.8 14.4 %all-to-all-start.2 = ((bf16[8,16,640]{2,1,0:T(8,128)(2,1)}), bf16[8,16,640]{2,1,0:T(8,128)(2,1)S(1)}, u32[]{:S(2)}, u32[]{:S(2)}) async-start(bf16[8,16,640]{2,1,0:T(8,128)(2,1)} %sum_ctx.1), calls=%async_computation.2 | async-start | bytes 327680 | tf_op jit(solution)/shard_map/all_to_all | solution.py:335
  83.9 4.4 %collective-permute-start.14 = (bf16[1024,128]{1,0:T(8,128)(2,1)S(1)}, bf16[1024,128]{1,0:T(8,128)(2,1)S(1)}, u32[]{:S(2)}, u32[]{:S(2)}) collective-permute-start(bf16[1024,128]{1,0:T(8,128)(2,1)S(1)} %join.1.refs_0_), channel_id=1, source_target_pairs={{0,8},{8,0},{1,9},{9,1},{2,10},{10,2},{3,11},{11,3},{4,12},{12,4},... | collective-permute-start | bytes 786440 | tf_op jit(solution)/shard_map/ppermute | solution.py:319
  87.7 1.5 %collective-permute-start.20 = (bf16[1024,128]{1,0:T(8,128)(2,1)S(1)}, bf16[1024,128]{1,0:T(8,128)(2,1)S(1)}, u32[]{:S(2)}, u32[]{:S(2)}) collective-permute-start(bf16[1024,128]{1,0:T(8,128)(2,1)S(1)} %collective-permute-done.19.refs_6_), channel_id=1, source_target_pairs={{0,8},{8,0},{1,9},{9,1},{2,10},{10,2},{3,11},{11,3},{4,12},{12,4},... | collective-permute-start | bytes 786440 | tf_op jit(solution)/shard_map/ppermute | solution.py:319
  87.7 1.9 %collective-permute-start.18 = (bf16[1024,128]{1,0:T(8,128)(2,1)S(1)}, bf16[1024,128]{1,0:T(8,128)(2,1)S(1)}, u32[]{:S(2)}, u32[]{:S(2)}) collective-permute-start(bf16[1024,128]{1,0:T(8,128)(2,1)S(1)} %collective-permute-done.17.refs_4_), channel_id=1, source_target_pairs={{0,8},{8,0},{1,9},{9,1},{2,10},{10,2},{3,11},{11,3},{4,12},{12,4},... | collective-permute-start | bytes 786440 | tf_op jit(solution)/shard_map/ppermute | solution.py:319
  88.3 1.6 %collective-permute-start.16 = (bf16[1024,128]{1,0:T(8,128)(2,1)S(1)}, bf16[1024,128]{1,0:T(8,128)(2,1)S(1)}, u32[]{:S(2)}, u32[]{:S(2)}) collective-permute-start(bf16[1024,128]{1,0:T(8,128)(2,1)S(1)} %collective-permute-done.15.refs_2_), channel_id=1, source_target_pairs={{0,8},{8,0},{1,9},{9,1},{2,10},{10,2},{3,11},{11,3},{4,12},{12,4},... | collective-permute-start | bytes 786440 | tf_op jit(solution)/shard_map/ppermute | solution.py:319
  (5 other events, 5.7 us)

commit v3 on v2

--- a/solution.py
+++ b/solution.py
@@ -48,26 +48,26 @@
     )(q_nope, q_rope, d_out, after)
 
 
-def attend_kernel(order_ref, x_hbm, *refs):
+def attend_kernel(order_ref, x_in, *refs):
     kv_hbm = refs[:8]
     uk_hbm, uv_hbm, seg_ref = refs[8:11]
     back_ref = refs[11]
-    dw_refs = refs[12:16]
-    x_in, kv_in, uk_in, uv_in, keys, keyt, qfull, qn, g, dob, pt, dst, ot, dqt, dqr, dqs, dkv, dw, sems = refs[16:]
+    duk_ref, duv_ref = refs[12:14]
+    kv_in, uk_in, uv_in, keys, keyt, qfull, qn, g, dob, pt, dst, ot, dqt, dqr, dqs, dkr, inverse, sems = refs[14:]
     y = lax.axis_index("y")
     core = lax.axis_index("core")
     me = y * 2 + core
     block = y ^ lax.axis_index("x")
     cols = pl.ds(pl.multiple_of(me * 128, 128), 128)
 
-    load_x = pltpu.make_async_copy(x_hbm, x_in, sems.at[8])
     load_uk = pltpu.make_async_copy(uk_hbm.at[:, cols], uk_in, sems.at[9])
     load_uv = pltpu.make_async_copy(uv_hbm.at[:, cols], uv_in, sems.at[10])
     loads = [pltpu.make_async_copy(kv_hbm[i], kv_in.at[i], sems.at[i]) for i in range(8)]
-    for load in [load_x, load_uk, load_uv] + loads:
+    for slot in range(16):
+        inverse[order_ref[slot]] = slot
+    for load in [load_uk, load_uv] + loads:
         load.start()
 
-    load_x.wait()
     for slot in range(16):
         c, e = slot // 2, slot % 2
         row = pl.ds(pl.multiple_of(order_ref[slot] * SPAN, SPAN), SPAN)
@@ -134,19 +134,18 @@
         softmax(b, *flight)
         outputs(b)
         flight = following
-    dw[0:512, :] = dot(dqt[...], qn[...], NN).astype(BF16)
-    dw[512:1024, :] = dot(ot[...], g[...], NN).astype(BF16)
-    dp = lax.axis_index("dp")
-    for d in range(4):
-        dw_refs[d][...] = dw[pl.ds(pl.multiple_of((dp ^ d) * 256, 256), 256), :]
-    dqs[:, 0:128] = dot(dqt[...], uk, TN).astype(BF16)
-    dqs[:, 128:192] = jnp.transpose(dqr[...], (1, 0))
-    for slot in range(16):
-        c, e = slot // 2, slot % 2
-        row = pl.ds(pl.multiple_of(order_ref[slot] * SPAN, SPAN), SPAN)
-        back_ref[c, 576 + e * 64:576 + (e + 1) * 64, :] = dqs[row, 0:128]
-        back_ref[c, 704:768, e * 64:(e + 1) * 64] = dqs[row, 128:192]
-
+    duk_ref[...] = dot(dqt[...], qn[...], NN).astype(BF16)
+    duv_ref[...] = dot(ot[...], g[...], NN).astype(BF16)
+    dqn = dot(dqt[...], uk, TN).astype(BF16)
+    dqs[...] = jnp.transpose(dqr[...], (1, 0))
+
+    def home(span):
+        slot = inverse[span]
+        return slot // 2, slot % 2
+
+    for span in range(16):
+        c, e = home(span)
+        back_ref[c, pl.ds(pl.multiple_of(576 + e * 64, 64), 64), :] = dqn[span * 64:(span + 1) * 64, :]
     for kb in range(4):
         last = min(kb + 3, 4)
         ds = []
@@ -158,26 +157,29 @@
         ds = jnp.concatenate(ds, axis=1)
         pb = jnp.concatenate(pb, axis=1)
         lo, hi = kb * 256, last * 256
-        dkv[lo:lo + 256, 0:LAT] = (dot(ds, qfull[lo:hi, 0:LAT], NN) + dot(pb, dob[lo:hi, :], NN)).astype(BF16)
-        dkv[lo:lo + 256, LAT:] = dot(ds, qfull[lo:hi, LAT:], NN).astype(BF16)
+        part = (dot(ds, qfull[lo:hi, 0:LAT], NN) + dot(pb, dob[lo:hi, :], NN)).astype(BF16)
+        dkr[lo:lo + 256, :] = dot(ds, qfull[lo:hi, LAT:], NN).astype(BF16)
+        for t in range(4):
+            c, e = home(kb * 4 + t)
+            for j in range(4):
+                row = pl.ds(pl.multiple_of(j * 128 + e * 64, 64), 64)
+                back_ref[c, row, :] = part[t * 64:(t + 1) * 64, j * 128:(j + 1) * 128]
     for slot in range(16):
         c, e = slot // 2, slot % 2
         row = pl.ds(pl.multiple_of(order_ref[slot] * SPAN, SPAN), SPAN)
-        for j in range(4):
-            back_ref[c, j * 128 + e * 64:j * 128 + (e + 1) * 64, :] = dkv[row, j * 128:(j + 1) * 128]
-        back_ref[c, 512:576, e * 64:(e + 1) * 64] = dkv[row, LAT:LAT + ROPE]
+        back_ref[c, 704:768, e * 64:(e + 1) * 64] = dqs[row, :]
+        back_ref[c, 512:576, e * 64:(e + 1) * 64] = dkr[row, :]
 
 
 def attend(order, x, kvs, w_uk, w_uv, seg):
     hbm = pl.BlockSpec(memory_space=pl.ANY)
     vmem = pl.BlockSpec(memory_space=pltpu.VMEM)
-    outs = [(8, 768, 128)] + [(256, 128)] * 4
+    outs = [(8, 768, 128), (512, 128), (512, 128)]
     return pl.pallas_call(
         attend_kernel,
-        in_specs=[pl.BlockSpec(memory_space=pltpu.SMEM)] + [hbm] * 11 + [vmem],
-        out_specs=[vmem] * 5,
+        in_specs=[pl.BlockSpec(memory_space=pltpu.SMEM), vmem] + [hbm] * 10 + [vmem],
+        out_specs=[vmem] * 3,
         scratch_shapes=[
-            pltpu.VMEM((8, 320, 128), BF16),
             pltpu.VMEM((8, 576, 128), BF16),
             pltpu.VMEM((LAT, 128), BF16),
             pltpu.VMEM((LAT, 128), BF16),
@@ -192,13 +194,13 @@
             pltpu.VMEM((LAT, SEQ), BF16),
             pltpu.VMEM((LAT, SEQ), BF16),
             pltpu.VMEM((64, SEQ), BF16),
-            pltpu.VMEM((SEQ, 192), BF16),
-            pltpu.VMEM((SEQ, 576), BF16),
-            pltpu.VMEM((1024, 128), BF16),
+            pltpu.VMEM((SEQ, ROPE), BF16),
+            pltpu.VMEM((SEQ, ROPE), BF16),
+            pltpu.SMEM((16,), jnp.int32),
             pltpu.SemaphoreType.DMA((11,)),
         ],
         out_shape=[jax.ShapeDtypeStruct(shape, BF16) for shape in outs],
-        compiler_params=pltpu.CompilerParams(vmem_limit_bytes=60 * MIB),
+        compiler_params=pltpu.CompilerParams(vmem_limit_bytes=36 * MIB),
         cost_estimate=pl.CostEstimate(flops=9_000_000_000, bytes_accessed=12 * MIB, transcendentals=600_000),
         name="attend",
     )(order, x, *kvs, w_uk, w_uv, seg)
@@ -214,9 +216,17 @@
     )(*args)
 
 
-def sum4_kernel(a_ref, b_ref, c_ref, d_ref, out_ref):
-    total = (a_ref[...].astype(F32) + b_ref[...].astype(F32)) + (c_ref[...].astype(F32) + d_ref[...].astype(F32))
-    out_ref[...] = total.astype(BF16)
+def add1_kernel(a_ref, b_ref, out_ref):
+    out_ref[...] = (a_ref[...].astype(F32) + b_ref[...].astype(F32)).astype(BF16)
+
+
+def add2_kernel(a_ref, b_ref, c_ref, d_ref, uk_ref, uv_ref):
+    uk_ref[...] = (a_ref[...].astype(F32) + b_ref[...].astype(F32)).astype(BF16)
+    uv_ref[...] = (c_ref[...].astype(F32) + d_ref[...].astype(F32)).astype(BF16)
+
+
+def add_join_kernel(a_ref, b_ref, c_ref, d_ref, out_ref):
+    add2_kernel(a_ref, b_ref, c_ref, d_ref, out_ref.at[0:512, :], out_ref.at[512:1024, :])
 
 
 def sum_ctx_kernel(x_ref, out_ref):
@@ -250,12 +260,6 @@
     for i in range(1, 8):
         total = total + x_ref[i].astype(F32)
     out_ref[0] = total[:, 0:576].astype(BF16)
-
-
-def join_kernel(a_ref, b_ref, c_ref, d_ref, out_ref):
-    dp = lax.axis_index("dp")
-    for d, ref in enumerate((a_ref, b_ref, c_ref, d_ref)):
-        out_ref[pl.ds(pl.multiple_of((dp ^ d) * 256, 256), 256), :] = ref[...]
 
 
 def unpack_kernel(x_ref, qn_ref, qr_ref):
@@ -329,18 +333,20 @@
     send = pack(q_nope, q_rope, d_out, kvt)
     send, first = lax.optimization_barrier((send, first))
     x = lax.all_to_all(send, ("y", "core"), 0, 0, tiled=True)
-    back, dw0, dw1, dw2, dw3 = attend(span_order, x, kvs, w_uk, w_uv, segment_ids)
+    back, duk, duv = attend(span_order, x, kvs, w_uk, w_uv, segment_ids)
     back = lax.all_to_all(back, ("y", "core"), 0, 0, tiled=True)
     dq_nope, dq_rope = unpack(back)
     parts = lax.all_to_all(sum_ctx(back), ("zl", "x"), 0, 0, tiled=True)
     d_kv = call(sum_head_kernel, "sum_head", jax.ShapeDtypeStruct((1, 16, 576), BF16), parts)
-    chunk = jax.ShapeDtypeStruct((256, 128), BF16)
-    total = call(sum4_kernel, "sum4", chunk, dw0, across(dw1, "dp", 1), across(dw2, "dp", 2), across(dw3, "dp", 3))
-    gathered = [across(total, "dp", d) for d in (1, 2, 3)]
-    whole = call(join_kernel, "join", jax.ShapeDtypeStruct((1024, 128), BF16), total, *gathered)
+    pair = [jax.ShapeDtypeStruct((512, 128), BF16)] * 2
+    duk = call(add1_kernel, "add_uk", pair[0], duk, across(duk, "dp", 1))
+    duv = call(add1_kernel, "add_uv", pair[0], duv, across(duv, "dp", 3))
+    whole = jax.ShapeDtypeStruct((1024, 128), BF16)
+    whole = call(add_join_kernel, "add_join", whole, duk, across(duk, "dp", 3), duv, across(duv, "dp", 1))
     pieces = []
     for piece in [whole] + [across(whole, "y", d) for d in (1, 2, 3)]:
         pieces += [piece, across(piece, "core", 1)]
+    pieces[-1], dq_nope, dq_rope = lax.optimization_barrier((pieces[-1], dq_nope, dq_rope))
     dw_uk, dw_uv = widen(pieces)
     return dq_nope, dq_rope, d_kv, dw_uk, dw_uv
 

time: 95.6 us -> 88.7 us (0.928)
  waiting for transfers between devices: 30.7 us -> 21.9 us
  starting transfers between devices: 43 us -> 45 us
    ppermute x20 -> x18, waiting for transfers between devices: 28.5 us -> 19.8 us  [across(): return lax.ppermute(x, axis, [(i, i ^ step) for i in range(SIZES[axis])])]
    all_to_all x1, starting transfers between devices: 5.08 us -> 7.2 us  [local(): parts = lax.all_to_all(sum_ctx(back), ('zl', 'x'), 0, 0, tiled=True)]
    ppermute x20 -> x18, starting transfers between devices: 25.4 us -> 25.3 us  [across(): return lax.ppermute(x, axis, [(i, i ^ step) for i in range(SIZES[axis])])]
  transfers between devices with their start and end apart: 24 -> 22, of which waited for: 13 -> 13; matrix products, arithmetic and copies ran while one was open for 0% -> 0% of each run, Pallas kernels for 7% -> 7%
where the time goes in v3:
time: 88.7 us; the launch traced here: 87.1 us
  starting transfers between devices  45 us (51%)
  waiting for transfers between devices  21.9 us (25%)
  Pallas kernels  18.3 us (21%)
  local copies, waits for them, and re-layouts  1.23 us (1%)
    ppermute x18, starting transfers between devices, across(): return lax.ppermute(x, axis, [(i, i ^ step) for i in range(SIZES[axis])])  25.3 us
    ppermute x18, waiting for transfers between devices, across(): return lax.ppermute(x, axis, [(i, i ^ step) for i in range(SIZES[axis])])  19.8 us
    pallas_call x1, Pallas kernels, attend(): pl.pallas_call(attend_kernel, in_specs=[pl.BlockSpec(memory_space=pltpu.S...  11.2 us
    all_to_all x1, starting transfers between devices, local(): parts = lax.all_to_all(sum_ctx(back), ('zl', 'x'), 0, 0, tiled=True)  7.2 us
    all_to_all x1, starting transfers between devices, local(): x = lax.all_to_all(send, ('y', 'core'), 0, 0, tiled=True)  4.47 us
    all_to_all x1, starting transfers between devices, local(): back = lax.all_to_all(back, ('y', 'core'), 0, 0, tiled=True)  4.44 us
    ppermute x1, starting transfers between devices, local(): first = lax.ppermute(kvt, ('y', 'x'), skew)  3.62 us
    pallas_call x1, Pallas kernels, widen(): pl.pallas_call(widen_kernel, grid=(4,), in_specs=[piece] * 8, out_specs=[...  2.46 us
  transfers between devices with their start and end apart: 22, of which 13 were waited for; matrix products, arithmetic and copies ran while one was open for 0% of the time, Pallas kernels for 7%

profile of v3, /device:TPU:2, one launch (start us, length us, event | category | flops | bytes accessed | tf_op | source)
XLA Modules:
  0.0 87.1 jit_solution(3518325833447738490)
XLA Ops:
  0.7 3.6 %collective-permute-start = (bf16[576,128]{1,0:T(8,128)(2,1)}, bf16[576,128]{1,0:T(8,128)(2,1)S(1)}, u32[]{:S(2)}, u32[]{:S(2)}) collective-permute-start(bf16[576,128]{1,0:T(8,128)(2,1)} %bitcast.3), channel_id=1, source_target_pairs={{0,0},{1,17},{2,34},{3,51},{16,16},{17,1},{18,50},{19,35},{32,32},... | collective-permute-start | bytes 442376 | tf_op jit(solution)/shard_map/ppermute | solution.py:329
  4.3 2.1 %pack.1 = bf16[8,320,128]{2,1,0:T(8,128)(2,1)} custom-call(bf16[1,128,1024]{2,1,0:T(8,128)(2,1)} %qn_ref.1, bf16[1,128,512]{2,1,0:T(8,128)(2,1)} %qr_ref.1, bf16[1,128,1024]{2,1,0:T(8,128)(2,1)} %do_ref.1, bf16[576,128]{1,0:T(8,128)(2,1)} %bitcast.4), custom_call_target="tpu_custom_call" | custom-call | bytes 5242880 | tf_op jit(solution)/shard_map/pack/pallas_call | solution.py:40
  6.4 2.1 %collective-permute-done.refs_0_ = bf16[576,128]{1,0:T(8,128)(2,1)S(1)} collective-permute-done((bf16[576,128]{1,0:T(8,128)(2,1)}, bf16[576,128]{1,0:T(8,128)(2,1)S(1)}, u32[]{:S(2)}, u32[]{:S(2)}) %collective-permute-start) | collective-permute-done | bytes 147488 | tf_op jit(solution)/shard_map/ppermute | solution.py:329
  8.5 4.5 %all-to-all-start = ((bf16[8,320,128]{2,1,0:T(8,128)(2,1)}), bf16[8,320,128]{2,1,0:T(8,128)(2,1)S(1)}, u32[]{:S(2)}, u32[]{:S(2)}) async-start(bf16[8,320,128]{2,1,0:T(8,128)(2,1)} %pack.1), calls=%async_computation | async-start | bytes 1310720 | tf_op jit(solution)/shard_map/all_to_all | solution.py:335
  13.0 3.0 %collective-permute-start.6 = (bf16[576,128]{1,0:T(8,128)(2,1)S(1)}, bf16[576,128]{1,0:T(8,128)(2,1)S(1)}, u32[]{:S(2)}, u32[]{:S(2)}) collective-permute-start(bf16[576,128]{1,0:T(8,128)(2,1)S(1)} %collective-permute-done.refs_0_), channel_id=1, source_target_pairs={{0,3},{1,2},{2,1},{3,0},{4,7},{5,6},{6,5},{7,4},{8,11},{9,10},{10,... | collective-permute-start | bytes 442376 | tf_op jit(solution)/shard_map/ppermute | solution.py:323
  16.2 1.9 %collective-permute-start.2 = (bf16[576,128]{1,0:T(8,128)(2,1)S(1)}, bf16[576,128]{1,0:T(8,128)(2,1)S(1)}, u32[]{:S(2)}, u32[]{:S(2)}) collective-permute-start(bf16[576,128]{1,0:T(8,128)(2,1)S(1)} %collective-permute-done.refs_0_), channel_id=1, source_target_pairs={{0,1},{1,0},{2,3},{3,2},{4,5},{5,4},{6,7},{7,6},{8,9},{9,8},{10,11... | collective-permute-start | bytes 442376 | tf_op jit(solution)/shard_map/ppermute | solution.py:323
  18.1 4.9 %collective-permute-done.6.refs_6_ = bf16[576,128]{1,0:T(8,128)(2,1)S(1)} collective-permute-done((bf16[576,128]{1,0:T(8,128)(2,1)S(1)}, bf16[576,128]{1,0:T(8,128)(2,1)S(1)}, u32[]{:S(2)}, u32[]{:S(2)}) %collective-permute-start.6) | collective-permute-done | bytes 147488 | tf_op jit(solution)/shard_map/ppermute | solution.py:323
  23.1 1.1 %collective-permute-done.4.refs_4_ = bf16[576,128]{1,0:T(8,128)(2,1)S(1)} collective-permute-done((bf16[576,128]{1,0:T(8,128)(2,1)S(1)}, bf16[576,128]{1,0:T(8,128)(2,1)S(1)}, u32[]{:S(2)}, u32[]{:S(2)}) %collective-permute-start.4) | collective-permute-done | bytes 147488 | tf_op jit(solution)/shard_map/ppermute | solution.py:323
  24.2 1.3 %collective-permute-done.2.refs_2_ = bf16[576,128]{1,0:T(8,128)(2,1)S(1)} collective-permute-done((bf16[576,128]{1,0:T(8,128)(2,1)S(1)}, bf16[576,128]{1,0:T(8,128)(2,1)S(1)}, u32[]{:S(2)}, u32[]{:S(2)}) %collective-permute-start.2) | collective-permute-done | bytes 147488 | tf_op jit(solution)/shard_map/ppermute | solution.py:323
  25.6 1.3 %collective-permute-done.3.refs_3_ = bf16[576,128]{1,0:T(8,128)(2,1)S(1)} collective-permute-done((bf16[576,128]{1,0:T(8,128)(2,1)S(1)}, bf16[576,128]{1,0:T(8,128)(2,1)S(1)}, u32[]{:S(2)}, u32[]{:S(2)}) %collective-permute-start.3) | collective-permute-done | bytes 147488 | tf_op jit(solution)/shard_map/ppermute | solution.py:323
  26.9 1.2 %copy-done.1 = bf16[512,1024]{1,0:T(8,128)(2,1)S(1)} copy-done((bf16[512,1024]{1,0:T(8,128)(2,1)S(1)}, bf16[512,1024]{1,0:T(8,128)(2,1)}, u32[]{:S(2)}) %copy-start.1) | copy-done | bytes 1048600
  28.1 11.2 %attend.1 = (bf16[8,768,128]{2,1,0:T(8,128)(2,1)}, bf16[512,128]{1,0:T(8,128)(2,1)S(1)}, bf16[512,128]{1,0:T(8,128)(2,1)S(1)}) custom-call(s32[16]{0:T(128)S(1)} %copy-done.3, bf16[8,320,128]{2,1,0:T(8,128)(2,1)S(1)} %all-to-all-done.x_in, bf16[576,128]{1,0:T(8,128)(2,1)S(1)} %collective-permute-done.refs_0_, ...), custom_call_target="tpu_custom_call" | custom-call | flops 8999999488 | bytes 12582912 | tf_op jit(solution)/shard_map/attend/pallas_call | solution.py:178
  39.3 4.4 %all-to-all-start.1 = ((bf16[8,768,128]{2,1,0:T(8,128)(2,1)}), bf16[8,768,128]{2,1,0:T(8,128)(2,1)S(1)}, u32[]{:S(2)}, u32[]{:S(2)}) async-start(bf16[8,768,128]{2,1,0:T(8,128)(2,1)} %get-tuple-element.19), calls=%async_computation.1 | async-start | bytes 3145728 | tf_op jit(solution)/shard_map/all_to_all | solution.py:337
  43.7 3.3 %collective-permute-start.8 = (bf16[512,128]{1,0:T(8,128)(2,1)S(1)}, bf16[512,128]{1,0:T(8,128)(2,1)S(1)}, u32[]{:S(2)}, u32[]{:S(2)}) collective-permute-start(bf16[512,128]{1,0:T(8,128)(2,1)S(1)} %get-tuple-element.17.a_ref), channel_id=1, source_target_pairs={{0,64},{64,0},{128,192},{192,128},{1,65},{65,1},{129,193},{193,129... | collective-permute-start | bytes 393224 | tf_op jit(solution)/shard_map/ppermute | solution.py:323
  47.0 4.5 %collective-permute-start.10 = (bf16[512,128]{1,0:T(8,128)(2,1)S(1)}, bf16[512,128]{1,0:T(8,128)(2,1)S(1)}, u32[]{:S(2)}, u32[]{:S(2)}) collective-permute-start(bf16[512,128]{1,0:T(8,128)(2,1)S(1)} %get-tuple-element.18.a_ref), channel_id=1, source_target_pairs={{0,192},{64,128},{128,64},{192,0},{1,193},{65,129},{129,65},{193,1... | collective-permute-start | bytes 393224 | tf_op jit(solution)/shard_map/ppermute | solution.py:323
  51.5 2.6 %collective-permute-done.8.b_ref = bf16[512,128]{1,0:T(8,128)(2,1)S(1)} collective-permute-done((bf16[512,128]{1,0:T(8,128)(2,1)S(1)}, bf16[512,128]{1,0:T(8,128)(2,1)S(1)}, u32[]{:S(2)}, u32[]{:S(2)}) %collective-permute-start.8) | collective-permute-done | bytes 131104 | tf_op jit(solution)/shard_map/ppermute | solution.py:323
  54.1 3.8 %collective-permute-start.9 = (bf16[512,128]{1,0:T(8,128)(2,1)S(1)}, bf16[512,128]{1,0:T(8,128)(2,1)S(1)}, u32[]{:S(2)}, u32[]{:S(2)}) collective-permute-start(bf16[512,128]{1,0:T(8,128)(2,1)S(1)} %add_uk.1.a_ref), channel_id=1, source_target_pairs={{0,192},{64,128},{128,64},{192,0},{1,193},{65,129},{129,65},{193,1... | collective-permute-start | bytes 393224 | tf_op jit(solution)/shard_map/ppermute | solution.py:323
  57.9 3.5 %collective-permute-start.11 = (bf16[512,128]{1,0:T(8,128)(2,1)S(1)}, bf16[512,128]{1,0:T(8,128)(2,1)S(1)}, u32[]{:S(2)}, u32[]{:S(2)}) collective-permute-start(bf16[512,128]{1,0:T(8,128)(2,1)S(1)} %add_uv.1.c_ref), channel_id=1, source_target_pairs={{0,64},{64,0},{128,192},{192,128},{1,65},{65,1},{129,193},{193,129... | collective-permute-start | bytes 393224 | tf_op jit(solution)/shard_map/ppermute | solution.py:323
  61.6 4.5 %collective-permute-done.11.d_ref = bf16[512,128]{1,0:T(8,128)(2,1)S(1)} collective-permute-done((bf16[512,128]{1,0:T(8,128)(2,1)S(1)}, bf16[512,128]{1,0:T(8,128)(2,1)S(1)}, u32[]{:S(2)}, u32[]{:S(2)}) %collective-permute-start.11) | collective-permute-done | bytes 131104 | tf_op jit(solution)/shard_map/ppermute | solution.py:323
  66.2 2.9 %collective-permute-start.12 = (bf16[1024,128]{1,0:T(8,128)(2,1)S(1)}, bf16[1024,128]{1,0:T(8,128)(2,1)S(1)}, u32[]{:S(2)}, u32[]{:S(2)}) collective-permute-start(bf16[1024,128]{1,0:T(8,128)(2,1)S(1)} %add_join.1.refs_0_), channel_id=1, source_target_pairs={{0,48},{16,32},{32,16},{48,0},{1,49},{17,33},{33,17},{49,1},{2,50}... | collective-permute-start | bytes 786440 | tf_op jit(solution)/shard_map/ppermute | solution.py:323
  69.1 0.9 collective-permute-start.17
  69.9 0.5 collective-permute-start.15
  70.4 0.9 %sum_ctx.1 = bf16[8,16,640]{2,1,0:T(8,128)(2,1)} custom-call(bf16[8,768,128]{2,1,0:T(8,128)(2,1)S(1)} %all-to-all-done.1.x_ref), custom_call_target="tpu_custom_call" | custom-call | tf_op jit(solution)/shard_map/sum_ctx/pallas_call | solution.py:247
  71.3 7.2 %all-to-all-start.2 = ((bf16[8,16,640]{2,1,0:T(8,128)(2,1)}), bf16[8,16,640]{2,1,0:T(8,128)(2,1)S(1)}, u32[]{:S(2)}, u32[]{:S(2)}) async-start(bf16[8,16,640]{2,1,0:T(8,128)(2,1)} %sum_ctx.1), calls=%async_computation.2 | async-start | bytes 327680 | tf_op jit(solution)/shard_map/all_to_all | solution.py:339
  78.5 2.8 %collective-permute-done.12.refs_6_ = bf16[1024,128]{1,0:T(8,128)(2,1)S(1)} collective-permute-done((bf16[1024,128]{1,0:T(8,128)(2,1)S(1)}, bf16[1024,128]{1,0:T(8,128)(2,1)S(1)}, u32[]{:S(2)}, u32[]{:S(2)}) %collective-permute-start.12) | collective-permute-done | bytes 262176 | tf_op jit(solution)/shard_map/ppermute | solution.py:323
  81.3 0.5 collective-permute-start.14
  81.9 0.4 collective-permute-start.16
  82.4 0.9 unpack.1
  83.2 0.4 collective-permute-done.18.refs_5_
  83.6 0.4 collective-permute-done.16.refs_3_
  84.0 2.5 %widen.1 = (f32[512,1024]{1,0:T(8,128)}, f32[512,1024]{1,0:T(8,128)}) custom-call(bf16[1024,128]{1,0:T(8,128)(2,1)S(1)} %add_join.1.refs_0_, bf16[1024,128]{1,0:T(8,128)(2,1)S(1)} %collective-permute-done.14.refs_1_, bf16[1024,128]{1,0:T(8,128)(2,1)S(1)} %collective-permute-done.15.refs_2_, bf16[1024,128]{1,0:T(8,128)(2,1)S(1)} %collective-permute-done.16.refs_3_, ...), custom_call_target="tpu_custom_call" | custom-call | tf_op jit(solution)/shard_map/widen/pallas_call | solution.py:308
  86.4 0.6 sum_head.1
  (29 shorter events, 0.9 us)
Async XLA Ops:
  0.6 26.2 %copy-start.3 = (s32[16]{0:T(128)S(1)}, s32[16]{0:T(128)}, u32[]{:S(2)}) copy-start(s32[16]{0:T(128)} %order_ref.1) | copy-start | bytes 196
  0.6 26.2 %copy-start.2 = (s32[1,1024]{1,0:T(1,128)S(1)}, s32[1,1024]{1,0:T(1,128)}, u32[]{:S(2)}) copy-start(s32[1,1024]{1,0:T(1,128)} %refs_10_.1) | copy-start | bytes 12292
  0.7 26.2 %copy-start = (bf16[512,1024]{1,0:T(8,128)(2,1)S(1)}, bf16[512,1024]{1,0:T(8,128)(2,1)}, u32[]{:S(2)}) copy-start(bf16[512,1024]{1,0:T(8,128)(2,1)} %refs_8_.1) | copy-start | bytes 3145732
  0.7 7.8 %collective-permute-start = (bf16[576,128]{1,0:T(8,128)(2,1)}, bf16[576,128]{1,0:T(8,128)(2,1)S(1)}, u32[]{:S(2)}, u32[]{:S(2)}) collective-permute-start(bf16[576,128]{1,0:T(8,128)(2,1)} %bitcast.3), channel_id=1, source_target_pairs={{0,0},{1,17},{2,34},{3,51},{16,16},{17,1},{18,50},{19,35},{32,32},... | collective-permute-start | bytes 442376 | tf_op jit(solution)/shard_map/ppermute | solution.py:329
  8.5 18.4 %all-to-all-start = ((bf16[8,320,128]{2,1,0:T(8,128)(2,1)}), bf16[8,320,128]{2,1,0:T(8,128)(2,1)S(1)}, u32[]{:S(2)}, u32[]{:S(2)}) async-start(bf16[8,320,128]{2,1,0:T(8,128)(2,1)} %pack.1), calls=%async_computation | async-start | bytes 1310720 | tf_op jit(solution)/shard_map/all_to_all | solution.py:335
  13.0 10.1 %collective-permute-start.6 = (bf16[576,128]{1,0:T(8,128)(2,1)S(1)}, bf16[576,128]{1,0:T(8,128)(2,1)S(1)}, u32[]{:S(2)}, u32[]{:S(2)}) collective-permute-start(bf16[576,128]{1,0:T(8,128)(2,1)S(1)} %collective-permute-done.refs_0_), channel_id=1, source_target_pairs={{0,3},{1,2},{2,1},{3,0},{4,7},{5,6},{6,5},{7,4},{8,11},{9,10},{10,... | collective-permute-start | bytes 442376 | tf_op jit(solution)/shard_map/ppermute | solution.py:323
  16.0 8.2 %collective-permute-start.4 = (bf16[576,128]{1,0:T(8,128)(2,1)S(1)}, bf16[576,128]{1,0:T(8,128)(2,1)S(1)}, u32[]{:S(2)}, u32[]{:S(2)}) collective-permute-start(bf16[576,128]{1,0:T(8,128)(2,1)S(1)} %collective-permute-done.refs_0_), channel_id=1, source_target_pairs={{0,2},{1,3},{2,0},{3,1},{4,6},{5,7},{6,4},{7,5},{8,10},{9,11},{10,... | collective-permute-start | bytes 442376 | tf_op jit(solution)/shard_map/ppermute | solution.py:323
  16.2 9.3 %collective-permute-start.2 = (bf16[576,128]{1,0:T(8,128)(2,1)S(1)}, bf16[576,128]{1,0:T(8,128)(2,1)S(1)}, u32[]{:S(2)}, u32[]{:S(2)}) collective-permute-start(bf16[576,128]{1,0:T(8,128)(2,1)S(1)} %collective-permute-done.refs_0_), channel_id=1, source_target_pairs={{0,1},{1,0},{2,3},{3,2},{4,5},{5,4},{6,7},{7,6},{8,9},{9,8},{10,11... | collective-permute-start | bytes 442376 | tf_op jit(solution)/shard_map/ppermute | solution.py:323
  18.1 7.4 %collective-permute-start.1 = (bf16[576,128]{1,0:T(8,128)(2,1)S(1)}, bf16[576,128]{1,0:T(8,128)(2,1)S(1)}, u32[]{:S(2)}, u32[]{:S(2)}) collective-permute-start(bf16[576,128]{1,0:T(8,128)(2,1)S(1)} %collective-permute-done.refs_0_), channel_id=1, source_target_pairs={{0,8},{8,0},{1,9},{9,1},{2,10},{10,2},{3,11},{11,3},{4,12},{12,4},... | collective-permute-start | bytes 442376 | tf_op jit(solution)/shard_map/ppermute | solution.py:323
  23.1 2.4 %collective-permute-start.7 = (bf16[576,128]{1,0:T(8,128)(2,1)S(1)}, bf16[576,128]{1,0:T(8,128)(2,1)S(1)}, u32[]{:S(2)}, u32[]{:S(2)}) collective-permute-start(bf16[576,128]{1,0:T(8,128)(2,1)S(1)} %collective-permute-done.6.refs_6_), channel_id=1, source_target_pairs={{0,8},{8,0},{1,9},{9,1},{2,10},{10,2},{3,11},{11,3},{4,12},{12,4},... | collective-permute-start | bytes 442376 | tf_op jit(solution)/shard_map/ppermute | solution.py:323
  24.2 1.4 %collective-permute-start.5 = (bf16[576,128]{1,0:T(8,128)(2,1)S(1)}, bf16[576,128]{1,0:T(8,128)(2,1)S(1)}, u32[]{:S(2)}, u32[]{:S(2)}) collective-permute-start(bf16[576,128]{1,0:T(8,128)(2,1)S(1)} %collective-permute-done.4.refs_4_), channel_id=1, source_target_pairs={{0,8},{8,0},{1,9},{9,1},{2,10},{10,2},{3,11},{11,3},{4,12},{12,4},... | collective-permute-start | bytes 442376 | tf_op jit(solution)/shard_map/ppermute | solution.py:323
  25.5 1.4 %collective-permute-start.3 = (bf16[576,128]{1,0:T(8,128)(2,1)S(1)}, bf16[576,128]{1,0:T(8,128)(2,1)S(1)}, u32[]{:S(2)}, u32[]{:S(2)}) collective-permute-start(bf16[576,128]{1,0:T(8,128)(2,1)S(1)} %collective-permute-done.2.refs_2_), channel_id=1, source_target_pairs={{0,8},{8,0},{1,9},{9,1},{2,10},{10,2},{3,11},{11,3},{4,12},{12,4},... | collective-permute-start | bytes 442376 | tf_op jit(solution)/shard_map/ppermute | solution.py:323
  26.9 1.2 %copy-start.1 = (bf16[512,1024]{1,0:T(8,128)(2,1)S(1)}, bf16[512,1024]{1,0:T(8,128)(2,1)}, u32[]{:S(2)}) copy-start(bf16[512,1024]{1,0:T(8,128)(2,1)} %refs_9_.1) | copy-start | bytes 3145732
  39.3 31.1 %all-to-all-start.1 = ((bf16[8,768,128]{2,1,0:T(8,128)(2,1)}), bf16[8,768,128]{2,1,0:T(8,128)(2,1)S(1)}, u32[]{:S(2)}, u32[]{:S(2)}) async-start(bf16[8,768,128]{2,1,0:T(8,128)(2,1)} %get-tuple-element.19), calls=%async_computation.1 | async-start | bytes 3145728 | tf_op jit(solution)/shard_map/all_to_all | solution.py:337
  43.7 10.3 %collective-permute-start.8 = (bf16[512,128]{1,0:T(8,128)(2,1)S(1)}, bf16[512,128]{1,0:T(8,128)(2,1)S(1)}, u32[]{:S(2)}, u32[]{:S(2)}) collective-permute-start(bf16[512,128]{1,0:T(8,128)(2,1)S(1)} %get-tuple-element.17.a_ref), channel_id=1, source_target_pairs={{0,64},{64,0},{128,192},{192,128},{1,65},{65,1},{129,193},{193,129... | collective-permute-start | bytes 393224 | tf_op jit(solution)/shard_map/ppermute | solution.py:323
  47.0 10.8 %collective-permute-start.10 = (bf16[512,128]{1,0:T(8,128)(2,1)S(1)}, bf16[512,128]{1,0:T(8,128)(2,1)S(1)}, u32[]{:S(2)}, u32[]{:S(2)}) collective-permute-start(bf16[512,128]{1,0:T(8,128)(2,1)S(1)} %get-tuple-element.18.a_ref), channel_id=1, source_target_pairs={{0,192},{64,128},{128,64},{192,0},{1,193},{65,129},{129,65},{193,1... | collective-permute-start | bytes 393224 | tf_op jit(solution)/shard_map/ppermute | solution.py:323
  54.1 7.6 %collective-permute-start.9 = (bf16[512,128]{1,0:T(8,128)(2,1)S(1)}, bf16[512,128]{1,0:T(8,128)(2,1)S(1)}, u32[]{:S(2)}, u32[]{:S(2)}) collective-permute-start(bf16[512,128]{1,0:T(8,128)(2,1)S(1)} %add_uk.1.a_ref), channel_id=1, source_target_pairs={{0,192},{64,128},{128,64},{192,0},{1,193},{65,129},{129,65},{193,1... | collective-permute-start | bytes 393224 | tf_op jit(solution)/shard_map/ppermute | solution.py:323
  57.9 8.3 %collective-permute-start.11 = (bf16[512,128]{1,0:T(8,128)(2,1)S(1)}, bf16[512,128]{1,0:T(8,128)(2,1)S(1)}, u32[]{:S(2)}, u32[]{:S(2)}) collective-permute-start(bf16[512,128]{1,0:T(8,128)(2,1)S(1)} %add_uv.1.c_ref), channel_id=1, source_target_pairs={{0,64},{64,0},{128,192},{192,128},{1,65},{65,1},{129,193},{193,129... | collective-permute-start | bytes 393224 | tf_op jit(solution)/shard_map/ppermute | solution.py:323
  66.2 15.1 %collective-permute-start.12 = (bf16[1024,128]{1,0:T(8,128)(2,1)S(1)}, bf16[1024,128]{1,0:T(8,128)(2,1)S(1)}, u32[]{:S(2)}, u32[]{:S(2)}) collective-permute-start(bf16[1024,128]{1,0:T(8,128)(2,1)S(1)} %add_join.1.refs_0_), channel_id=1, source_target_pairs={{0,48},{16,32},{32,16},{48,0},{1,49},{17,33},{33,17},{49,1},{2,50}... | collective-permute-start | bytes 786440 | tf_op jit(solution)/shard_map/ppermute | solution.py:323
  69.1 12.8 %collective-permute-start.17 = (bf16[1024,128]{1,0:T(8,128)(2,1)S(1)}, bf16[1024,128]{1,0:T(8,128)(2,1)S(1)}, u32[]{:S(2)}, u32[]{:S(2)}) collective-permute-start(bf16[1024,128]{1,0:T(8,128)(2,1)S(1)} %add_join.1.refs_0_), channel_id=1, source_target_pairs={{0,32},{16,48},{32,0},{48,16},{1,33},{17,49},{33,1},{49,17},{2,34}... | collective-permute-start | bytes 786440 | tf_op jit(solution)/shard_map/ppermute | solution.py:323
  69.9 12.0 %collective-permute-start.15 = (bf16[1024,128]{1,0:T(8,128)(2,1)S(1)}, bf16[1024,128]{1,0:T(8,128)(2,1)S(1)}, u32[]{:S(2)}, u32[]{:S(2)}) collective-permute-start(bf16[1024,128]{1,0:T(8,128)(2,1)S(1)} %add_join.1.refs_0_), channel_id=1, source_target_pairs={{0,16},{16,0},{32,48},{48,32},{1,17},{17,1},{33,49},{49,33},{2,18}... | collective-permute-start | bytes 786440 | tf_op jit(solution)/shard_map/ppermute | solution.py:323
  71.3 15.1 %all-to-all-start.2 = ((bf16[8,16,640]{2,1,0:T(8,128)(2,1)}), bf16[8,16,640]{2,1,0:T(8,128)(2,1)S(1)}, u32[]{:S(2)}, u32[]{:S(2)}) async-start(bf16[8,16,640]{2,1,0:T(8,128)(2,1)} %sum_ctx.1), calls=%async_computation.2 | async-start | bytes 327680 | tf_op jit(solution)/shard_map/all_to_all | solution.py:339
  81.3 1.9 %collective-permute-start.13 = (bf16[1024,128]{1,0:T(8,128)(2,1)S(1)}, bf16[1024,128]{1,0:T(8,128)(2,1)S(1)}, u32[]{:S(2)}, u32[]{:S(2)}) collective-permute-start(bf16[1024,128]{1,0:T(8,128)(2,1)S(1)} %collective-permute-done.12.refs_6_), channel_id=1, source_target_pairs={{0,8},{8,0},{1,9},{9,1},{2,10},{10,2},{3,11},{11,3},{4,12},{12,4},... | collective-permute-start | bytes 786440 | tf_op jit(solution)/shard_map/ppermute | solution.py:323
  81.3 1.9 %collective-permute-start.14 = (bf16[1024,128]{1,0:T(8,128)(2,1)S(1)}, bf16[1024,128]{1,0:T(8,128)(2,1)S(1)}, u32[]{:S(2)}, u32[]{:S(2)}) collective-permute-start(bf16[1024,128]{1,0:T(8,128)(2,1)S(1)} %add_join.1.refs_0_), channel_id=1, source_target_pairs={{0,8},{8,0},{1,9},{9,1},{2,10},{10,2},{3,11},{11,3},{4,12},{12,4},... | collective-permute-start | bytes 786440 | tf_op jit(solution)/shard_map/ppermute | solution.py:323
  81.8 1.8 %collective-permute-start.18 = (bf16[1024,128]{1,0:T(8,128)(2,1)S(1)}, bf16[1024,128]{1,0:T(8,128)(2,1)S(1)}, u32[]{:S(2)}, u32[]{:S(2)}) collective-permute-start(bf16[1024,128]{1,0:T(8,128)(2,1)S(1)} %collective-permute-done.17.refs_4_), channel_id=1, source_target_pairs={{0,8},{8,0},{1,9},{9,1},{2,10},{10,2},{3,11},{11,3},{4,12},{12,4},... | collective-permute-start | bytes 786440 | tf_op jit(solution)/shard_map/ppermute | solution.py:323
  81.9 2.0 %collective-permute-start.16 = (bf16[1024,128]{1,0:T(8,128)(2,1)S(1)}, bf16[1024,128]{1,0:T(8,128)(2,1)S(1)}, u32[]{:S(2)}, u32[]{:S(2)}) collective-permute-start(bf16[1024,128]{1,0:T(8,128)(2,1)S(1)} %collective-permute-done.15.refs_2_), channel_id=1, source_target_pairs={{0,8},{8,0},{1,9},{9,1},{2,10},{10,2},{3,11},{11,3},{4,12},{12,4},... | collective-permute-start | bytes 786440 | tf_op jit(solution)/shard_map/ppermute | solution.py:323

commit v4 on v3

--- a/solution.py
+++ b/solution.py
@@ -27,67 +27,81 @@
 TN = ((0,), (0,))
 
 
-def pack_kernel(qn_ref, qr_ref, do_ref, after_ref, x_ref):
-    for h in range(8):
-        x_ref[h, 0:128, :] = qn_ref[0, :, h * 128:(h + 1) * 128]
-        x_ref[h, 128:256, :] = do_ref[0, :, h * 128:(h + 1) * 128]
-        x_ref[h, 256:320, 0:64] = qr_ref[0, 0:64, h * 64:(h + 1) * 64]
-        x_ref[h, 256:320, 64:128] = qr_ref[0, 64:128, h * 64:(h + 1) * 64]
-
-
-def pack(q_nope, q_rope, d_out, after):
+def pack_kernel(qn_ref, qr_ref, do_ref, kv_ref, *out_refs):
+    y = lax.axis_index("y")
+    core = lax.axis_index("core")
+    for d in range(4):
+        out = out_refs[d]
+        both = pl.ds(pl.multiple_of((y ^ d) * 128, 128), 128)
+        ropes = qr_ref[0, :, both]
+        for cr in range(2):
+            head = pl.ds(pl.multiple_of(((y ^ d) * 2 + (core ^ cr)) * 128, 128), 128)
+            at = cr * 320
+            out[at:at + 128, :] = qn_ref[0, :, head]
+            out[at + 128:at + 256, :] = do_ref[0, :, head]
+            rope = jnp.where(core == cr, ropes[:, 0:64], ropes[:, 64:128])
+            out[at + 256:at + 320, 0:64] = rope[0:64, :]
+            out[at + 256:at + 320, 64:128] = rope[64:128, :]
+        out[640:1216, :] = kv_ref[...]
+
+
+def pack(q_nope, q_rope, d_out, kvt):
     whole = pl.BlockSpec(memory_space=pltpu.VMEM)
     return pl.pallas_call(
         pack_kernel,
-        in_specs=[whole] * 3 + [pl.BlockSpec(memory_space=pl.ANY)],
-        out_specs=whole,
-        out_shape=jax.ShapeDtypeStruct((8, 320, 128), BF16),
+        in_specs=[whole] * 4,
+        out_specs=[whole] * 4,
+        out_shape=[jax.ShapeDtypeStruct((1216, 128), BF16)] * 4,
         compiler_params=pltpu.CompilerParams(vmem_limit_bytes=60 * MIB),
         cost_estimate=pl.CostEstimate(flops=0, bytes_accessed=5 * MIB, transcendentals=0),
         name="pack",
-    )(q_nope, q_rope, d_out, after)
-
-
-def attend_kernel(order_ref, x_in, *refs):
-    kv_hbm = refs[:8]
+    )(q_nope, q_rope, d_out, kvt)
+
+
+def attend_kernel(order_ref, *refs):
+    parts_hbm = refs[:8]
     uk_hbm, uv_hbm, seg_ref = refs[8:11]
     back_ref = refs[11]
     duk_ref, duv_ref = refs[12:14]
-    kv_in, uk_in, uv_in, keys, keyt, qfull, qn, g, dob, pt, dst, ot, dqt, dqr, dqs, dkr, inverse, sems = refs[14:]
+    x_in, kv_in, uk_in, uv_in, keys, keyt, qfull, qn, g, dob, pt, dst, ot, dqt, dqr, dqs, dkr, inverse, sems = refs[14:]
     y = lax.axis_index("y")
     core = lax.axis_index("core")
     me = y * 2 + core
-    block = y ^ lax.axis_index("x")
     cols = pl.ds(pl.multiple_of(me * 128, 128), 128)
 
-    load_uk = pltpu.make_async_copy(uk_hbm.at[:, cols], uk_in, sems.at[9])
-    load_uv = pltpu.make_async_copy(uv_hbm.at[:, cols], uv_in, sems.at[10])
-    loads = [pltpu.make_async_copy(kv_hbm[i], kv_in.at[i], sems.at[i]) for i in range(8)]
+    load_uk = pltpu.make_async_copy(uk_hbm.at[:, cols], uk_in, sems.at[16])
+    load_uv = pltpu.make_async_copy(uv_hbm.at[:, cols], uv_in, sems.at[17])
+    load_x = []
+    load_kv = []
+    for i in range(8):
+        at = (i % 2) * 320
+        load_x.append(pltpu.make_async_copy(parts_hbm[i].at[at:at + 320, :], x_in.at[i], sems.at[i]))
+        load_kv.append(pltpu.make_async_copy(parts_hbm[i].at[640:1216, :], kv_in.at[i], sems.at[8 + i]))
+    for load in [load_uk, load_uv] + load_x + load_kv:
+        load.start()
     for slot in range(16):
         inverse[order_ref[slot]] = slot
-    for load in [load_uk, load_uv] + loads:
-        load.start()
-
-    for slot in range(16):
-        c, e = slot // 2, slot % 2
-        row = pl.ds(pl.multiple_of(order_ref[slot] * SPAN, SPAN), SPAN)
-        qn[row, :] = x_in[c, e * 64:(e + 1) * 64, :]
-        g[row, :] = x_in[c, 128 + e * 64:128 + (e + 1) * 64, :]
-        qfull[row, LAT:LAT + ROPE] = x_in[c, 256:320, e * 64:(e + 1) * 64]
+
+    def place(i, e):
+        return pl.ds(pl.multiple_of(order_ref[(me ^ i) * 2 + e] * SPAN, SPAN), SPAN)
+
+    for i in range(8):
+        load_x[i].wait()
+        for e in range(2):
+            row = place(i, e)
+            qn[row, :] = x_in[i, e * 64:(e + 1) * 64, :]
+            g[row, :] = x_in[i, 128 + e * 64:128 + (e + 1) * 64, :]
+            qfull[row, LAT:LAT + ROPE] = x_in[i, 256:320, e * 64:(e + 1) * 64]
     load_uk.wait()
     load_uv.wait()
     uk = uk_in[...]
     qfull[:, 0:LAT] = dot(qn[...], uk, NT).astype(BF16)
     dob[...] = dot(g[...], uv_in[...], NT).astype(BF16)
-    for d in range(4):
-        for cr in range(2):
-            i = d * 2 + cr
-            ctx = (block ^ d) * 2 + (core ^ cr)
-            loads[i].wait()
-            piece = jnp.transpose(kv_in[i], (1, 0))
-            for e in range(2):
-                row = pl.ds(pl.multiple_of(order_ref[ctx * 2 + e] * SPAN, SPAN), SPAN)
-                keys[row, :] = piece[e * 64:(e + 1) * 64, :]
+    for i in range(8):
+        load_kv[i].wait()
+        piece = jnp.transpose(kv_in[i], (1, 0))
+        for e in range(2):
+            keys[place(i, e), :] = piece[e * 64:(e + 1) * 64, :]
     for b in range(4):
         keyt[:, b * 256:(b + 1) * 256] = jnp.transpose(keys[b * 256:(b + 1) * 256, :], (1, 0))
     seg = seg_ref[...]
@@ -171,15 +185,16 @@
         back_ref[c, 512:576, e * 64:(e + 1) * 64] = dkr[row, :]
 
 
-def attend(order, x, kvs, w_uk, w_uv, seg):
+def attend(order, parts, w_uk, w_uv, seg):
     hbm = pl.BlockSpec(memory_space=pl.ANY)
     vmem = pl.BlockSpec(memory_space=pltpu.VMEM)
     outs = [(8, 768, 128), (512, 128), (512, 128)]
     return pl.pallas_call(
         attend_kernel,
-        in_specs=[pl.BlockSpec(memory_space=pltpu.SMEM), vmem] + [hbm] * 10 + [vmem],
+        in_specs=[pl.BlockSpec(memory_space=pltpu.SMEM)] + [hbm] * 10 + [vmem],
         out_specs=[vmem] * 3,
         scratch_shapes=[
+            pltpu.VMEM((8, 320, 128), BF16),
             pltpu.VMEM((8, 576, 128), BF16),
             pltpu.VMEM((LAT, 128), BF16),
             pltpu.VMEM((LAT, 128), BF16),
@@ -197,13 +212,13 @@
             pltpu.VMEM((SEQ, ROPE), BF16),
             pltpu.VMEM((SEQ, ROPE), BF16),
             pltpu.SMEM((16,), jnp.int32),
-            pltpu.SemaphoreType.DMA((11,)),
+            pltpu.SemaphoreType.DMA((18,)),
         ],
         out_shape=[jax.ShapeDtypeStruct(shape, BF16) for shape in outs],
-        compiler_params=pltpu.CompilerParams(vmem_limit_bytes=36 * MIB),
+        compiler_params=pltpu.CompilerParams(vmem_limit_bytes=60 * MIB),
         cost_estimate=pl.CostEstimate(flops=9_000_000_000, bytes_accessed=12 * MIB, transcendentals=600_000),
         name="attend",
-    )(order, x, *kvs, w_uk, w_uv, seg)
+    )(order, *parts, w_uk, w_uv, seg)
 
 
 def call(kernel, name, out, *args):
@@ -324,20 +339,15 @@
 
 
 def local(q_nope, q_rope, kv_latent, d_out, w_uk, w_uv, segment_ids, span_order):
-    kvt = kv_latent[0].T
-    skew = [(i * 4 + j, (i ^ j) * 4 + j) for i in range(4) for j in range(4)]
-    first = lax.ppermute(kvt, ("y", "x"), skew)
-    kvs = []
-    for piece in [first] + [across(first, "x", d) for d in (1, 2, 3)]:
-        kvs += [piece, across(piece, "core", 1)]
-    send = pack(q_nope, q_rope, d_out, kvt)
-    send, first = lax.optimization_barrier((send, first))
-    x = lax.all_to_all(send, ("y", "core"), 0, 0, tiled=True)
-    back, duk, duv = attend(span_order, x, kvs, w_uk, w_uv, segment_ids)
+    sends = pack(q_nope, q_rope, d_out, kv_latent[0].T)
+    parts = []
+    for piece in [sends[0]] + [across(sends[d], "y", d) for d in (1, 2, 3)]:
+        parts += [piece, across(piece, "core", 1)]
+    back, duk, duv = attend(span_order, parts, w_uk, w_uv, segment_ids)
     back = lax.all_to_all(back, ("y", "core"), 0, 0, tiled=True)
     dq_nope, dq_rope = unpack(back)
-    parts = lax.all_to_all(sum_ctx(back), ("zl", "x"), 0, 0, tiled=True)
-    d_kv = call(sum_head_kernel, "sum_head", jax.ShapeDtypeStruct((1, 16, 576), BF16), parts)
+    sums = lax.all_to_all(sum_ctx(back), ("zl", "x"), 0, 0, tiled=True)
+    d_kv = call(sum_head_kernel, "sum_head", jax.ShapeDtypeStruct((1, 16, 576), BF16), sums)
     pair = [jax.ShapeDtypeStruct((512, 128), BF16)] * 2
     duk = call(add1_kernel, "add_uk", pair[0], duk, across(duk, "dp", 1))
     duv = call(add1_kernel, "add_uv", pair[0], duv, across(duv, "dp", 3))

time: 88.7 us -> 86.2 us (0.972)
  starting transfers between devices: 45 us -> 35.6 us
  waiting for transfers between devices: 21.9 us -> 28.9 us
    ppermute x18, waiting for transfers between devices: 19.8 us -> 28.9 us  [across(): return lax.ppermute(x, axis, [(i, i ^ step) for i in range(SIZES[axis])])]
    all_to_all x2 -> x1, starting transfers between devices: 11.7 us -> 6.89 us  [local(): sums = lax.all_to_all(sum_ctx(back), ('zl', 'x'), 0, 0, tiled=True)]
    ppermute x1 -> x0, starting transfers between devices: 3.62 us -> none  [local(): first = lax.ppermute(kvt, ('y', 'x'), skew)]
    ppermute x1 -> x0, waiting for transfers between devices: 2.12 us -> none  [local(): first = lax.ppermute(kvt, ('y', 'x'), skew)]
  transfers between devices with their start and end apart: 22 -> 20, of which waited for: 13 -> 11; matrix products, arithmetic and copies ran while one was open for 0% -> 0% of each run, Pallas kernels for 7% -> 5%
where the time goes in v4:
time: 86.2 us; the launch traced here: 84.7 us
  starting transfers between devices  35.6 us (41%)
  waiting for transfers between devices  28.9 us (34%)
  Pallas kernels  18.7 us (22%)
    ppermute x18, waiting for transfers between devices, across(): return lax.ppermute(x, axis, [(i, i ^ step) for i in range(SIZES[axis])])  28.9 us
    ppermute x18, starting transfers between devices, across(): return lax.ppermute(x, axis, [(i, i ^ step) for i in range(SIZES[axis])])  25 us
    pallas_call x1, Pallas kernels, attend(): pl.pallas_call(attend_kernel, in_specs=[pl.BlockSpec(memory_space=pltpu.S...  11.2 us
    all_to_all x1, starting transfers between devices, local(): sums = lax.all_to_all(sum_ctx(back), ('zl', 'x'), 0, 0, tiled=True)  6.89 us
    all_to_all x1, starting transfers between devices, local(): back = lax.all_to_all(back, ('y', 'core'), 0, 0, tiled=True)  3.73 us
    pallas_call x1, Pallas kernels, widen(): pl.pallas_call(widen_kernel, grid=(4,), in_specs=[piece] * 8, out_specs=[...  2.46 us
    pallas_call x1, Pallas kernels, pack(): pl.pallas_call(pack_kernel, in_specs=[whole] * 4, out_specs=[whole] * 4,...  2.45 us
  transfers between devices with their start and end apart: 20, of which 11 were waited for; matrix products, arithmetic and copies ran while one was open for 0% of the time, Pallas kernels for 5%

profile of v4, /device:TPU:2, one launch (start us, length us, event | category | flops | bytes accessed | tf_op | source)
XLA Modules:
  0.0 84.7 jit_solution(3270171023190667151)
XLA Ops:
  0.6 2.4 %pack.1 = (bf16[1216,128]{1,0:T(8,128)(2,1)}, bf16[1216,128]{1,0:T(8,128)(2,1)}, bf16[1216,128]{1,0:T(8,128)(2,1)}, bf16[1216,128]{1,0:T(8,128)(2,1)}) custom-call(bf16[1,128,1024]{2,1,0:T(8,128)(2,1)} %qn_ref.1, bf16[1,128,512]{2,1,0:T(8,128)(2,1)} %qr_ref.1, bf16[1,128,1024]{2,1,0:T(8,128)(2,1)} %do_ref.1, bf16[576,128]{1,0:T(8,128)(2,1)} %bitcast.3), custom_call_target="tpu_custom_call" | custom-call | bytes 5242880 | tf_op jit(solution)/shard_map/pack/pallas_call | solution.py:50
  3.1 1.6 %collective-permute-start.1 = (bf16[1216,128]{1,0:T(8,128)(2,1)}, bf16[1216,128]{1,0:T(8,128)(2,1)S(1)}, u32[]{:S(2)}, u32[]{:S(2)}) collective-permute-start(bf16[1216,128]{1,0:T(8,128)(2,1)} %get-tuple-element.20), channel_id=1, source_target_pairs={{0,16},{16,0},{32,48},{48,32},{1,17},{17,1},{33,49},{49,33},{2,18}... | collective-permute-start | bytes 933896 | tf_op jit(solution)/shard_map/ppermute | solution.py:338
  4.7 2.9 %collective-permute-start.3 = (bf16[1216,128]{1,0:T(8,128)(2,1)}, bf16[1216,128]{1,0:T(8,128)(2,1)S(1)}, u32[]{:S(2)}, u32[]{:S(2)}) collective-permute-start(bf16[1216,128]{1,0:T(8,128)(2,1)} %get-tuple-element.21), channel_id=1, source_target_pairs={{0,32},{16,48},{32,0},{48,16},{1,33},{17,49},{33,1},{49,17},{2,34}... | collective-permute-start | bytes 933896 | tf_op jit(solution)/shard_map/ppermute | solution.py:338
  7.6 0.2 collective-permute-start.5
  7.8 5.8 %collective-permute-done.1.refs_2_ = bf16[1216,128]{1,0:T(8,128)(2,1)S(1)} collective-permute-done((bf16[1216,128]{1,0:T(8,128)(2,1)}, bf16[1216,128]{1,0:T(8,128)(2,1)S(1)}, u32[]{:S(2)}, u32[]{:S(2)}) %collective-permute-start.1) | collective-permute-done | bytes 311328 | tf_op jit(solution)/shard_map/ppermute | solution.py:338
  13.5 8.1 %collective-permute-done.3.refs_4_ = bf16[1216,128]{1,0:T(8,128)(2,1)S(1)} collective-permute-done((bf16[1216,128]{1,0:T(8,128)(2,1)}, bf16[1216,128]{1,0:T(8,128)(2,1)S(1)}, u32[]{:S(2)}, u32[]{:S(2)}) %collective-permute-start.3) | collective-permute-done | bytes 311328 | tf_op jit(solution)/shard_map/ppermute | solution.py:338
  21.6 2.6 %collective-permute-done.5.refs_6_ = bf16[1216,128]{1,0:T(8,128)(2,1)S(1)} collective-permute-done((bf16[1216,128]{1,0:T(8,128)(2,1)}, bf16[1216,128]{1,0:T(8,128)(2,1)S(1)}, u32[]{:S(2)}, u32[]{:S(2)}) %collective-permute-start.5) | collective-permute-done | bytes 311328 | tf_op jit(solution)/shard_map/ppermute | solution.py:338
  24.3 1.5 %collective-permute-done.6.refs_7_ = bf16[1216,128]{1,0:T(8,128)(2,1)S(1)} collective-permute-done((bf16[1216,128]{1,0:T(8,128)(2,1)S(1)}, bf16[1216,128]{1,0:T(8,128)(2,1)S(1)}, u32[]{:S(2)}, u32[]{:S(2)}) %collective-permute-start.6) | collective-permute-done | bytes 311328 | tf_op jit(solution)/shard_map/ppermute | solution.py:338
  25.9 0.7 copy-done.8
  26.6 11.2 %attend.1 = (bf16[8,768,128]{2,1,0:T(8,128)(2,1)}, bf16[512,128]{1,0:T(8,128)(2,1)}, bf16[512,128]{1,0:T(8,128)(2,1)}) custom-call(s32[16]{0:T(128)} %order_ref.1, bf16[1216,128]{1,0:T(8,128)(2,1)} %get-tuple-element.19.refs_0_, bf16[1216,128]{1,0:T(8,128)(2,1)} %copy-done.5, bf16[1216,128]{1,0:T(8,128)(2,1)} %copy-done.2, bf16[1216,128]{1,0:T(8,128)(2,1)} %copy-done.6, ...), custom_call_target="tpu_custom_call" | custom-call | flops 8999999488 | bytes 12582912 | tf_op jit(solution)/shard_map/attend/pallas_call | solution.py:192
  37.8 3.7 %all-to-all-start = ((bf16[8,768,128]{2,1,0:T(8,128)(2,1)}), bf16[8,768,128]{2,1,0:T(8,128)(2,1)S(1)}, u32[]{:S(2)}, u32[]{:S(2)}) async-start(bf16[8,768,128]{2,1,0:T(8,128)(2,1)} %get-tuple-element.25), calls=%async_computation | async-start | bytes 3145728 | tf_op jit(solution)/shard_map/all_to_all | solution.py:347
  41.6 3.5 %collective-permute-start.7 = (bf16[512,128]{1,0:T(8,128)(2,1)S(1)}, bf16[512,128]{1,0:T(8,128)(2,1)S(1)}, u32[]{:S(2)}, u32[]{:S(2)}) collective-permute-start(bf16[512,128]{1,0:T(8,128)(2,1)S(1)} %copy-done.1), channel_id=1, source_target_pairs={{0,64},{64,0},{128,192},{192,128},{1,65},{65,1},{129,193},{193,129... | collective-permute-start | bytes 393224 | tf_op jit(solution)/shard_map/ppermute | solution.py:338
  45.1 4.5 %collective-permute-start.9 = (bf16[512,128]{1,0:T(8,128)(2,1)S(1)}, bf16[512,128]{1,0:T(8,128)(2,1)S(1)}, u32[]{:S(2)}, u32[]{:S(2)}) collective-permute-start(bf16[512,128]{1,0:T(8,128)(2,1)S(1)} %copy-done), channel_id=1, source_target_pairs={{0,192},{64,128},{128,64},{192,0},{1,193},{65,129},{129,65},{193,1... | collective-permute-start | bytes 393224 | tf_op jit(solution)/shard_map/ppermute | solution.py:338
  49.6 2.2 %collective-permute-done.7.b_ref = bf16[512,128]{1,0:T(8,128)(2,1)S(1)} collective-permute-done((bf16[512,128]{1,0:T(8,128)(2,1)S(1)}, bf16[512,128]{1,0:T(8,128)(2,1)S(1)}, u32[]{:S(2)}, u32[]{:S(2)}) %collective-permute-start.7) | collective-permute-done | bytes 131104 | tf_op jit(solution)/shard_map/ppermute | solution.py:338
  51.8 3.7 %collective-permute-start.8 = (bf16[512,128]{1,0:T(8,128)(2,1)S(1)}, bf16[512,128]{1,0:T(8,128)(2,1)S(1)}, u32[]{:S(2)}, u32[]{:S(2)}) collective-permute-start(bf16[512,128]{1,0:T(8,128)(2,1)S(1)} %add_uk.1.a_ref), channel_id=1, source_target_pairs={{0,192},{64,128},{128,64},{192,0},{1,193},{65,129},{129,65},{193,1... | collective-permute-start | bytes 393224 | tf_op jit(solution)/shard_map/ppermute | solution.py:338
  55.6 3.5 %collective-permute-start.10 = (bf16[512,128]{1,0:T(8,128)(2,1)S(1)}, bf16[512,128]{1,0:T(8,128)(2,1)S(1)}, u32[]{:S(2)}, u32[]{:S(2)}) collective-permute-start(bf16[512,128]{1,0:T(8,128)(2,1)S(1)} %add_uv.1.c_ref), channel_id=1, source_target_pairs={{0,64},{64,0},{128,192},{192,128},{1,65},{65,1},{129,193},{193,129... | collective-permute-start | bytes 393224 | tf_op jit(solution)/shard_map/ppermute | solution.py:338
  59.1 0.2 collective-permute-done.8.b_ref
  59.3 4.5 %collective-permute-done.10.d_ref = bf16[512,128]{1,0:T(8,128)(2,1)S(1)} collective-permute-done((bf16[512,128]{1,0:T(8,128)(2,1)S(1)}, bf16[512,128]{1,0:T(8,128)(2,1)S(1)}, u32[]{:S(2)}, u32[]{:S(2)}) %collective-permute-start.10) | collective-permute-done | bytes 131104 | tf_op jit(solution)/shard_map/ppermute | solution.py:338
  63.8 3.0 %collective-permute-start.11 = (bf16[1024,128]{1,0:T(8,128)(2,1)S(1)}, bf16[1024,128]{1,0:T(8,128)(2,1)S(1)}, u32[]{:S(2)}, u32[]{:S(2)}) collective-permute-start(bf16[1024,128]{1,0:T(8,128)(2,1)S(1)} %add_join.1.refs_0_), channel_id=1, source_target_pairs={{0,48},{16,32},{32,16},{48,0},{1,49},{17,33},{33,17},{49,1},{2,50}... | collective-permute-start | bytes 786440 | tf_op jit(solution)/shard_map/ppermute | solution.py:338
  66.8 0.8 collective-permute-start.16
  67.7 0.4 collective-permute-start.14
  68.0 0.9 %sum_ctx.1 = bf16[8,16,640]{2,1,0:T(8,128)(2,1)} custom-call(bf16[8,768,128]{2,1,0:T(8,128)(2,1)S(1)} %all-to-all-done.x_ref), custom_call_target="tpu_custom_call" | custom-call | tf_op jit(solution)/shard_map/sum_ctx/pallas_call | solution.py:262
  68.9 6.9 %all-to-all-start.1 = ((bf16[8,16,640]{2,1,0:T(8,128)(2,1)}), bf16[8,16,640]{2,1,0:T(8,128)(2,1)S(1)}, u32[]{:S(2)}, u32[]{:S(2)}) async-start(bf16[8,16,640]{2,1,0:T(8,128)(2,1)} %sum_ctx.1), calls=%async_computation.1 | async-start | bytes 327680 | tf_op jit(solution)/shard_map/all_to_all | solution.py:349
  75.8 3.1 %collective-permute-done.11.refs_6_ = bf16[1024,128]{1,0:T(8,128)(2,1)S(1)} collective-permute-done((bf16[1024,128]{1,0:T(8,128)(2,1)S(1)}, bf16[1024,128]{1,0:T(8,128)(2,1)S(1)}, u32[]{:S(2)}, u32[]{:S(2)}) %collective-permute-start.11) | collective-permute-done | bytes 262176 | tf_op jit(solution)/shard_map/ppermute | solution.py:338
  79.0 0.5 collective-permute-start.13
  79.5 0.2 collective-permute-done.14.refs_2_
  79.7 0.4 collective-permute-start.15
  80.0 0.9 %unpack.1 = (bf16[1,128,1024]{2,1,0:T(8,128)(2,1)}, bf16[1,128,512]{2,1,0:T(8,128)(2,1)}) custom-call(bf16[8,768,128]{2,1,0:T(8,128)(2,1)S(1)} %all-to-all-done.x_ref), custom_call_target="tpu_custom_call" | custom-call | tf_op jit(solution)/shard_map/unpack/pallas_call | solution.py:288
  80.9 0.4 collective-permute-done.17.refs_5_
  81.3 0.4 collective-permute-done.15.refs_3_
  81.6 2.5 %widen.1 = (f32[512,1024]{1,0:T(8,128)}, f32[512,1024]{1,0:T(8,128)}) custom-call(bf16[1024,128]{1,0:T(8,128)(2,1)S(1)} %add_join.1.refs_0_, bf16[1024,128]{1,0:T(8,128)(2,1)S(1)} %collective-permute-done.13.refs_1_, bf16[1024,128]{1,0:T(8,128)(2,1)S(1)} %collective-permute-done.14.refs_2_, bf16[1024,128]{1,0:T(8,128)(2,1)S(1)} %collective-permute-done.15.refs_3_, ...), custom_call_target="tpu_custom_call" | custom-call | tf_op jit(solution)/shard_map/widen/pallas_call | solution.py:323
  84.1 0.6 sum_head.1
  (35 shorter events, 0.2 us)
Async XLA Ops:
  3.1 10.5 %collective-permute-start.1 = (bf16[1216,128]{1,0:T(8,128)(2,1)}, bf16[1216,128]{1,0:T(8,128)(2,1)S(1)}, u32[]{:S(2)}, u32[]{:S(2)}) collective-permute-start(bf16[1216,128]{1,0:T(8,128)(2,1)} %get-tuple-element.20), channel_id=1, source_target_pairs={{0,16},{16,0},{32,48},{48,32},{1,17},{17,1},{33,49},{49,33},{2,18}... | collective-permute-start | bytes 933896 | tf_op jit(solution)/shard_map/ppermute | solution.py:338
  4.7 17.0 %collective-permute-start.3 = (bf16[1216,128]{1,0:T(8,128)(2,1)}, bf16[1216,128]{1,0:T(8,128)(2,1)S(1)}, u32[]{:S(2)}, u32[]{:S(2)}) collective-permute-start(bf16[1216,128]{1,0:T(8,128)(2,1)} %get-tuple-element.21), channel_id=1, source_target_pairs={{0,32},{16,48},{32,0},{48,16},{1,33},{17,49},{33,1},{49,17},{2,34}... | collective-permute-start | bytes 933896 | tf_op jit(solution)/shard_map/ppermute | solution.py:338
  7.6 16.6 %collective-permute-start.5 = (bf16[1216,128]{1,0:T(8,128)(2,1)}, bf16[1216,128]{1,0:T(8,128)(2,1)S(1)}, u32[]{:S(2)}, u32[]{:S(2)}) collective-permute-start(bf16[1216,128]{1,0:T(8,128)(2,1)} %get-tuple-element.22), channel_id=1, source_target_pairs={{0,48},{16,32},{32,16},{48,0},{1,49},{17,33},{33,17},{49,1},{2,50}... | collective-permute-start | bytes 933896 | tf_op jit(solution)/shard_map/ppermute | solution.py:338
  7.8 16.4 %collective-permute-start = (bf16[1216,128]{1,0:T(8,128)(2,1)}, bf16[1216,128]{1,0:T(8,128)(2,1)S(1)}, u32[]{:S(2)}, u32[]{:S(2)}) collective-permute-start(bf16[1216,128]{1,0:T(8,128)(2,1)} %get-tuple-element.19.refs_0_), channel_id=1, source_target_pairs={{0,8},{8,0},{1,9},{9,1},{2,10},{10,2},{3,11},{11,3},{4,12},{12,4},... | collective-permute-start | bytes 933896 | tf_op jit(solution)/shard_map/ppermute | solution.py:338
  13.5 12.3 %copy-start.2 = (bf16[1216,128]{1,0:T(8,128)(2,1)}, bf16[1216,128]{1,0:T(8,128)(2,1)S(1)}, u32[]{:S(2)}) copy-start(bf16[1216,128]{1,0:T(8,128)(2,1)S(1)} %collective-permute-done.1.refs_2_) | copy-start | bytes 933892
  13.5 10.7 %collective-permute-start.2 = (bf16[1216,128]{1,0:T(8,128)(2,1)S(1)}, bf16[1216,128]{1,0:T(8,128)(2,1)S(1)}, u32[]{:S(2)}, u32[]{:S(2)}) collective-permute-start(bf16[1216,128]{1,0:T(8,128)(2,1)S(1)} %collective-permute-done.1.refs_2_), channel_id=1, source_target_pairs={{0,8},{8,0},{1,9},{9,1},{2,10},{10,2},{3,11},{11,3},{4,12},{12,4},... | collective-permute-start | bytes 933896 | tf_op jit(solution)/shard_map/ppermute | solution.py:338
  21.6 4.2 %copy-start.3 = (bf16[1216,128]{1,0:T(8,128)(2,1)}, bf16[1216,128]{1,0:T(8,128)(2,1)S(1)}, u32[]{:S(2)}) copy-start(bf16[1216,128]{1,0:T(8,128)(2,1)S(1)} %collective-permute-done.3.refs_4_) | copy-start | bytes 933892
  21.6 2.6 %collective-permute-start.4 = (bf16[1216,128]{1,0:T(8,128)(2,1)S(1)}, bf16[1216,128]{1,0:T(8,128)(2,1)S(1)}, u32[]{:S(2)}, u32[]{:S(2)}) collective-permute-start(bf16[1216,128]{1,0:T(8,128)(2,1)S(1)} %collective-permute-done.3.refs_4_), channel_id=1, source_target_pairs={{0,8},{8,0},{1,9},{9,1},{2,10},{10,2},{3,11},{11,3},{4,12},{12,4},... | collective-permute-start | bytes 933896 | tf_op jit(solution)/shard_map/ppermute | solution.py:338
  24.2 1.6 %copy-start.4 = (bf16[1216,128]{1,0:T(8,128)(2,1)}, bf16[1216,128]{1,0:T(8,128)(2,1)S(1)}, u32[]{:S(2)}) copy-start(bf16[1216,128]{1,0:T(8,128)(2,1)S(1)} %collective-permute-done.5.refs_6_) | copy-start | bytes 933892
  24.2 1.6 %collective-permute-start.6 = (bf16[1216,128]{1,0:T(8,128)(2,1)S(1)}, bf16[1216,128]{1,0:T(8,128)(2,1)S(1)}, u32[]{:S(2)}, u32[]{:S(2)}) collective-permute-start(bf16[1216,128]{1,0:T(8,128)(2,1)S(1)} %collective-permute-done.5.refs_6_), channel_id=1, source_target_pairs={{0,8},{8,0},{1,9},{9,1},{2,10},{10,2},{3,11},{11,3},{4,12},{12,4},... | collective-permute-start | bytes 933896 | tf_op jit(solution)/shard_map/ppermute | solution.py:338
  24.2 1.6 %copy-start.5 = (bf16[1216,128]{1,0:T(8,128)(2,1)}, bf16[1216,128]{1,0:T(8,128)(2,1)S(1)}, u32[]{:S(2)}) copy-start(bf16[1216,128]{1,0:T(8,128)(2,1)S(1)} %collective-permute-done.refs_1_) | copy-start | bytes 933892
  24.2 1.6 %copy-start.6 = (bf16[1216,128]{1,0:T(8,128)(2,1)}, bf16[1216,128]{1,0:T(8,128)(2,1)S(1)}, u32[]{:S(2)}) copy-start(bf16[1216,128]{1,0:T(8,128)(2,1)S(1)} %collective-permute-done.2.refs_3_) | copy-start | bytes 933892
  24.2 1.6 %copy-start.7 = (bf16[1216,128]{1,0:T(8,128)(2,1)}, bf16[1216,128]{1,0:T(8,128)(2,1)S(1)}, u32[]{:S(2)}) copy-start(bf16[1216,128]{1,0:T(8,128)(2,1)S(1)} %collective-permute-done.4.refs_5_) | copy-start | bytes 933892
  25.8 0.7 copy-start.8
  37.8 3.8 %copy-start.1 = (bf16[512,128]{1,0:T(8,128)(2,1)S(1)}, bf16[512,128]{1,0:T(8,128)(2,1)}, u32[]{:S(2)}) copy-start(bf16[512,128]{1,0:T(8,128)(2,1)} %get-tuple-element.23.a_ref) | copy-start | bytes 393220
  37.8 7.3 %copy-start = (bf16[512,128]{1,0:T(8,128)(2,1)S(1)}, bf16[512,128]{1,0:T(8,128)(2,1)}, u32[]{:S(2)}) copy-start(bf16[512,128]{1,0:T(8,128)(2,1)} %get-tuple-element.24.a_ref) | copy-start | bytes 393220
  37.8 30.2 %all-to-all-start = ((bf16[8,768,128]{2,1,0:T(8,128)(2,1)}), bf16[8,768,128]{2,1,0:T(8,128)(2,1)S(1)}, u32[]{:S(2)}, u32[]{:S(2)}) async-start(bf16[8,768,128]{2,1,0:T(8,128)(2,1)} %get-tuple-element.25), calls=%async_computation | async-start | bytes 3145728 | tf_op jit(solution)/shard_map/all_to_all | solution.py:347
  41.6 10.2 %collective-permute-start.7 = (bf16[512,128]{1,0:T(8,128)(2,1)S(1)}, bf16[512,128]{1,0:T(8,128)(2,1)S(1)}, u32[]{:S(2)}, u32[]{:S(2)}) collective-permute-start(bf16[512,128]{1,0:T(8,128)(2,1)S(1)} %copy-done.1), channel_id=1, source_target_pairs={{0,64},{64,0},{128,192},{192,128},{1,65},{65,1},{129,193},{193,129... | collective-permute-start | bytes 393224 | tf_op jit(solution)/shard_map/ppermute | solution.py:338
  45.1 10.5 %collective-permute-start.9 = (bf16[512,128]{1,0:T(8,128)(2,1)S(1)}, bf16[512,128]{1,0:T(8,128)(2,1)S(1)}, u32[]{:S(2)}, u32[]{:S(2)}) collective-permute-start(bf16[512,128]{1,0:T(8,128)(2,1)S(1)} %copy-done), channel_id=1, source_target_pairs={{0,192},{64,128},{128,64},{192,0},{1,193},{65,129},{129,65},{193,1... | collective-permute-start | bytes 393224 | tf_op jit(solution)/shard_map/ppermute | solution.py:338
  51.8 7.5 %collective-permute-start.8 = (bf16[512,128]{1,0:T(8,128)(2,1)S(1)}, bf16[512,128]{1,0:T(8,128)(2,1)S(1)}, u32[]{:S(2)}, u32[]{:S(2)}) collective-permute-start(bf16[512,128]{1,0:T(8,128)(2,1)S(1)} %add_uk.1.a_ref), channel_id=1, source_target_pairs={{0,192},{64,128},{128,64},{192,0},{1,193},{65,129},{129,65},{193,1... | collective-permute-start | bytes 393224 | tf_op jit(solution)/shard_map/ppermute | solution.py:338
  55.6 8.2 %collective-permute-start.10 = (bf16[512,128]{1,0:T(8,128)(2,1)S(1)}, bf16[512,128]{1,0:T(8,128)(2,1)S(1)}, u32[]{:S(2)}, u32[]{:S(2)}) collective-permute-start(bf16[512,128]{1,0:T(8,128)(2,1)S(1)} %add_uv.1.c_ref), channel_id=1, source_target_pairs={{0,64},{64,0},{128,192},{192,128},{1,65},{65,1},{129,193},{193,129... | collective-permute-start | bytes 393224 | tf_op jit(solution)/shard_map/ppermute | solution.py:338
  63.8 15.1 %collective-permute-start.11 = (bf16[1024,128]{1,0:T(8,128)(2,1)S(1)}, bf16[1024,128]{1,0:T(8,128)(2,1)S(1)}, u32[]{:S(2)}, u32[]{:S(2)}) collective-permute-start(bf16[1024,128]{1,0:T(8,128)(2,1)S(1)} %add_join.1.refs_0_), channel_id=1, source_target_pairs={{0,48},{16,32},{32,16},{48,0},{1,49},{17,33},{33,17},{49,1},{2,50}... | collective-permute-start | bytes 786440 | tf_op jit(solution)/shard_map/ppermute | solution.py:338
  66.8 12.7 %collective-permute-start.16 = (bf16[1024,128]{1,0:T(8,128)(2,1)S(1)}, bf16[1024,128]{1,0:T(8,128)(2,1)S(1)}, u32[]{:S(2)}, u32[]{:S(2)}) collective-permute-start(bf16[1024,128]{1,0:T(8,128)(2,1)S(1)} %add_join.1.refs_0_), channel_id=1, source_target_pairs={{0,32},{16,48},{32,0},{48,16},{1,33},{17,49},{33,1},{49,17},{2,34}... | collective-permute-start | bytes 786440 | tf_op jit(solution)/shard_map/ppermute | solution.py:338
  67.7 12.0 %collective-permute-start.14 = (bf16[1024,128]{1,0:T(8,128)(2,1)S(1)}, bf16[1024,128]{1,0:T(8,128)(2,1)S(1)}, u32[]{:S(2)}, u32[]{:S(2)}) collective-permute-start(bf16[1024,128]{1,0:T(8,128)(2,1)S(1)} %add_join.1.refs_0_), channel_id=1, source_target_pairs={{0,16},{16,0},{32,48},{48,32},{1,17},{17,1},{33,49},{49,33},{2,18}... | collective-permute-start | bytes 786440 | tf_op jit(solution)/shard_map/ppermute | solution.py:338
  68.9 15.2 %all-to-all-start.1 = ((bf16[8,16,640]{2,1,0:T(8,128)(2,1)}), bf16[8,16,640]{2,1,0:T(8,128)(2,1)S(1)}, u32[]{:S(2)}, u32[]{:S(2)}) async-start(bf16[8,16,640]{2,1,0:T(8,128)(2,1)} %sum_ctx.1), calls=%async_computation.1 | async-start | bytes 327680 | tf_op jit(solution)/shard_map/all_to_all | solution.py:349
  79.0 1.9 %collective-permute-start.12 = (bf16[1024,128]{1,0:T(8,128)(2,1)S(1)}, bf16[1024,128]{1,0:T(8,128)(2,1)S(1)}, u32[]{:S(2)}, u32[]{:S(2)}) collective-permute-start(bf16[1024,128]{1,0:T(8,128)(2,1)S(1)} %collective-permute-done.11.refs_6_), channel_id=1, source_target_pairs={{0,8},{8,0},{1,9},{9,1},{2,10},{10,2},{3,11},{11,3},{4,12},{12,4},... | collective-permute-start | bytes 786440 | tf_op jit(solution)/shard_map/ppermute | solution.py:338
  79.0 1.9 %collective-permute-start.13 = (bf16[1024,128]{1,0:T(8,128)(2,1)S(1)}, bf16[1024,128]{1,0:T(8,128)(2,1)S(1)}, u32[]{:S(2)}, u32[]{:S(2)}) collective-permute-start(bf16[1024,128]{1,0:T(8,128)(2,1)S(1)} %add_join.1.refs_0_), channel_id=1, source_target_pairs={{0,8},{8,0},{1,9},{9,1},{2,10},{10,2},{3,11},{11,3},{4,12},{12,4},... | collective-permute-start | bytes 786440 | tf_op jit(solution)/shard_map/ppermute | solution.py:338
  79.5 1.8 %collective-permute-start.17 = (bf16[1024,128]{1,0:T(8,128)(2,1)S(1)}, bf16[1024,128]{1,0:T(8,128)(2,1)S(1)}, u32[]{:S(2)}, u32[]{:S(2)}) collective-permute-start(bf16[1024,128]{1,0:T(8,128)(2,1)S(1)} %collective-permute-done.16.refs_4_), channel_id=1, source_target_pairs={{0,8},{8,0},{1,9},{9,1},{2,10},{10,2},{3,11},{11,3},{4,12},{12,4},... | collective-permute-start | bytes 786440 | tf_op jit(solution)/shard_map/ppermute | solution.py:338
  79.7 2.0 %collective-permute-start.15 = (bf16[1024,128]{1,0:T(8,128)(2,1)S(1)}, bf16[1024,128]{1,0:T(8,128)(2,1)S(1)}, u32[]{:S(2)}, u32[]{:S(2)}) collective-permute-start(bf16[1024,128]{1,0:T(8,128)(2,1)S(1)} %collective-permute-done.14.refs_2_), channel_id=1, source_target_pairs={{0,8},{8,0},{1,9},{9,1},{2,10},{10,2},{3,11},{11,3},{4,12},{12,4},... | collective-permute-start | bytes 786440 | tf_op jit(solution)/shard_map/ppermute | solution.py:338

commit v5 on v4

--- a/solution.py
+++ b/solution.py
@@ -346,7 +346,8 @@
     back, duk, duv = attend(span_order, parts, w_uk, w_uv, segment_ids)
     back = lax.all_to_all(back, ("y", "core"), 0, 0, tiled=True)
     dq_nope, dq_rope = unpack(back)
-    sums = lax.all_to_all(sum_ctx(back), ("zl", "x"), 0, 0, tiled=True)
+    own, dq_nope, dq_rope = lax.optimization_barrier((sum_ctx(back), dq_nope, dq_rope))
+    sums = lax.all_to_all(own, ("zl", "x"), 0, 0, tiled=True)
     d_kv = call(sum_head_kernel, "sum_head", jax.ShapeDtypeStruct((1, 16, 576), BF16), sums)
     pair = [jax.ShapeDtypeStruct((512, 128), BF16)] * 2
     duk = call(add1_kernel, "add_uk", pair[0], duk, across(duk, "dp", 1))
@@ -356,7 +357,7 @@
     pieces = []
     for piece in [whole] + [across(whole, "y", d) for d in (1, 2, 3)]:
         pieces += [piece, across(piece, "core", 1)]
-    pieces[-1], dq_nope, dq_rope = lax.optimization_barrier((pieces[-1], dq_nope, dq_rope))
+    pieces[-1], d_kv = lax.optimization_barrier((pieces[-1], d_kv))
     dw_uk, dw_uv = widen(pieces)
     return dq_nope, dq_rope, d_kv, dw_uk, dw_uv
 

time: 86.2 us -> 86.5 us (level)
    all_to_all x1, waiting for transfers between devices: 0.01 us -> 1.86 us  [local(): sums = lax.all_to_all(own, ('zl', 'x'), 0, 0, tiled=True)]
    ppermute x18, waiting for transfers between devices: 28.9 us -> 27.3 us  [across(): return lax.ppermute(x, axis, [(i, i ^ step) for i in range(SIZES[axis])])]
  transfers between devices with their start and end apart: 20 -> 20, of which waited for: 11 -> 10; matrix products, arithmetic and copies ran while one was open for 0% -> 0% of each run, Pallas kernels for 5% -> 3%
where the time goes in v5:
time: 86.5 us; the launch traced here: 85 us
  starting transfers between devices  35.6 us (41%)
  waiting for transfers between devices  29.1 us (34%)
  Pallas kernels  18.7 us (22%)
    ppermute x18, waiting for transfers between devices, across(): return lax.ppermute(x, axis, [(i, i ^ step) for i in range(SIZES[axis])])  27.3 us
    ppermute x18, starting transfers between devices, across(): return lax.ppermute(x, axis, [(i, i ^ step) for i in range(SIZES[axis])])  25 us
    pallas_call x1, Pallas kernels, attend(): pl.pallas_call(attend_kernel, in_specs=[pl.BlockSpec(memory_space=pltpu.S...  11.2 us
    all_to_all x1, starting transfers between devices, local(): sums = lax.all_to_all(own, ('zl', 'x'), 0, 0, tiled=True)  6.89 us
    all_to_all x1, starting transfers between devices, local(): back = lax.all_to_all(back, ('y', 'core'), 0, 0, tiled=True)  3.73 us
    pallas_call x1, Pallas kernels, widen(): pl.pallas_call(widen_kernel, grid=(4,), in_specs=[piece] * 8, out_specs=[...  2.5 us
    pallas_call x1, Pallas kernels, pack(): pl.pallas_call(pack_kernel, in_specs=[whole] * 4, out_specs=[whole] * 4,...  2.45 us
    all_to_all x1, waiting for transfers between devices, local(): sums = lax.all_to_all(own, ('zl', 'x'), 0, 0, tiled=True)  1.86 us
  transfers between devices with their start and end apart: 20, of which 10 were waited for; matrix products, arithmetic and copies ran while one was open for 0% of the time, Pallas kernels for 3%

profile of v5, /device:TPU:2, one launch (start us, length us, event | category | flops | bytes accessed | tf_op | source)
XLA Modules:
  0.0 85.0 jit_solution(14233569688379032746)
XLA Ops:
  0.6 2.4 %pack.1 = (bf16[1216,128]{1,0:T(8,128)(2,1)}, bf16[1216,128]{1,0:T(8,128)(2,1)}, bf16[1216,128]{1,0:T(8,128)(2,1)}, bf16[1216,128]{1,0:T(8,128)(2,1)}) custom-call(bf16[1,128,1024]{2,1,0:T(8,128)(2,1)} %qn_ref.1, bf16[1,128,512]{2,1,0:T(8,128)(2,1)} %qr_ref.1, bf16[1,128,1024]{2,1,0:T(8,128)(2,1)} %do_ref.1, bf16[576,128]{1,0:T(8,128)(2,1)} %bitcast.3), custom_call_target="tpu_custom_call" | custom-call | bytes 5242880 | tf_op jit(solution)/shard_map/pack/pallas_call | solution.py:50
  3.1 1.6 %collective-permute-start.1 = (bf16[1216,128]{1,0:T(8,128)(2,1)}, bf16[1216,128]{1,0:T(8,128)(2,1)S(1)}, u32[]{:S(2)}, u32[]{:S(2)}) collective-permute-start(bf16[1216,128]{1,0:T(8,128)(2,1)} %get-tuple-element.22), channel_id=1, source_target_pairs={{0,16},{16,0},{32,48},{48,32},{1,17},{17,1},{33,49},{49,33},{2,18}... | collective-permute-start | bytes 933896 | tf_op jit(solution)/shard_map/ppermute | solution.py:338
  4.7 2.9 %collective-permute-start.3 = (bf16[1216,128]{1,0:T(8,128)(2,1)}, bf16[1216,128]{1,0:T(8,128)(2,1)S(1)}, u32[]{:S(2)}, u32[]{:S(2)}) collective-permute-start(bf16[1216,128]{1,0:T(8,128)(2,1)} %get-tuple-element.23), channel_id=1, source_target_pairs={{0,32},{16,48},{32,0},{48,16},{1,33},{17,49},{33,1},{49,17},{2,34}... | collective-permute-start | bytes 933896 | tf_op jit(solution)/shard_map/ppermute | solution.py:338
  7.6 0.2 collective-permute-start.5
  7.8 5.8 %collective-permute-done.1.refs_2_ = bf16[1216,128]{1,0:T(8,128)(2,1)S(1)} collective-permute-done((bf16[1216,128]{1,0:T(8,128)(2,1)}, bf16[1216,128]{1,0:T(8,128)(2,1)S(1)}, u32[]{:S(2)}, u32[]{:S(2)}) %collective-permute-start.1) | collective-permute-done | bytes 311328 | tf_op jit(solution)/shard_map/ppermute | solution.py:338
  13.5 8.1 %collective-permute-done.3.refs_4_ = bf16[1216,128]{1,0:T(8,128)(2,1)S(1)} collective-permute-done((bf16[1216,128]{1,0:T(8,128)(2,1)}, bf16[1216,128]{1,0:T(8,128)(2,1)S(1)}, u32[]{:S(2)}, u32[]{:S(2)}) %collective-permute-start.3) | collective-permute-done | bytes 311328 | tf_op jit(solution)/shard_map/ppermute | solution.py:338
  21.6 2.6 %collective-permute-done.5.refs_6_ = bf16[1216,128]{1,0:T(8,128)(2,1)S(1)} collective-permute-done((bf16[1216,128]{1,0:T(8,128)(2,1)}, bf16[1216,128]{1,0:T(8,128)(2,1)S(1)}, u32[]{:S(2)}, u32[]{:S(2)}) %collective-permute-start.5) | collective-permute-done | bytes 311328 | tf_op jit(solution)/shard_map/ppermute | solution.py:338
  24.3 1.5 %collective-permute-done.6.refs_7_ = bf16[1216,128]{1,0:T(8,128)(2,1)S(1)} collective-permute-done((bf16[1216,128]{1,0:T(8,128)(2,1)S(1)}, bf16[1216,128]{1,0:T(8,128)(2,1)S(1)}, u32[]{:S(2)}, u32[]{:S(2)}) %collective-permute-start.6) | collective-permute-done | bytes 311328 | tf_op jit(solution)/shard_map/ppermute | solution.py:338
  25.9 0.7 copy-done.8
  26.6 11.2 %attend.1 = (bf16[8,768,128]{2,1,0:T(8,128)(2,1)}, bf16[512,128]{1,0:T(8,128)(2,1)}, bf16[512,128]{1,0:T(8,128)(2,1)}) custom-call(s32[16]{0:T(128)} %order_ref.1, bf16[1216,128]{1,0:T(8,128)(2,1)} %get-tuple-element.21.refs_0_, bf16[1216,128]{1,0:T(8,128)(2,1)} %copy-done.5, bf16[1216,128]{1,0:T(8,128)(2,1)} %copy-done.2, bf16[1216,128]{1,0:T(8,128)(2,1)} %copy-done.6, ...), custom_call_target="tpu_custom_call" | custom-call | flops 8999999488 | bytes 12582912 | tf_op jit(solution)/shard_map/attend/pallas_call | solution.py:192
  37.8 3.7 %all-to-all-start = ((bf16[8,768,128]{2,1,0:T(8,128)(2,1)}), bf16[8,768,128]{2,1,0:T(8,128)(2,1)S(1)}, u32[]{:S(2)}, u32[]{:S(2)}) async-start(bf16[8,768,128]{2,1,0:T(8,128)(2,1)} %get-tuple-element.25), calls=%async_computation | async-start | bytes 3145728 | tf_op jit(solution)/shard_map/all_to_all | solution.py:347
  41.6 3.5 %collective-permute-start.7 = (bf16[512,128]{1,0:T(8,128)(2,1)S(1)}, bf16[512,128]{1,0:T(8,128)(2,1)S(1)}, u32[]{:S(2)}, u32[]{:S(2)}) collective-permute-start(bf16[512,128]{1,0:T(8,128)(2,1)S(1)} %copy-done.1), channel_id=1, source_target_pairs={{0,64},{64,0},{128,192},{192,128},{1,65},{65,1},{129,193},{193,129... | collective-permute-start | bytes 393224 | tf_op jit(solution)/shard_map/ppermute | solution.py:338
  45.1 4.5 %collective-permute-start.9 = (bf16[512,128]{1,0:T(8,128)(2,1)S(1)}, bf16[512,128]{1,0:T(8,128)(2,1)S(1)}, u32[]{:S(2)}, u32[]{:S(2)}) collective-permute-start(bf16[512,128]{1,0:T(8,128)(2,1)S(1)} %copy-done), channel_id=1, source_target_pairs={{0,192},{64,128},{128,64},{192,0},{1,193},{65,129},{129,65},{193,1... | collective-permute-start | bytes 393224 | tf_op jit(solution)/shard_map/ppermute | solution.py:338
  49.6 2.2 %collective-permute-done.7.b_ref = bf16[512,128]{1,0:T(8,128)(2,1)S(1)} collective-permute-done((bf16[512,128]{1,0:T(8,128)(2,1)S(1)}, bf16[512,128]{1,0:T(8,128)(2,1)S(1)}, u32[]{:S(2)}, u32[]{:S(2)}) %collective-permute-start.7) | collective-permute-done | bytes 131104 | tf_op jit(solution)/shard_map/ppermute | solution.py:338
  51.8 3.7 %collective-permute-start.8 = (bf16[512,128]{1,0:T(8,128)(2,1)S(1)}, bf16[512,128]{1,0:T(8,128)(2,1)S(1)}, u32[]{:S(2)}, u32[]{:S(2)}) collective-permute-start(bf16[512,128]{1,0:T(8,128)(2,1)S(1)} %add_uk.1.a_ref), channel_id=1, source_target_pairs={{0,192},{64,128},{128,64},{192,0},{1,193},{65,129},{129,65},{193,1... | collective-permute-start | bytes 393224 | tf_op jit(solution)/shard_map/ppermute | solution.py:338
  55.6 3.5 %collective-permute-start.10 = (bf16[512,128]{1,0:T(8,128)(2,1)S(1)}, bf16[512,128]{1,0:T(8,128)(2,1)S(1)}, u32[]{:S(2)}, u32[]{:S(2)}) collective-permute-start(bf16[512,128]{1,0:T(8,128)(2,1)S(1)} %add_uv.1.c_ref), channel_id=1, source_target_pairs={{0,64},{64,0},{128,192},{192,128},{1,65},{65,1},{129,193},{193,129... | collective-permute-start | bytes 393224 | tf_op jit(solution)/shard_map/ppermute | solution.py:338
  59.1 0.2 collective-permute-done.8.b_ref
  59.3 4.5 %collective-permute-done.10.d_ref = bf16[512,128]{1,0:T(8,128)(2,1)S(1)} collective-permute-done((bf16[512,128]{1,0:T(8,128)(2,1)S(1)}, bf16[512,128]{1,0:T(8,128)(2,1)S(1)}, u32[]{:S(2)}, u32[]{:S(2)}) %collective-permute-start.10) | collective-permute-done | bytes 131104 | tf_op jit(solution)/shard_map/ppermute | solution.py:338
  63.8 0.1 add_join.1.refs_0_
  63.8 3.0 %collective-permute-start.11 = (bf16[1024,128]{1,0:T(8,128)(2,1)S(1)}, bf16[1024,128]{1,0:T(8,128)(2,1)S(1)}, u32[]{:S(2)}, u32[]{:S(2)}) collective-permute-start(bf16[1024,128]{1,0:T(8,128)(2,1)S(1)} %add_join.1.refs_0_), channel_id=1, source_target_pairs={{0,48},{16,32},{32,16},{48,0},{1,49},{17,33},{33,17},{49,1},{2,50}... | collective-permute-start | bytes 786440 | tf_op jit(solution)/shard_map/ppermute | solution.py:338
  66.8 0.8 collective-permute-start.16
  67.7 0.4 collective-permute-start.14
  68.0 0.9 %sum_ctx.1 = bf16[8,16,640]{2,1,0:T(8,128)(2,1)} custom-call(bf16[8,768,128]{2,1,0:T(8,128)(2,1)S(1)} %all-to-all-done.x_ref), custom_call_target="tpu_custom_call" | custom-call | tf_op jit(solution)/shard_map/sum_ctx/pallas_call | solution.py:262
  69.0 0.9 %unpack.1 = (bf16[1,128,1024]{2,1,0:T(8,128)(2,1)}, bf16[1,128,512]{2,1,0:T(8,128)(2,1)}) custom-call(bf16[8,768,128]{2,1,0:T(8,128)(2,1)S(1)} %all-to-all-done.x_ref), custom_call_target="tpu_custom_call" | custom-call | tf_op jit(solution)/shard_map/unpack/pallas_call | solution.py:288
  69.8 6.9 %all-to-all-start.1 = ((bf16[8,16,640]{2,1,0:T(8,128)(2,1)}), bf16[8,16,640]{2,1,0:T(8,128)(2,1)S(1)}, u32[]{:S(2)}, u32[]{:S(2)}) async-start(bf16[8,16,640]{2,1,0:T(8,128)(2,1)} %sum_ctx.1), calls=%async_computation.1 | async-start | bytes 327680 | tf_op jit(solution)/shard_map/all_to_all | solution.py:350
  76.7 2.3 %collective-permute-done.11.refs_6_ = bf16[1024,128]{1,0:T(8,128)(2,1)S(1)} collective-permute-done((bf16[1024,128]{1,0:T(8,128)(2,1)S(1)}, bf16[1024,128]{1,0:T(8,128)(2,1)S(1)}, u32[]{:S(2)}, u32[]{:S(2)}) %collective-permute-start.11) | collective-permute-done | bytes 262176 | tf_op jit(solution)/shard_map/ppermute | solution.py:338
  79.0 0.5 collective-permute-start.13
  79.5 0.2 collective-permute-done.14.refs_2_
  79.7 0.4 collective-permute-start.15
  80.0 1.9 %all-to-all-done.1.x_ref = bf16[8,16,640]{2,1,0:T(8,128)(2,1)S(1)} async-done(((bf16[8,16,640]{2,1,0:T(8,128)(2,1)}), bf16[8,16,640]{2,1,0:T(8,128)(2,1)S(1)}, u32[]{:S(2)}, u32[]{:S(2)}) %all-to-all-start.1) | async-done | bytes 163872 | tf_op jit(solution)/shard_map/all_to_all | solution.py:350
  81.9 0.6 sum_head.1
  82.5 2.5 %widen.1 = (f32[512,1024]{1,0:T(8,128)}, f32[512,1024]{1,0:T(8,128)}) custom-call(bf16[1024,128]{1,0:T(8,128)(2,1)S(1)} %add_join.1.refs_0_, bf16[1024,128]{1,0:T(8,128)(2,1)S(1)} %collective-permute-done.13.refs_1_, bf16[1024,128]{1,0:T(8,128)(2,1)S(1)} %collective-permute-done.14.refs_2_, bf16[1024,128]{1,0:T(8,128)(2,1)S(1)} %collective-permute-done.15.refs_3_, ...), custom_call_target="tpu_custom_call" | custom-call | tf_op jit(solution)/shard_map/widen/pallas_call | solution.py:323
  (35 shorter events, 0.1 us)
Async XLA Ops:
  3.1 10.5 %collective-permute-start.1 = (bf16[1216,128]{1,0:T(8,128)(2,1)}, bf16[1216,128]{1,0:T(8,128)(2,1)S(1)}, u32[]{:S(2)}, u32[]{:S(2)}) collective-permute-start(bf16[1216,128]{1,0:T(8,128)(2,1)} %get-tuple-element.22), channel_id=1, source_target_pairs={{0,16},{16,0},{32,48},{48,32},{1,17},{17,1},{33,49},{49,33},{2,18}... | collective-permute-start | bytes 933896 | tf_op jit(solution)/shard_map/ppermute | solution.py:338
  4.7 17.0 %collective-permute-start.3 = (bf16[1216,128]{1,0:T(8,128)(2,1)}, bf16[1216,128]{1,0:T(8,128)(2,1)S(1)}, u32[]{:S(2)}, u32[]{:S(2)}) collective-permute-start(bf16[1216,128]{1,0:T(8,128)(2,1)} %get-tuple-element.23), channel_id=1, source_target_pairs={{0,32},{16,48},{32,0},{48,16},{1,33},{17,49},{33,1},{49,17},{2,34}... | collective-permute-start | bytes 933896 | tf_op jit(solution)/shard_map/ppermute | solution.py:338
  7.6 16.6 %collective-permute-start.5 = (bf16[1216,128]{1,0:T(8,128)(2,1)}, bf16[1216,128]{1,0:T(8,128)(2,1)S(1)}, u32[]{:S(2)}, u32[]{:S(2)}) collective-permute-start(bf16[1216,128]{1,0:T(8,128)(2,1)} %get-tuple-element.24), channel_id=1, source_target_pairs={{0,48},{16,32},{32,16},{48,0},{1,49},{17,33},{33,17},{49,1},{2,50}... | collective-permute-start | bytes 933896 | tf_op jit(solution)/shard_map/ppermute | solution.py:338
  7.8 16.4 %collective-permute-start = (bf16[1216,128]{1,0:T(8,128)(2,1)}, bf16[1216,128]{1,0:T(8,128)(2,1)S(1)}, u32[]{:S(2)}, u32[]{:S(2)}) collective-permute-start(bf16[1216,128]{1,0:T(8,128)(2,1)} %get-tuple-element.21.refs_0_), channel_id=1, source_target_pairs={{0,8},{8,0},{1,9},{9,1},{2,10},{10,2},{3,11},{11,3},{4,12},{12,4},... | collective-permute-start | bytes 933896 | tf_op jit(solution)/shard_map/ppermute | solution.py:338
  13.5 12.3 %copy-start.2 = (bf16[1216,128]{1,0:T(8,128)(2,1)}, bf16[1216,128]{1,0:T(8,128)(2,1)S(1)}, u32[]{:S(2)}) copy-start(bf16[1216,128]{1,0:T(8,128)(2,1)S(1)} %collective-permute-done.1.refs_2_) | copy-start | bytes 933892
  13.5 10.7 %collective-permute-start.2 = (bf16[1216,128]{1,0:T(8,128)(2,1)S(1)}, bf16[1216,128]{1,0:T(8,128)(2,1)S(1)}, u32[]{:S(2)}, u32[]{:S(2)}) collective-permute-start(bf16[1216,128]{1,0:T(8,128)(2,1)S(1)} %collective-permute-done.1.refs_2_), channel_id=1, source_target_pairs={{0,8},{8,0},{1,9},{9,1},{2,10},{10,2},{3,11},{11,3},{4,12},{12,4},... | collective-permute-start | bytes 933896 | tf_op jit(solution)/shard_map/ppermute | solution.py:338
  21.6 4.2 %copy-start.3 = (bf16[1216,128]{1,0:T(8,128)(2,1)}, bf16[1216,128]{1,0:T(8,128)(2,1)S(1)}, u32[]{:S(2)}) copy-start(bf16[1216,128]{1,0:T(8,128)(2,1)S(1)} %collective-permute-done.3.refs_4_) | copy-start | bytes 933892
  21.6 2.6 %collective-permute-start.4 = (bf16[1216,128]{1,0:T(8,128)(2,1)S(1)}, bf16[1216,128]{1,0:T(8,128)(2,1)S(1)}, u32[]{:S(2)}, u32[]{:S(2)}) collective-permute-start(bf16[1216,128]{1,0:T(8,128)(2,1)S(1)} %collective-permute-done.3.refs_4_), channel_id=1, source_target_pairs={{0,8},{8,0},{1,9},{9,1},{2,10},{10,2},{3,11},{11,3},{4,12},{12,4},... | collective-permute-start | bytes 933896 | tf_op jit(solution)/shard_map/ppermute | solution.py:338
  24.2 1.6 %copy-start.4 = (bf16[1216,128]{1,0:T(8,128)(2,1)}, bf16[1216,128]{1,0:T(8,128)(2,1)S(1)}, u32[]{:S(2)}) copy-start(bf16[1216,128]{1,0:T(8,128)(2,1)S(1)} %collective-permute-done.5.refs_6_) | copy-start | bytes 933892
  24.2 1.6 %collective-permute-start.6 = (bf16[1216,128]{1,0:T(8,128)(2,1)S(1)}, bf16[1216,128]{1,0:T(8,128)(2,1)S(1)}, u32[]{:S(2)}, u32[]{:S(2)}) collective-permute-start(bf16[1216,128]{1,0:T(8,128)(2,1)S(1)} %collective-permute-done.5.refs_6_), channel_id=1, source_target_pairs={{0,8},{8,0},{1,9},{9,1},{2,10},{10,2},{3,11},{11,3},{4,12},{12,4},... | collective-permute-start | bytes 933896 | tf_op jit(solution)/shard_map/ppermute | solution.py:338
  24.2 1.6 %copy-start.5 = (bf16[1216,128]{1,0:T(8,128)(2,1)}, bf16[1216,128]{1,0:T(8,128)(2,1)S(1)}, u32[]{:S(2)}) copy-start(bf16[1216,128]{1,0:T(8,128)(2,1)S(1)} %collective-permute-done.refs_1_) | copy-start | bytes 933892
  24.2 1.6 %copy-start.6 = (bf16[1216,128]{1,0:T(8,128)(2,1)}, bf16[1216,128]{1,0:T(8,128)(2,1)S(1)}, u32[]{:S(2)}) copy-start(bf16[1216,128]{1,0:T(8,128)(2,1)S(1)} %collective-permute-done.2.refs_3_) | copy-start | bytes 933892
  24.2 1.6 %copy-start.7 = (bf16[1216,128]{1,0:T(8,128)(2,1)}, bf16[1216,128]{1,0:T(8,128)(2,1)S(1)}, u32[]{:S(2)}) copy-start(bf16[1216,128]{1,0:T(8,128)(2,1)S(1)} %collective-permute-done.4.refs_5_) | copy-start | bytes 933892
  25.8 0.7 copy-start.8
  37.8 3.8 %copy-start.1 = (bf16[512,128]{1,0:T(8,128)(2,1)S(1)}, bf16[512,128]{1,0:T(8,128)(2,1)}, u32[]{:S(2)}) copy-start(bf16[512,128]{1,0:T(8,128)(2,1)} %get-tuple-element.30.a_ref) | copy-start | bytes 393220
  37.8 7.3 %copy-start = (bf16[512,128]{1,0:T(8,128)(2,1)S(1)}, bf16[512,128]{1,0:T(8,128)(2,1)}, u32[]{:S(2)}) copy-start(bf16[512,128]{1,0:T(8,128)(2,1)} %get-tuple-element.31.a_ref) | copy-start | bytes 393220
  37.8 30.2 %all-to-all-start = ((bf16[8,768,128]{2,1,0:T(8,128)(2,1)}), bf16[8,768,128]{2,1,0:T(8,128)(2,1)S(1)}, u32[]{:S(2)}, u32[]{:S(2)}) async-start(bf16[8,768,128]{2,1,0:T(8,128)(2,1)} %get-tuple-element.25), calls=%async_computation | async-start | bytes 3145728 | tf_op jit(solution)/shard_map/all_to_all | solution.py:347
  41.6 10.2 %collective-permute-start.7 = (bf16[512,128]{1,0:T(8,128)(2,1)S(1)}, bf16[512,128]{1,0:T(8,128)(2,1)S(1)}, u32[]{:S(2)}, u32[]{:S(2)}) collective-permute-start(bf16[512,128]{1,0:T(8,128)(2,1)S(1)} %copy-done.1), channel_id=1, source_target_pairs={{0,64},{64,0},{128,192},{192,128},{1,65},{65,1},{129,193},{193,129... | collective-permute-start | bytes 393224 | tf_op jit(solution)/shard_map/ppermute | solution.py:338
  45.1 10.5 %collective-permute-start.9 = (bf16[512,128]{1,0:T(8,128)(2,1)S(1)}, bf16[512,128]{1,0:T(8,128)(2,1)S(1)}, u32[]{:S(2)}, u32[]{:S(2)}) collective-permute-start(bf16[512,128]{1,0:T(8,128)(2,1)S(1)} %copy-done), channel_id=1, source_target_pairs={{0,192},{64,128},{128,64},{192,0},{1,193},{65,129},{129,65},{193,1... | collective-permute-start | bytes 393224 | tf_op jit(solution)/shard_map/ppermute | solution.py:338
  51.8 7.5 %collective-permute-start.8 = (bf16[512,128]{1,0:T(8,128)(2,1)S(1)}, bf16[512,128]{1,0:T(8,128)(2,1)S(1)}, u32[]{:S(2)}, u32[]{:S(2)}) collective-permute-start(bf16[512,128]{1,0:T(8,128)(2,1)S(1)} %add_uk.1.a_ref), channel_id=1, source_target_pairs={{0,192},{64,128},{128,64},{192,0},{1,193},{65,129},{129,65},{193,1... | collective-permute-start | bytes 393224 | tf_op jit(solution)/shard_map/ppermute | solution.py:338
  55.6 8.2 %collective-permute-start.10 = (bf16[512,128]{1,0:T(8,128)(2,1)S(1)}, bf16[512,128]{1,0:T(8,128)(2,1)S(1)}, u32[]{:S(2)}, u32[]{:S(2)}) collective-permute-start(bf16[512,128]{1,0:T(8,128)(2,1)S(1)} %add_uv.1.c_ref), channel_id=1, source_target_pairs={{0,64},{64,0},{128,192},{192,128},{1,65},{65,1},{129,193},{193,129... | collective-permute-start | bytes 393224 | tf_op jit(solution)/shard_map/ppermute | solution.py:338
  63.8 15.1 %collective-permute-start.11 = (bf16[1024,128]{1,0:T(8,128)(2,1)S(1)}, bf16[1024,128]{1,0:T(8,128)(2,1)S(1)}, u32[]{:S(2)}, u32[]{:S(2)}) collective-permute-start(bf16[1024,128]{1,0:T(8,128)(2,1)S(1)} %add_join.1.refs_0_), channel_id=1, source_target_pairs={{0,48},{16,32},{32,16},{48,0},{1,49},{17,33},{33,17},{49,1},{2,50}... | collective-permute-start | bytes 786440 | tf_op jit(solution)/shard_map/ppermute | solution.py:338
  66.8 12.7 %collective-permute-start.16 = (bf16[1024,128]{1,0:T(8,128)(2,1)S(1)}, bf16[1024,128]{1,0:T(8,128)(2,1)S(1)}, u32[]{:S(2)}, u32[]{:S(2)}) collective-permute-start(bf16[1024,128]{1,0:T(8,128)(2,1)S(1)} %add_join.1.refs_0_), channel_id=1, source_target_pairs={{0,32},{16,48},{32,0},{48,16},{1,33},{17,49},{33,1},{49,17},{2,34}... | collective-permute-start | bytes 786440 | tf_op jit(solution)/shard_map/ppermute | solution.py:338
  67.7 12.0 %collective-permute-start.14 = (bf16[1024,128]{1,0:T(8,128)(2,1)S(1)}, bf16[1024,128]{1,0:T(8,128)(2,1)S(1)}, u32[]{:S(2)}, u32[]{:S(2)}) collective-permute-start(bf16[1024,128]{1,0:T(8,128)(2,1)S(1)} %add_join.1.refs_0_), channel_id=1, source_target_pairs={{0,16},{16,0},{32,48},{48,32},{1,17},{17,1},{33,49},{49,33},{2,18}... | collective-permute-start | bytes 786440 | tf_op jit(solution)/shard_map/ppermute | solution.py:338
  69.8 12.0 %all-to-all-start.1 = ((bf16[8,16,640]{2,1,0:T(8,128)(2,1)}), bf16[8,16,640]{2,1,0:T(8,128)(2,1)S(1)}, u32[]{:S(2)}, u32[]{:S(2)}) async-start(bf16[8,16,640]{2,1,0:T(8,128)(2,1)} %sum_ctx.1), calls=%async_computation.1 | async-start | bytes 327680 | tf_op jit(solution)/shard_map/all_to_all | solution.py:350
  79.0 3.5 %collective-permute-start.12 = (bf16[1024,128]{1,0:T(8,128)(2,1)S(1)}, bf16[1024,128]{1,0:T(8,128)(2,1)S(1)}, u32[]{:S(2)}, u32[]{:S(2)}) collective-permute-start(bf16[1024,128]{1,0:T(8,128)(2,1)S(1)} %collective-permute-done.11.refs_6_), channel_id=1, source_target_pairs={{0,8},{8,0},{1,9},{9,1},{2,10},{10,2},{3,11},{11,3},{4,12},{12,4},... | collective-permute-start | bytes 786440 | tf_op jit(solution)/shard_map/ppermute | solution.py:338
  79.0 3.5 %collective-permute-start.13 = (bf16[1024,128]{1,0:T(8,128)(2,1)S(1)}, bf16[1024,128]{1,0:T(8,128)(2,1)S(1)}, u32[]{:S(2)}, u32[]{:S(2)}) collective-permute-start(bf16[1024,128]{1,0:T(8,128)(2,1)S(1)} %add_join.1.refs_0_), channel_id=1, source_target_pairs={{0,8},{8,0},{1,9},{9,1},{2,10},{10,2},{3,11},{11,3},{4,12},{12,4},... | collective-permute-start | bytes 786440 | tf_op jit(solution)/shard_map/ppermute | solution.py:338
  79.5 3.0 %collective-permute-start.17 = (bf16[1024,128]{1,0:T(8,128)(2,1)S(1)}, bf16[1024,128]{1,0:T(8,128)(2,1)S(1)}, u32[]{:S(2)}, u32[]{:S(2)}) collective-permute-start(bf16[1024,128]{1,0:T(8,128)(2,1)S(1)} %collective-permute-done.16.refs_4_), channel_id=1, source_target_pairs={{0,8},{8,0},{1,9},{9,1},{2,10},{10,2},{3,11},{11,3},{4,12},{12,4},... | collective-permute-start | bytes 786440 | tf_op jit(solution)/shard_map/ppermute | solution.py:338
  79.7 2.9 %collective-permute-start.15 = (bf16[1024,128]{1,0:T(8,128)(2,1)S(1)}, bf16[1024,128]{1,0:T(8,128)(2,1)S(1)}, u32[]{:S(2)}, u32[]{:S(2)}) collective-permute-start(bf16[1024,128]{1,0:T(8,128)(2,1)S(1)} %collective-permute-done.14.refs_2_), channel_id=1, source_target_pairs={{0,8},{8,0},{1,9},{9,1},{2,10},{10,2},{3,11},{11,3},{4,12},{12,4},... | collective-permute-start | bytes 786440 | tf_op jit(solution)/shard_map/ppermute | solution.py:338

commit v6 on v5

--- a/solution.py
+++ b/solution.py
@@ -145,9 +145,11 @@
     flight = products(0)
     for b in range(4):
         following = products(b + 1) if b < 3 else None
+        if b > 0:
+            outputs(b - 1)
         softmax(b, *flight)
-        outputs(b)
         flight = following
+    outputs(3)
     duk_ref[...] = dot(dqt[...], qn[...], NN).astype(BF16)
     duv_ref[...] = dot(ot[...], g[...], NN).astype(BF16)
     dqn = dot(dqt[...], uk, TN).astype(BF16)
@@ -357,7 +359,6 @@
     pieces = []
     for piece in [whole] + [across(whole, "y", d) for d in (1, 2, 3)]:
         pieces += [piece, across(piece, "core", 1)]
-    pieces[-1], d_kv = lax.optimization_barrier((pieces[-1], d_kv))
     dw_uk, dw_uv = widen(pieces)
     return dq_nope, dq_rope, d_kv, dw_uk, dw_uv
 

time: 86.5 us -> 85.7 us (level)
    all_to_all x1, waiting for transfers between devices: 1.86 us -> 0.01 us  [local(): sums = lax.all_to_all(own, ('zl', 'x'), 0, 0, tiled=True)]
    ppermute x18, waiting for transfers between devices: 27.3 us -> 29 us  [across(): return lax.ppermute(x, axis, [(i, i ^ step) for i in range(SIZES[axis])])]
  transfers between devices with their start and end apart: 20 -> 20, of which waited for: 10 -> 12; matrix products, arithmetic and copies ran while one was open for 0% -> 0% of each run, Pallas kernels for 3% -> 5%
where the time goes in v6:
time: 85.7 us; the launch traced here: 84.3 us
  starting transfers between devices  35.1 us (41%)
  waiting for transfers between devices  29 us (34%)
  Pallas kernels  18.6 us (22%)
    ppermute x18, waiting for transfers between devices, across(): return lax.ppermute(x, axis, [(i, i ^ step) for i in range(SIZES[axis])])  29 us
    ppermute x18, starting transfers between devices, across(): return lax.ppermute(x, axis, [(i, i ^ step) for i in range(SIZES[axis])])  24.5 us
    pallas_call x1, Pallas kernels, attend(): pl.pallas_call(attend_kernel, in_specs=[pl.BlockSpec(memory_space=pltpu.S...  11.1 us
    all_to_all x1, starting transfers between devices, local(): sums = lax.all_to_all(own, ('zl', 'x'), 0, 0, tiled=True)  6.92 us
    all_to_all x1, starting transfers between devices, local(): back = lax.all_to_all(back, ('y', 'core'), 0, 0, tiled=True)  3.73 us
    pallas_call x1, Pallas kernels, widen(): pl.pallas_call(widen_kernel, grid=(4,), in_specs=[piece] * 8, out_specs=[...  2.46 us
    pallas_call x1, Pallas kernels, pack(): pl.pallas_call(pack_kernel, in_specs=[whole] * 4, out_specs=[whole] * 4,...  2.45 us
  transfers between devices with their start and end apart: 20, of which 12 were waited for; matrix products, arithmetic and copies ran while one was open for 0% of the time, Pallas kernels for 5%

profile of v6, /device:TPU:2, one launch (start us, length us, event | category | flops | bytes accessed | tf_op | source)
XLA Modules:
  0.0 84.3 jit_solution(135364698002995282)
XLA Ops:
  0.6 2.4 %pack.1 = (bf16[1216,128]{1,0:T(8,128)(2,1)}, bf16[1216,128]{1,0:T(8,128)(2,1)}, bf16[1216,128]{1,0:T(8,128)(2,1)}, bf16[1216,128]{1,0:T(8,128)(2,1)}) custom-call(bf16[1,128,1024]{2,1,0:T(8,128)(2,1)} %qn_ref.1, bf16[1,128,512]{2,1,0:T(8,128)(2,1)} %qr_ref.1, bf16[1,128,1024]{2,1,0:T(8,128)(2,1)} %do_ref.1, bf16[576,128]{1,0:T(8,128)(2,1)} %bitcast.3), custom_call_target="tpu_custom_call" | custom-call | bytes 5242880 | tf_op jit(solution)/shard_map/pack/pallas_call | solution.py:50
  3.1 1.6 %collective-permute-start.1 = (bf16[1216,128]{1,0:T(8,128)(2,1)}, bf16[1216,128]{1,0:T(8,128)(2,1)S(1)}, u32[]{:S(2)}, u32[]{:S(2)}) collective-permute-start(bf16[1216,128]{1,0:T(8,128)(2,1)} %get-tuple-element.20), channel_id=1, source_target_pairs={{0,16},{16,0},{32,48},{48,32},{1,17},{17,1},{33,49},{49,33},{2,18}... | collective-permute-start | bytes 933896 | tf_op jit(solution)/shard_map/ppermute | solution.py:340
  4.7 2.9 %collective-permute-start.3 = (bf16[1216,128]{1,0:T(8,128)(2,1)}, bf16[1216,128]{1,0:T(8,128)(2,1)S(1)}, u32[]{:S(2)}, u32[]{:S(2)}) collective-permute-start(bf16[1216,128]{1,0:T(8,128)(2,1)} %get-tuple-element.21), channel_id=1, source_target_pairs={{0,32},{16,48},{32,0},{48,16},{1,33},{17,49},{33,1},{49,17},{2,34}... | collective-permute-start | bytes 933896 | tf_op jit(solution)/shard_map/ppermute | solution.py:340
  7.6 0.2 collective-permute-start.5
  7.8 5.8 %collective-permute-done.1.refs_2_ = bf16[1216,128]{1,0:T(8,128)(2,1)S(1)} collective-permute-done((bf16[1216,128]{1,0:T(8,128)(2,1)}, bf16[1216,128]{1,0:T(8,128)(2,1)S(1)}, u32[]{:S(2)}, u32[]{:S(2)}) %collective-permute-start.1) | collective-permute-done | bytes 311328 | tf_op jit(solution)/shard_map/ppermute | solution.py:340
  13.5 8.1 %collective-permute-done.3.refs_4_ = bf16[1216,128]{1,0:T(8,128)(2,1)S(1)} collective-permute-done((bf16[1216,128]{1,0:T(8,128)(2,1)}, bf16[1216,128]{1,0:T(8,128)(2,1)S(1)}, u32[]{:S(2)}, u32[]{:S(2)}) %collective-permute-start.3) | collective-permute-done | bytes 311328 | tf_op jit(solution)/shard_map/ppermute | solution.py:340
  21.6 2.6 %collective-permute-done.5.refs_6_ = bf16[1216,128]{1,0:T(8,128)(2,1)S(1)} collective-permute-done((bf16[1216,128]{1,0:T(8,128)(2,1)}, bf16[1216,128]{1,0:T(8,128)(2,1)S(1)}, u32[]{:S(2)}, u32[]{:S(2)}) %collective-permute-start.5) | collective-permute-done | bytes 311328 | tf_op jit(solution)/shard_map/ppermute | solution.py:340
  24.3 1.5 %collective-permute-done.6.refs_7_ = bf16[1216,128]{1,0:T(8,128)(2,1)S(1)} collective-permute-done((bf16[1216,128]{1,0:T(8,128)(2,1)S(1)}, bf16[1216,128]{1,0:T(8,128)(2,1)S(1)}, u32[]{:S(2)}, u32[]{:S(2)}) %collective-permute-start.6) | collective-permute-done | bytes 311328 | tf_op jit(solution)/shard_map/ppermute | solution.py:340
  25.9 0.7 copy-done.8
  26.6 11.1 %attend.1 = (bf16[8,768,128]{2,1,0:T(8,128)(2,1)}, bf16[512,128]{1,0:T(8,128)(2,1)}, bf16[512,128]{1,0:T(8,128)(2,1)}) custom-call(s32[16]{0:T(128)} %order_ref.1, bf16[1216,128]{1,0:T(8,128)(2,1)} %get-tuple-element.19.refs_0_, bf16[1216,128]{1,0:T(8,128)(2,1)} %copy-done.5, bf16[1216,128]{1,0:T(8,128)(2,1)} %copy-done.2, bf16[1216,128]{1,0:T(8,128)(2,1)} %copy-done.6, ...), custom_call_target="tpu_custom_call" | custom-call | flops 8999999488 | bytes 12582912 | tf_op jit(solution)/shard_map/attend/pallas_call | solution.py:194
  37.7 3.7 %all-to-all-start = ((bf16[8,768,128]{2,1,0:T(8,128)(2,1)}), bf16[8,768,128]{2,1,0:T(8,128)(2,1)S(1)}, u32[]{:S(2)}, u32[]{:S(2)}) async-start(bf16[8,768,128]{2,1,0:T(8,128)(2,1)} %get-tuple-element.23), calls=%async_computation | async-start | bytes 3145728 | tf_op jit(solution)/shard_map/all_to_all | solution.py:349
  41.5 3.4 %collective-permute-start.7 = (bf16[512,128]{1,0:T(8,128)(2,1)S(1)}, bf16[512,128]{1,0:T(8,128)(2,1)S(1)}, u32[]{:S(2)}, u32[]{:S(2)}) collective-permute-start(bf16[512,128]{1,0:T(8,128)(2,1)S(1)} %copy-done.1), channel_id=1, source_target_pairs={{0,64},{64,0},{128,192},{192,128},{1,65},{65,1},{129,193},{193,129... | collective-permute-start | bytes 393224 | tf_op jit(solution)/shard_map/ppermute | solution.py:340
  44.8 4.5 %collective-permute-start.9 = (bf16[512,128]{1,0:T(8,128)(2,1)S(1)}, bf16[512,128]{1,0:T(8,128)(2,1)S(1)}, u32[]{:S(2)}, u32[]{:S(2)}) collective-permute-start(bf16[512,128]{1,0:T(8,128)(2,1)S(1)} %copy-done), channel_id=1, source_target_pairs={{0,192},{64,128},{128,64},{192,0},{1,193},{65,129},{129,65},{193,1... | collective-permute-start | bytes 393224 | tf_op jit(solution)/shard_map/ppermute | solution.py:340
  49.3 2.4 %collective-permute-done.7.b_ref = bf16[512,128]{1,0:T(8,128)(2,1)S(1)} collective-permute-done((bf16[512,128]{1,0:T(8,128)(2,1)S(1)}, bf16[512,128]{1,0:T(8,128)(2,1)S(1)}, u32[]{:S(2)}, u32[]{:S(2)}) %collective-permute-start.7) | collective-permute-done | bytes 131104 | tf_op jit(solution)/shard_map/ppermute | solution.py:340
  51.7 3.8 %collective-permute-start.8 = (bf16[512,128]{1,0:T(8,128)(2,1)S(1)}, bf16[512,128]{1,0:T(8,128)(2,1)S(1)}, u32[]{:S(2)}, u32[]{:S(2)}) collective-permute-start(bf16[512,128]{1,0:T(8,128)(2,1)S(1)} %add_uk.1.a_ref), channel_id=1, source_target_pairs={{0,192},{64,128},{128,64},{192,0},{1,193},{65,129},{129,65},{193,1... | collective-permute-start | bytes 393224 | tf_op jit(solution)/shard_map/ppermute | solution.py:340
  55.5 3.5 %collective-permute-start.10 = (bf16[512,128]{1,0:T(8,128)(2,1)S(1)}, bf16[512,128]{1,0:T(8,128)(2,1)S(1)}, u32[]{:S(2)}, u32[]{:S(2)}) collective-permute-start(bf16[512,128]{1,0:T(8,128)(2,1)S(1)} %add_uv.1.c_ref), channel_id=1, source_target_pairs={{0,64},{64,0},{128,192},{192,128},{1,65},{65,1},{129,193},{193,129... | collective-permute-start | bytes 393224 | tf_op jit(solution)/shard_map/ppermute | solution.py:340
  59.0 0.2 collective-permute-done.8.b_ref
  59.2 4.5 %collective-permute-done.10.d_ref = bf16[512,128]{1,0:T(8,128)(2,1)S(1)} collective-permute-done((bf16[512,128]{1,0:T(8,128)(2,1)S(1)}, bf16[512,128]{1,0:T(8,128)(2,1)S(1)}, u32[]{:S(2)}, u32[]{:S(2)}) %collective-permute-start.10) | collective-permute-done | bytes 131104 | tf_op jit(solution)/shard_map/ppermute | solution.py:340
  63.7 3.0 %collective-permute-start.16 = (bf16[1024,128]{1,0:T(8,128)(2,1)S(1)}, bf16[1024,128]{1,0:T(8,128)(2,1)S(1)}, u32[]{:S(2)}, u32[]{:S(2)}) collective-permute-start(bf16[1024,128]{1,0:T(8,128)(2,1)S(1)} %add_join.1.refs_0_), channel_id=1, source_target_pairs={{0,48},{16,32},{32,16},{48,0},{1,49},{17,33},{33,17},{49,1},{2,50}... | collective-permute-start | bytes 786440 | tf_op jit(solution)/shard_map/ppermute | solution.py:340
  66.7 0.8 collective-permute-start.14
  67.6 0.4 collective-permute-start.12
  67.9 0.9 %sum_ctx.1 = bf16[8,16,640]{2,1,0:T(8,128)(2,1)} custom-call(bf16[8,768,128]{2,1,0:T(8,128)(2,1)S(1)} %all-to-all-done.x_ref), custom_call_target="tpu_custom_call" | custom-call | tf_op jit(solution)/shard_map/sum_ctx/pallas_call | solution.py:264
  68.8 0.9 %unpack.1 = (bf16[1,128,1024]{2,1,0:T(8,128)(2,1)}, bf16[1,128,512]{2,1,0:T(8,128)(2,1)}) custom-call(bf16[8,768,128]{2,1,0:T(8,128)(2,1)S(1)} %all-to-all-done.x_ref), custom_call_target="tpu_custom_call" | custom-call | tf_op jit(solution)/shard_map/unpack/pallas_call | solution.py:290
  69.7 6.9 %all-to-all-start.1 = ((bf16[8,16,640]{2,1,0:T(8,128)(2,1)}), bf16[8,16,640]{2,1,0:T(8,128)(2,1)S(1)}, u32[]{:S(2)}, u32[]{:S(2)}) async-start(bf16[8,16,640]{2,1,0:T(8,128)(2,1)} %sum_ctx.1), calls=%async_computation.1 | async-start | bytes 327680 | tf_op jit(solution)/shard_map/all_to_all | solution.py:352
  76.6 2.2 %collective-permute-done.16.refs_6_ = bf16[1024,128]{1,0:T(8,128)(2,1)S(1)} collective-permute-done((bf16[1024,128]{1,0:T(8,128)(2,1)S(1)}, bf16[1024,128]{1,0:T(8,128)(2,1)S(1)}, u32[]{:S(2)}, u32[]{:S(2)}) %collective-permute-start.16) | collective-permute-done | bytes 262176 | tf_op jit(solution)/shard_map/ppermute | solution.py:340
  78.9 0.5 collective-permute-start.15
  79.4 0.2 collective-permute-done.12.refs_2_
  79.6 0.9 %collective-permute-done.17.refs_7_ = bf16[1024,128]{1,0:T(8,128)(2,1)S(1)} collective-permute-done((bf16[1024,128]{1,0:T(8,128)(2,1)S(1)}, bf16[1024,128]{1,0:T(8,128)(2,1)S(1)}, u32[]{:S(2)}, u32[]{:S(2)}) %collective-permute-start.17) | collective-permute-done | bytes 262176 | tf_op jit(solution)/shard_map/ppermute | solution.py:340
  80.4 0.4 collective-permute-done.15.refs_5_
  80.8 0.4 collective-permute-done.13.refs_3_
  81.2 2.5 %widen.1 = (f32[512,1024]{1,0:T(8,128)}, f32[512,1024]{1,0:T(8,128)}) custom-call(bf16[1024,128]{1,0:T(8,128)(2,1)S(1)} %add_join.1.refs_0_, bf16[1024,128]{1,0:T(8,128)(2,1)S(1)} %collective-permute-done.11.refs_1_, bf16[1024,128]{1,0:T(8,128)(2,1)S(1)} %collective-permute-done.12.refs_2_, bf16[1024,128]{1,0:T(8,128)(2,1)S(1)} %collective-permute-done.13.refs_3_, ...), custom_call_target="tpu_custom_call" | custom-call | tf_op jit(solution)/shard_map/widen/pallas_call | solution.py:325
  83.6 0.6 sum_head.1
  (35 shorter events, 0.2 us)
Async XLA Ops:
  3.1 10.5 %collective-permute-start.1 = (bf16[1216,128]{1,0:T(8,128)(2,1)}, bf16[1216,128]{1,0:T(8,128)(2,1)S(1)}, u32[]{:S(2)}, u32[]{:S(2)}) collective-permute-start(bf16[1216,128]{1,0:T(8,128)(2,1)} %get-tuple-element.20), channel_id=1, source_target_pairs={{0,16},{16,0},{32,48},{48,32},{1,17},{17,1},{33,49},{49,33},{2,18}... | collective-permute-start | bytes 933896 | tf_op jit(solution)/shard_map/ppermute | solution.py:340
  4.7 17.0 %collective-permute-start.3 = (bf16[1216,128]{1,0:T(8,128)(2,1)}, bf16[1216,128]{1,0:T(8,128)(2,1)S(1)}, u32[]{:S(2)}, u32[]{:S(2)}) collective-permute-start(bf16[1216,128]{1,0:T(8,128)(2,1)} %get-tuple-element.21), channel_id=1, source_target_pairs={{0,32},{16,48},{32,0},{48,16},{1,33},{17,49},{33,1},{49,17},{2,34}... | collective-permute-start | bytes 933896 | tf_op jit(solution)/shard_map/ppermute | solution.py:340
  7.6 16.6 %collective-permute-start.5 = (bf16[1216,128]{1,0:T(8,128)(2,1)}, bf16[1216,128]{1,0:T(8,128)(2,1)S(1)}, u32[]{:S(2)}, u32[]{:S(2)}) collective-permute-start(bf16[1216,128]{1,0:T(8,128)(2,1)} %get-tuple-element.22), channel_id=1, source_target_pairs={{0,48},{16,32},{32,16},{48,0},{1,49},{17,33},{33,17},{49,1},{2,50}... | collective-permute-start | bytes 933896 | tf_op jit(solution)/shard_map/ppermute | solution.py:340
  7.8 16.4 %collective-permute-start = (bf16[1216,128]{1,0:T(8,128)(2,1)}, bf16[1216,128]{1,0:T(8,128)(2,1)S(1)}, u32[]{:S(2)}, u32[]{:S(2)}) collective-permute-start(bf16[1216,128]{1,0:T(8,128)(2,1)} %get-tuple-element.19.refs_0_), channel_id=1, source_target_pairs={{0,8},{8,0},{1,9},{9,1},{2,10},{10,2},{3,11},{11,3},{4,12},{12,4},... | collective-permute-start | bytes 933896 | tf_op jit(solution)/shard_map/ppermute | solution.py:340
  13.5 12.3 %copy-start.2 = (bf16[1216,128]{1,0:T(8,128)(2,1)}, bf16[1216,128]{1,0:T(8,128)(2,1)S(1)}, u32[]{:S(2)}) copy-start(bf16[1216,128]{1,0:T(8,128)(2,1)S(1)} %collective-permute-done.1.refs_2_) | copy-start | bytes 933892
  13.5 10.7 %collective-permute-start.2 = (bf16[1216,128]{1,0:T(8,128)(2,1)S(1)}, bf16[1216,128]{1,0:T(8,128)(2,1)S(1)}, u32[]{:S(2)}, u32[]{:S(2)}) collective-permute-start(bf16[1216,128]{1,0:T(8,128)(2,1)S(1)} %collective-permute-done.1.refs_2_), channel_id=1, source_target_pairs={{0,8},{8,0},{1,9},{9,1},{2,10},{10,2},{3,11},{11,3},{4,12},{12,4},... | collective-permute-start | bytes 933896 | tf_op jit(solution)/shard_map/ppermute | solution.py:340
  21.6 4.2 %copy-start.3 = (bf16[1216,128]{1,0:T(8,128)(2,1)}, bf16[1216,128]{1,0:T(8,128)(2,1)S(1)}, u32[]{:S(2)}) copy-start(bf16[1216,128]{1,0:T(8,128)(2,1)S(1)} %collective-permute-done.3.refs_4_) | copy-start | bytes 933892
  21.6 2.6 %collective-permute-start.4 = (bf16[1216,128]{1,0:T(8,128)(2,1)S(1)}, bf16[1216,128]{1,0:T(8,128)(2,1)S(1)}, u32[]{:S(2)}, u32[]{:S(2)}) collective-permute-start(bf16[1216,128]{1,0:T(8,128)(2,1)S(1)} %collective-permute-done.3.refs_4_), channel_id=1, source_target_pairs={{0,8},{8,0},{1,9},{9,1},{2,10},{10,2},{3,11},{11,3},{4,12},{12,4},... | collective-permute-start | bytes 933896 | tf_op jit(solution)/shard_map/ppermute | solution.py:340
  24.2 1.6 %copy-start.4 = (bf16[1216,128]{1,0:T(8,128)(2,1)}, bf16[1216,128]{1,0:T(8,128)(2,1)S(1)}, u32[]{:S(2)}) copy-start(bf16[1216,128]{1,0:T(8,128)(2,1)S(1)} %collective-permute-done.5.refs_6_) | copy-start | bytes 933892
  24.2 1.6 %collective-permute-start.6 = (bf16[1216,128]{1,0:T(8,128)(2,1)S(1)}, bf16[1216,128]{1,0:T(8,128)(2,1)S(1)}, u32[]{:S(2)}, u32[]{:S(2)}) collective-permute-start(bf16[1216,128]{1,0:T(8,128)(2,1)S(1)} %collective-permute-done.5.refs_6_), channel_id=1, source_target_pairs={{0,8},{8,0},{1,9},{9,1},{2,10},{10,2},{3,11},{11,3},{4,12},{12,4},... | collective-permute-start | bytes 933896 | tf_op jit(solution)/shard_map/ppermute | solution.py:340
  24.2 1.6 %copy-start.5 = (bf16[1216,128]{1,0:T(8,128)(2,1)}, bf16[1216,128]{1,0:T(8,128)(2,1)S(1)}, u32[]{:S(2)}) copy-start(bf16[1216,128]{1,0:T(8,128)(2,1)S(1)} %collective-permute-done.refs_1_) | copy-start | bytes 933892
  24.2 1.6 %copy-start.6 = (bf16[1216,128]{1,0:T(8,128)(2,1)}, bf16[1216,128]{1,0:T(8,128)(2,1)S(1)}, u32[]{:S(2)}) copy-start(bf16[1216,128]{1,0:T(8,128)(2,1)S(1)} %collective-permute-done.2.refs_3_) | copy-start | bytes 933892
  24.2 1.6 %copy-start.7 = (bf16[1216,128]{1,0:T(8,128)(2,1)}, bf16[1216,128]{1,0:T(8,128)(2,1)S(1)}, u32[]{:S(2)}) copy-start(bf16[1216,128]{1,0:T(8,128)(2,1)S(1)} %collective-permute-done.4.refs_5_) | copy-start | bytes 933892
  25.8 0.7 copy-start.8
  37.7 3.8 %copy-start.1 = (bf16[512,128]{1,0:T(8,128)(2,1)S(1)}, bf16[512,128]{1,0:T(8,128)(2,1)}, u32[]{:S(2)}) copy-start(bf16[512,128]{1,0:T(8,128)(2,1)} %get-tuple-element.29.a_ref) | copy-start | bytes 393220
  37.7 7.1 %copy-start = (bf16[512,128]{1,0:T(8,128)(2,1)S(1)}, bf16[512,128]{1,0:T(8,128)(2,1)}, u32[]{:S(2)}) copy-start(bf16[512,128]{1,0:T(8,128)(2,1)} %get-tuple-element.30.a_ref) | copy-start | bytes 393220
  37.7 30.2 %all-to-all-start = ((bf16[8,768,128]{2,1,0:T(8,128)(2,1)}), bf16[8,768,128]{2,1,0:T(8,128)(2,1)S(1)}, u32[]{:S(2)}, u32[]{:S(2)}) async-start(bf16[8,768,128]{2,1,0:T(8,128)(2,1)} %get-tuple-element.23), calls=%async_computation | async-start | bytes 3145728 | tf_op jit(solution)/shard_map/all_to_all | solution.py:349
  41.5 10.2 %collective-permute-start.7 = (bf16[512,128]{1,0:T(8,128)(2,1)S(1)}, bf16[512,128]{1,0:T(8,128)(2,1)S(1)}, u32[]{:S(2)}, u32[]{:S(2)}) collective-permute-start(bf16[512,128]{1,0:T(8,128)(2,1)S(1)} %copy-done.1), channel_id=1, source_target_pairs={{0,64},{64,0},{128,192},{192,128},{1,65},{65,1},{129,193},{193,129... | collective-permute-start | bytes 393224 | tf_op jit(solution)/shard_map/ppermute | solution.py:340
  44.8 10.6 %collective-permute-start.9 = (bf16[512,128]{1,0:T(8,128)(2,1)S(1)}, bf16[512,128]{1,0:T(8,128)(2,1)S(1)}, u32[]{:S(2)}, u32[]{:S(2)}) collective-permute-start(bf16[512,128]{1,0:T(8,128)(2,1)S(1)} %copy-done), channel_id=1, source_target_pairs={{0,192},{64,128},{128,64},{192,0},{1,193},{65,129},{129,65},{193,1... | collective-permute-start | bytes 393224 | tf_op jit(solution)/shard_map/ppermute | solution.py:340
  51.7 7.5 %collective-permute-start.8 = (bf16[512,128]{1,0:T(8,128)(2,1)S(1)}, bf16[512,128]{1,0:T(8,128)(2,1)S(1)}, u32[]{:S(2)}, u32[]{:S(2)}) collective-permute-start(bf16[512,128]{1,0:T(8,128)(2,1)S(1)} %add_uk.1.a_ref), channel_id=1, source_target_pairs={{0,192},{64,128},{128,64},{192,0},{1,193},{65,129},{129,65},{193,1... | collective-permute-start | bytes 393224 | tf_op jit(solution)/shard_map/ppermute | solution.py:340
  55.5 8.2 %collective-permute-start.10 = (bf16[512,128]{1,0:T(8,128)(2,1)S(1)}, bf16[512,128]{1,0:T(8,128)(2,1)S(1)}, u32[]{:S(2)}, u32[]{:S(2)}) collective-permute-start(bf16[512,128]{1,0:T(8,128)(2,1)S(1)} %add_uv.1.c_ref), channel_id=1, source_target_pairs={{0,64},{64,0},{128,192},{192,128},{1,65},{65,1},{129,193},{193,129... | collective-permute-start | bytes 393224 | tf_op jit(solution)/shard_map/ppermute | solution.py:340
  63.7 15.1 %collective-permute-start.16 = (bf16[1024,128]{1,0:T(8,128)(2,1)S(1)}, bf16[1024,128]{1,0:T(8,128)(2,1)S(1)}, u32[]{:S(2)}, u32[]{:S(2)}) collective-permute-start(bf16[1024,128]{1,0:T(8,128)(2,1)S(1)} %add_join.1.refs_0_), channel_id=1, source_target_pairs={{0,48},{16,32},{32,16},{48,0},{1,49},{17,33},{33,17},{49,1},{2,50}... | collective-permute-start | bytes 786440 | tf_op jit(solution)/shard_map/ppermute | solution.py:340
  66.7 12.2 %collective-permute-start.14 = (bf16[1024,128]{1,0:T(8,128)(2,1)S(1)}, bf16[1024,128]{1,0:T(8,128)(2,1)S(1)}, u32[]{:S(2)}, u32[]{:S(2)}) collective-permute-start(bf16[1024,128]{1,0:T(8,128)(2,1)S(1)} %add_join.1.refs_0_), channel_id=1, source_target_pairs={{0,32},{16,48},{32,0},{48,16},{1,33},{17,49},{33,1},{49,17},{2,34}... | collective-permute-start | bytes 786440 | tf_op jit(solution)/shard_map/ppermute | solution.py:340
  67.6 12.0 %collective-permute-start.12 = (bf16[1024,128]{1,0:T(8,128)(2,1)S(1)}, bf16[1024,128]{1,0:T(8,128)(2,1)S(1)}, u32[]{:S(2)}, u32[]{:S(2)}) collective-permute-start(bf16[1024,128]{1,0:T(8,128)(2,1)S(1)} %add_join.1.refs_0_), channel_id=1, source_target_pairs={{0,16},{16,0},{32,48},{48,32},{1,17},{17,1},{33,49},{49,33},{2,18}... | collective-permute-start | bytes 786440 | tf_op jit(solution)/shard_map/ppermute | solution.py:340
  69.7 13.9 %all-to-all-start.1 = ((bf16[8,16,640]{2,1,0:T(8,128)(2,1)}), bf16[8,16,640]{2,1,0:T(8,128)(2,1)S(1)}, u32[]{:S(2)}, u32[]{:S(2)}) async-start(bf16[8,16,640]{2,1,0:T(8,128)(2,1)} %sum_ctx.1), calls=%async_computation.1 | async-start | bytes 327680 | tf_op jit(solution)/shard_map/all_to_all | solution.py:352
  76.6 2.9 %collective-permute-start.11 = (bf16[1024,128]{1,0:T(8,128)(2,1)S(1)}, bf16[1024,128]{1,0:T(8,128)(2,1)S(1)}, u32[]{:S(2)}, u32[]{:S(2)}) collective-permute-start(bf16[1024,128]{1,0:T(8,128)(2,1)S(1)} %add_join.1.refs_0_), channel_id=1, source_target_pairs={{0,8},{8,0},{1,9},{9,1},{2,10},{10,2},{3,11},{11,3},{4,12},{12,4},... | collective-permute-start | bytes 786440 | tf_op jit(solution)/shard_map/ppermute | solution.py:340
  78.9 1.5 %collective-permute-start.17 = (bf16[1024,128]{1,0:T(8,128)(2,1)S(1)}, bf16[1024,128]{1,0:T(8,128)(2,1)S(1)}, u32[]{:S(2)}, u32[]{:S(2)}) collective-permute-start(bf16[1024,128]{1,0:T(8,128)(2,1)S(1)} %collective-permute-done.16.refs_6_), channel_id=1, source_target_pairs={{0,8},{8,0},{1,9},{9,1},{2,10},{10,2},{3,11},{11,3},{4,12},{12,4},... | collective-permute-start | bytes 786440 | tf_op jit(solution)/shard_map/ppermute | solution.py:340
  78.9 1.9 %collective-permute-start.15 = (bf16[1024,128]{1,0:T(8,128)(2,1)S(1)}, bf16[1024,128]{1,0:T(8,128)(2,1)S(1)}, u32[]{:S(2)}, u32[]{:S(2)}) collective-permute-start(bf16[1024,128]{1,0:T(8,128)(2,1)S(1)} %collective-permute-done.14.refs_4_), channel_id=1, source_target_pairs={{0,8},{8,0},{1,9},{9,1},{2,10},{10,2},{3,11},{11,3},{4,12},{12,4},... | collective-permute-start | bytes 786440 | tf_op jit(solution)/shard_map/ppermute | solution.py:340
  79.5 1.6 %collective-permute-start.13 = (bf16[1024,128]{1,0:T(8,128)(2,1)S(1)}, bf16[1024,128]{1,0:T(8,128)(2,1)S(1)}, u32[]{:S(2)}, u32[]{:S(2)}) collective-permute-start(bf16[1024,128]{1,0:T(8,128)(2,1)S(1)} %collective-permute-done.12.refs_2_), channel_id=1, source_target_pairs={{0,8},{8,0},{1,9},{9,1},{2,10},{10,2},{3,11},{11,3},{4,12},{12,4},... | collective-permute-start | bytes 786440 | tf_op jit(solution)/shard_map/ppermute | solution.py:340
